TPU v7x, 32 devices: a whole 2x2x4 slice. The times are simulated.
32 devices in a mesh: row: 4 (over y, x), col: 8 (over z, core).
Axes of the slice: x: 2, y: 2, z: 4, core: 2. Of those that a mesh axis runs over, the one named last changes fastest.
Arguments:
- send_blocks: bfloat16 [16, 16, 128, 128], P('row', 'col'), may hold values from -0.125 to 0.125
- send_count: int32 [16, 8], P('row', 'col'), may hold values from 0 to 2, as said below
- send_place: int32 [16, 16], P('row', 'col'), may hold values from 0 to 31, as said below
- term_current: bfloat16 [2, 1024, 8192], P(None, 'row', 'col'), may hold values from -6 to 6
- term_previous: bfloat16 [8192, 8192], P('row', 'col'), may hold values from -6 to 6
- keep_mask: int32 [64, 64], P('row', 'col'), may hold values 0 or 1
Outputs:
- term_next: bfloat16 [8192, 8192], P('row', 'col')
Inputs may be any that keep to these rules, and one draw needn't show every extreme that they name: `send_count`: records from sending row s to receiving row d in column c. In every draw some receiver gets 2 from every sending row, and every receiver gets 2 from at least one sending row. `send_place`: over all live records to one receiver (same receiving row and column) the places are distinct. Slots past the count hold 0.
All inputs are finite; a program needn't handle non-finite values. No bound on the sum of `keep_mask` on one device may be relied on, other than what follows from the above.
Results may differ from a plain program's by a relative error of at most 0.001.
Values may be sent and summed in bfloat16 or wider, within the bound.
No kernel may reach another device: no remote copies, remote signals or barrier semaphores. Data moves between devices by JAX's collectives and lax.ppermute only.
A program may use at most 128 MiB of HBM per device.

v0:
```python
import jax
import jax.numpy as jnp
from jax import lax
from jax.sharding import PartitionSpec as P


def add_portion(term_panel, running, portion):
    return running + jnp.dot(portion, term_panel, preferred_element_type=jnp.float32)


def per_device(send_blocks, send_count, send_place, term_current, term_previous, keep_mask):
    grid_rows = lax.axis_size("row")
    block = send_blocks.shape[-1]
    slot_count = send_blocks.shape[1]
    panels = term_current.shape[0]
    tile_rows = term_previous.shape[0]
    tile_cols = term_previous.shape[1]
    row_blocks = tile_rows // block
    col_blocks = tile_cols // block
    positions = row_blocks * panels
    slot_index = jnp.arange(slot_count, dtype=jnp.int32)
    is_live = slot_index[None, :] < send_count
    slot_codes = jnp.where(is_live, send_place, -1).astype(jnp.bfloat16)
    arrived, arrived_codes = (
        lax.all_to_all(send_blocks, "row", split_axis=0, concat_axis=0, tiled=True),
        lax.all_to_all(slot_codes, "row", split_axis=0, concat_axis=0, tiled=True),
    )
    records = arrived.reshape(grid_rows * slot_count, block, block)
    record_codes = arrived_codes.reshape(grid_rows * slot_count)
    term_panels = [
        lax.all_gather(term_current[panel], "row", axis=0, tiled=True) for panel in range(panels)
    ]
    code_values = record_codes.astype(jnp.int32)
    onehot = (code_values[None, :] == jnp.arange(positions, dtype=jnp.int32)[:, None]).astype(
        jnp.bfloat16
    )
    own_tile = jnp.dot(
        onehot, records.reshape(-1, block * block), preferred_element_type=jnp.float32
    )
    own_tile = own_tile.astype(jnp.bfloat16).reshape(row_blocks, panels, block, block)
    running = jnp.zeros((tile_rows, tile_cols), jnp.float32)
    for panel in range(panels):
        own_part = own_tile[:, panel].reshape(tile_rows, block)
        running = add_portion(
            term_panels[panel], running, lax.all_gather(own_part, "col", axis=1, tiled=True)
        )
    update = 2.0 * running - term_previous.astype(jnp.float32)
    update = update.reshape(row_blocks, block, col_blocks, block)
    wanted = (keep_mask > 0)[:, None, :, None]
    result = jnp.where(wanted, update, jnp.zeros_like(update))
    return result.reshape(tile_rows, tile_cols).astype(jnp.bfloat16)


def solution(mesh):
    placed = (
        P("row", "col", None, None),
        P("row", "col"),
        P("row", "col"),
        P(None, "row", "col"),
        P("row", "col"),
        P("row", "col"),
    )
    return jax.shard_map(
        per_device, mesh=mesh, in_specs=placed, out_specs=P("row", "col"), check_vma=False
    )
```

profile of v0, /device:TPU:0, one launch (start us, length us, event | category | flops | bytes accessed | tf_op | source)
XLA Modules:
  0.0 205.7 jit_solution(1875053856609406229)
XLA Ops:
  6.5 0.0 all-gather.11.cloned.1.call-start
  6.5 2.2 %fusion.9 = (bf16[1,256,1024]{2,1,0:T(8,128)(2,1)}, bf16[1,256,1024]{2,1,0:T(8,128)(2,1)}) fusion(bf16[2,256,1024]{2,1,0:T(8,128)(2,1)} %param.9), kind=kLoop, calls=%fused_computation.15 | loop fusion | bytes 2097152 | tf_op jit(solution)/shard_map/slice | solution.py:31
  8.8 0.0 copy-start
  8.8 0.0 all-gather.11.cloned.1.call-update
  8.8 0.7 fusion.8
  9.5 0.1 copy.12
  9.6 9.6 %all_to_all.14 = bf16[4,1,2]{2,1,0:T(2,128)(2,1)S(1)} all-to-all(bf16[4,1,2]{2,1,0:T(2,128)(2,1)S(1)} %copy.12), channel_id=1, replica_groups=mesh['row'=4,'col'=8] {'row'}, dimensions={0} | all-to-all | bytes 32 | tf_op jit(solution)/shard_map/all_to_all | solution.py:26
  19.2 3.4 %all-to-all-start.1 = ((bf16[4,2,128,128]{3,2,1,0:T(8,128)(2,1)}), bf16[4,2,128,128]{3,2,1,0:T(8,128)(2,1)S(1)}, u32[]{:S(2)}, u32[]{:S(2)}) async-start(bf16[4,2,128,128]{3,2,1,0:T(8,128)(2,1)} %param.6), calls=%async_computation.1 | async-start | bytes 524288 | tf_op jit(solution)/shard_map/all_to_all | solution.py:25
  22.6 0.0 all-gather.7.cloned.1.call-start
  22.7 0.1 reshape.19
  22.8 7.8 %all-to-all-done.1 = bf16[4,2,128,128]{3,2,1,0:T(8,128)(2,1)S(1)} async-done(((bf16[4,2,128,128]{3,2,1,0:T(8,128)(2,1)}), bf16[4,2,128,128]{3,2,1,0:T(8,128)(2,1)S(1)}, u32[]{:S(2)}, u32[]{:S(2)}) %all-to-all-start.1) | async-done | bytes 262176 | tf_op jit(solution)/shard_map/all_to_all | solution.py:25
  30.6 0.4 fusion.3
  31.0 0.2 copy.15
  31.2 1.1 fusion.10
  32.3 0.0 all-gather.7.cloned.1.call-update
  32.3 0.0 all-gather.13.cloned.1.call-start
  32.3 0.7 all-gather.13.cloned.1.call-update
  33.0 0.0 all-gather.9.cloned.1.call-start
  33.1 0.5 all-gather.9.cloned.1.call-update
  33.6 0.0 copy-done
  33.6 0.1 copy.11
  33.7 16.3 %all-gather.11.cloned.1.call-done = bf16[1,1024,1024]{2,1,0:T(8,128)(2,1)} async-done(((bf16[1,256,1024]{2,1,0:T(8,128)(2,1)}), bf16[1,1024,1024]{2,1,0:T(8,128)(2,1)}) %all-gather.11.cloned.1.call-update) | async-done | bytes 2097168 | tf_op jit(solution)/shard_map/all_gather | solution.py:31
  50.1 49.4 %all-gather.7.cloned.1.call-done = bf16[2048,1024]{1,0:T(8,128)(2,1)} async-done(((bf16[2048,128]{1,0:T(8,128)(2,1)}), bf16[2048,1024]{1,0:T(8,128)(2,1)}) %all-gather.7.cloned.1.call-update) | async-done | bytes 4194320 | tf_op jit(solution)/shard_map/all_gather | solution.py:45
  99.5 10.6 %fusion.1 = f32[2048,1024]{1,0:T(8,128)} fusion(bf16[2048,1024]{1,0:T(8,128)(2,1)} %all-gather.7.cloned.1.call-done, bf16[1,1024,1024]{2,1,0:T(8,128)(2,1)} %all-gather.11.cloned.1.call-done), kind=kOutput, calls=%fused_computation.3 | convolution fusion | flops 4294967296 | bytes 14680064 | tf_op jit(solution)/shard_map/dot_general | solution.py:8
  110.1 24.8 %all-gather.13.cloned.1.call-done = bf16[1,1024,1024]{2,1,0:T(8,128)(2,1)} async-done(((bf16[1,256,1024]{2,1,0:T(8,128)(2,1)}), bf16[1,1024,1024]{2,1,0:T(8,128)(2,1)}) %all-gather.13.cloned.1.call-update) | async-done | bytes 2097168 | tf_op jit(solution)/shard_map/all_gather | solution.py:31
  134.9 49.3 %all-gather.9.cloned.1.call-done = bf16[2048,1024]{1,0:T(8,128)(2,1)} async-done(((bf16[2048,128]{1,0:T(8,128)(2,1)}), bf16[2048,1024]{1,0:T(8,128)(2,1)}) %all-gather.9.cloned.1.call-update) | async-done | bytes 4194320 | tf_op jit(solution)/shard_map/all_gather | solution.py:45
  184.2 0.6 broadcast_in_dim.21
  184.8 14.3 %select_convert_fusion = bf16[2048,1024]{1,0:T(8,128)(2,1)} fusion(bf16[2048,1024]{1,0:T(8,128)(2,1)} %param.10, f32[2048,1024]{1,0:T(8,128)} %fusion.1, pred[256,8,8,128]{3,2,1,0:T(8,128)(4,1)S(1)} %bitcast.27, bf16[2048,1024]{1,0:T(8,128)(2,1)} %all-gather.9.cloned.1.call-done, bf16[1,1024,1024]{2,1,0:T(8,128)(2,1)} %all-gather.13.cloned.1.call-done), kind=kOutput, calls=%fused_computation.1 | convolution fusion | flops 4307550208 | bytes 25165824 | tf_op jit(solution)/shard_map/dot_general | solution.py:8
  (2 shorter events, 0.0 us)
Async XLA Ops:
  6.5 43.5 %all-gather.11.cloned.1.call-start = ((), (), s32[]{:S(2)}) async-start(), calls=%async_computation.4 | async-start | bytes 2621440 | tf_op jit(solution)/shard_map/all_gather | solution.py:31
  8.8 24.9 %copy-start = (s32[16,8]{0,1:T(8,128)S(1)}, s32[16,8]{0,1:T(8,128)}, u32[]{:S(2)}) copy-start(s32[16,8]{0,1:T(8,128)} %param.11) | copy-start | bytes 1540
  19.2 11.4 %all-to-all-start.1 = ((bf16[4,2,128,128]{3,2,1,0:T(8,128)(2,1)}), bf16[4,2,128,128]{3,2,1,0:T(8,128)(2,1)S(1)}, u32[]{:S(2)}, u32[]{:S(2)}) async-start(bf16[4,2,128,128]{3,2,1,0:T(8,128)(2,1)} %param.6), calls=%async_computation.1 | async-start | bytes 524288 | tf_op jit(solution)/shard_map/all_to_all | solution.py:25
  22.6 76.9 %all-gather.7.cloned.1.call-start = ((), (), s32[]{:S(2)}) async-start(), calls=%async_computation.2 | async-start | bytes 4718592 | tf_op jit(solution)/shard_map/all_gather | solution.py:45
  32.3 102.6 %all-gather.13.cloned.1.call-start = ((), (), s32[]{:S(2)}) async-start(), calls=%async_computation.5 | async-start | bytes 2621440 | tf_op jit(solution)/shard_map/all_gather | solution.py:31
  33.0 151.1 %all-gather.9.cloned.1.call-start = ((), (), s32[]{:S(2)}) async-start(), calls=%async_computation.3 | async-start | bytes 4718592 | tf_op jit(solution)/shard_map/all_gather | solution.py:45
Sparse Core Ops, SparseCore 0:
  9.2 40.8 all-gather.10
  51.6 47.7 all-gather.6
  101.3 33.5 all-gather.12
  136.3 47.7 all-gather.8
where the time goes:
time: 206 us
  waiting for transfers between devices  149 us (72%)
  matrix products  25.4 us (12%)
  between operations  13.2 us (6%)
  blocking collectives  9.6 us (5%)
  local copies, waits for them, and re-layouts  4.4 us (2%)
  starting transfers between devices  3.53 us (2%)
    all_gather x2, waiting for transfers between devices, per_device(): lax.all_gather(own_part, 'col', axis=1, tiled=True)  98.7 us
    all_gather x2, waiting for transfers between devices, per_device(): lax.all_gather(term_current[panel], 'row', axis=0, tiled=True)  41.1 us
    dot_general x2, matrix products, add_portion(): jnp.dot(portion, term_panel, preferred_element_type=jnp.float32)  24.9 us
    all_to_all x1, blocking collectives, per_device(): lax.all_to_all(slot_codes, 'row', split_axis=0, concat_axis=0, tiled=True)  9.6 us
    all_to_all x1, waiting for transfers between devices, per_device(): lax.all_to_all(send_blocks, 'row', split_axis=0, concat_axis=0, tiled=True)  7.8 us
  transfers between devices with their start and end apart: 5, of which 5 were waited for; matrix products, arithmetic and copies ran while one was open for 6% of the time, Pallas kernels for 0%

commit v1 on v0

v1 whole, which is shorter than its diff:
```python
import functools

import jax
import jax.numpy as jnp
from jax import lax
from jax.experimental import pallas as pl
from jax.experimental.pallas import tpu as pltpu
from jax.sharding import PartitionSpec as P

PAD = 16
TILE = 256


def swap(x, axis, offset):
    size = lax.axis_size(axis)
    return lax.ppermute(x, axis, [(i, i ^ offset) for i in range(size)])


def early_kernel(
    dims, codes, spot, *refs
):
    grid_rows, grid_cols, slots, panels, block = dims
    span = slots * block + PAD
    per_row = grid_cols // grid_rows
    own_refs = refs[:grid_cols]
    rest_refs = refs[grid_cols : 2 * grid_cols]
    term_refs = refs[2 * grid_cols : -7]
    previous, acc, late, matrix, terms, held, sems = refs[-7:]
    depth = per_row * block
    early = matrix.shape[0]

    @pl.when(pl.program_id(0) == 0)
    def _():
        copies = []
        for o in range(grid_cols):
            copies.append(pltpu.make_async_copy(own_refs[o], held.at[o, pl.ds(0, span)], sems.at[0]))
            copies.append(
                pltpu.make_async_copy(
                    rest_refs[o], held.at[o, pl.ds(span, (grid_rows - 1) * span)], sems.at[0]
                )
            )
        at = 0
        for ref in term_refs:
            rows = ref.shape[0]
            copies.append(pltpu.make_async_copy(ref, terms.at[pl.ds(at, rows)], sems.at[0]))
            at += rows
        for copy in copies:
            copy.start()
        matrix[...] = jnp.zeros_like(matrix)
        late[...] = jnp.zeros_like(late)
        for copy in copies:
            copy.wait()
        my_row, my_col = spot[0], spot[1]

        def place(n, carry):
            o = n // grid_rows
            s = n % grid_rows
            col = my_col ^ o
            source = (col // per_row) ^ my_row
            inner = col % per_row
            for j in range(slots):
                code = codes[n * slots + j]
                row = code // panels
                k = (source * panels + code % panels) * per_row + inner
                at = pl.multiple_of(row * block, block)
                first = pl.multiple_of(s * span + j * block, PAD)

                @pl.when((code >= 0) & (k < early))
                def _():
                    matrix[k, pl.ds(at, block), :] = held[o, pl.ds(first, block), :]

                @pl.when((code >= 0) & (k >= early))
                def _():
                    late[k - early, pl.ds(at, block), :] = held[o, pl.ds(first, block), :]

            return carry

        lax.fori_loop(0, grid_cols * grid_rows, place, 0)

    base = pl.multiple_of(pl.program_id(0) * TILE, TILE)
    left = jnp.concatenate([matrix[k, pl.ds(base, TILE), :] for k in range(early)], axis=1)
    product = jnp.dot(left, terms[...], preferred_element_type=jnp.float32)
    acc[...] = 2.0 * product - previous[...].astype(jnp.float32)


def late_kernel(dims, keep, acc, late, *refs):
    block = dims[-1]
    term_refs, out = refs[:-1], refs[-1]
    blocks = late.shape[0]
    left = jnp.concatenate([late[k] for k in range(blocks)], axis=1)
    right = jnp.concatenate([ref[...] for ref in term_refs], axis=0)
    product = jnp.dot(left, right, preferred_element_type=jnp.float32)
    update = acc[...] + 2.0 * product
    per_tile = TILE // block
    step = pl.program_id(0)
    for i in range(per_tile):
        for j in range(out.shape[1] // block):
            wanted = keep[step * per_tile + i, j] > 0
            part = update[i * block : (i + 1) * block, j * block : (j + 1) * block]
            out[pl.ds(i * block, block), pl.ds(j * block, block)] = jnp.where(
                wanted, part, jnp.zeros_like(part)
            ).astype(out.dtype)


def per_device(send_blocks, send_count, send_place, term_current, term_previous, keep_mask):
    grid_rows, grid_cols = lax.axis_size("row"), lax.axis_size("col")
    my_row, my_col = lax.axis_index("row"), lax.axis_index("col")
    block = send_blocks.shape[-1]
    slots = send_blocks.shape[1]
    panels = term_current.shape[0]
    tile_rows, tile_cols = term_previous.shape
    per_row = grid_cols // grid_rows
    dims = (grid_rows, grid_cols, slots, panels, block)

    lane = jnp.arange(slots, dtype=jnp.int32)
    places = jnp.where(lane[None, :] < send_count, send_place, -1).astype(jnp.bfloat16)
    pad = jnp.broadcast_to(
        jnp.pad(places, ((0, 0), (0, block - slots)))[:, None, :], (grid_rows, PAD, block)
    )

    def payload(offset):
        to = my_row ^ offset
        records = lax.dynamic_index_in_dim(send_blocks, to, 0, keepdims=False)
        tail = lax.dynamic_index_in_dim(pad, to, 0, keepdims=False)
        return jnp.concatenate([records.reshape(slots * block, block), tail], axis=0)

    own = payload(0)
    got = [swap(payload(o), "row", o) for o in range(1, grid_rows)]

    mine = [term_current[p] for p in range(panels)]
    term = {}
    last = grid_rows - 1
    if grid_rows == 4 and panels == 2:
        term[1, 0] = swap(mine[0], "row", 1)
        term[2, 1] = swap(mine[1], "row", 2)
        term[1, 1] = swap(mine[1], "row", 1)
        term[2, 0] = swap(mine[0], "row", 2)
        term[3, 0] = swap(term[1, 0], "row", 2)
        term[3, 1] = swap(term[2, 1], "row", 1)
    else:
        for o in range(1, grid_rows):
            for p in range(panels):
                term[o, p] = swap(mine[p], "row", o)

    rest = jnp.concatenate(got, axis=0)
    owns, rests = {0: own}, {0: rest}
    for o in range(2, grid_cols, 2):
        owns[o] = swap(own, "col", o)
        rests[o] = swap(rest, "col", o)
    for o in range(0, grid_cols, 2):
        owns[o ^ 1] = swap(owns[o], "col", 1)
        rests[o ^ 1] = swap(rests[o], "col", 1)
    span = slots * block + PAD
    codes = []
    for o in range(grid_cols):
        codes.append(owns[o][slots * block, :slots])
        for s in range(grid_rows - 1):
            codes.append(rests[o][s * span + slots * block, :slots])
    codes = jnp.concatenate(codes).astype(jnp.int32)

    early = (grid_rows - 1) * panels * per_row
    any_spec = pl.BlockSpec(memory_space=pl.ANY)
    smem_spec = pl.BlockSpec(memory_space=pltpu.SMEM)
    early_terms = [term_current.reshape(-1, tile_cols)] + [
        term[o, p] for o in range(1, last) for p in range(panels)
    ]
    late_blocks = panels * per_row
    steps = tile_rows // TILE
    acc, late = pl.pallas_call(
        functools.partial(early_kernel, dims),
        grid=(steps,),
        out_shape=[
            jax.ShapeDtypeStruct((tile_rows, tile_cols), jnp.float32),
            jax.ShapeDtypeStruct((late_blocks, tile_rows, block), jnp.bfloat16),
        ],
        in_specs=[smem_spec, smem_spec]
        + [any_spec] * (2 * grid_cols + len(early_terms))
        + [pl.BlockSpec((TILE, tile_cols), lambda i: (i, 0))],
        out_specs=[
            pl.BlockSpec((TILE, tile_cols), lambda i: (i, 0)),
            pl.BlockSpec((late_blocks, tile_rows, block), lambda i: (0, 0, 0)),
        ],
        scratch_shapes=[
            pltpu.VMEM((early, tile_rows, block), jnp.bfloat16),
            pltpu.VMEM((early * block, tile_cols), jnp.bfloat16),
            pltpu.VMEM((grid_cols, grid_rows * span, block), jnp.bfloat16),
            pltpu.SemaphoreType.DMA((1,)),
        ],
        compiler_params=pltpu.CompilerParams(vmem_limit_bytes=48 * 1024 * 1024),
        cost_estimate=pl.CostEstimate(
            flops=2 * tile_rows * tile_cols * early * block,
            bytes_accessed=tile_rows * tile_cols * 6,
            transcendentals=0,
        ),
        name="early_product",
    )(
        codes,
        jnp.stack([my_row, my_col]).astype(jnp.int32),
        *[owns[o] for o in range(grid_cols)],
        *[rests[o] for o in range(grid_cols)],
        *early_terms,
        term_previous,
    )
    return pl.pallas_call(
        functools.partial(late_kernel, dims),
        grid=(steps,),
        out_shape=jax.ShapeDtypeStruct((tile_rows, tile_cols), term_previous.dtype),
        in_specs=[
            smem_spec,
            pl.BlockSpec((TILE, tile_cols), lambda i: (i, 0)),
            pl.BlockSpec((late_blocks, TILE, block), lambda i: (0, i, 0)),
        ]
        + [pl.BlockSpec(term[last, p].shape, lambda i: (0, 0)) for p in range(panels)],
        out_specs=pl.BlockSpec((TILE, tile_cols), lambda i: (i, 0)),
        compiler_params=pltpu.CompilerParams(vmem_limit_bytes=32 * 1024 * 1024),
        cost_estimate=pl.CostEstimate(
            flops=2 * tile_rows * tile_cols * late_blocks * block,
            bytes_accessed=tile_rows * tile_cols * 6,
            transcendentals=0,
        ),
        name="late_product",
    )(keep_mask, acc, late, *[term[last, p] for p in range(panels)])


def solution(mesh):
    placed = (
        P("row", "col", None, None),
        P("row", "col"),
        P("row", "col"),
        P(None, "row", "col"),
        P("row", "col"),
        P("row", "col"),
    )
    return jax.shard_map(
        per_device, mesh=mesh, in_specs=placed, out_specs=P("row", "col"), check_vma=False
    )
```

time: 206 us -> 132 us (0.64)
  waiting for transfers between devices: 149 us -> 34.1 us
  local copies, waits for them, and re-layouts: 4.4 us -> 44.3 us
  matrix products: 25.4 us -> 0 us
  Pallas kernels: 0 us -> 24.4 us
  starting transfers between devices: 3.53 us -> 26.6 us
  between operations: 13.2 us -> 0.15 us
  blocking collectives: 9.6 us -> 0 us
    all_gather x4 -> x0, waiting for transfers between devices: 140 us -> none  [the longest x2 98.7 us: per_device(): lax.all_gather(own_part, 'col', axis=1, tiled=True)]
    ppermute x0 -> x23, waiting for transfers between devices: none -> 34.1 us  [swap(): return lax.ppermute(x, axis, [(i, i ^ offset) for i in range(size)])]
    ppermute x0 -> x23, starting transfers between devices: none -> 26.6 us  [swap(): return lax.ppermute(x, axis, [(i, i ^ offset) for i in range(size)])]
    dot_general x3 -> x0, matrix products: 25.4 us -> none  [the longest x2 24.9 us: add_portion(): jnp.dot(portion, term_panel, preferred_element_type=jnp.float32)]
    pallas_call x0 -> x2, Pallas kernels: none -> 24.4 us  [the longest x1 18.1 us: per_device(): pl.pallas_call(functools.partial(early_kernel, dims), grid=(steps,), out_...]
    concatenate x0 -> x2, local copies, waits for them, and re-layouts: none -> 18.2 us  [the longest x1 18.2 us: per_device(): codes = jnp.concatenate(codes).astype(jnp.int32)]
    unnamed x3 -> x25, local copies, waits for them, and re-layouts: 0.24 us -> 13 us
    squeeze x0 -> x18, local copies, waits for them, and re-layouts: none -> 11.2 us  [the longest x10 5.14 us: per_device(): codes.append(rests[o][s * span + slots * block, :slots])]
  transfers between devices with their start and end apart: 5 -> 23, of which waited for: 5 -> 9; matrix products, arithmetic and copies ran while one was open for 6% -> 24% of each run, Pallas kernels for 0% -> 14%
where the time goes in v1:
time: 132 us; the launch traced here: 131 us
  local copies, waits for them, and re-layouts  44.3 us (34%)
  waiting for transfers between devices  34.1 us (26%)
  starting transfers between devices  26.6 us (20%)
  Pallas kernels  24.4 us (18%)
  other arithmetic  1.48 us (1%)
    ppermute x23, waiting for transfers between devices, swap(): return lax.ppermute(x, axis, [(i, i ^ offset) for i in range(size)])  34.1 us
    ppermute x23, starting transfers between devices, swap(): return lax.ppermute(x, axis, [(i, i ^ offset) for i in range(size)])  26.6 us
    concatenate x1, local copies, waits for them, and re-layouts, per_device(): codes = jnp.concatenate(codes).astype(jnp.int32)  18.2 us
    pallas_call x1, Pallas kernels, per_device(): pl.pallas_call(functools.partial(early_kernel, dims), grid=(steps,), out_...  18.1 us
    unnamed x25, local copies, waits for them, and re-layouts  13 us
    pallas_call x1, Pallas kernels, per_device(): pl.pallas_call(functools.partial(late_kernel, dims), grid=(steps,), out_s...  6.26 us
    squeeze x10, local copies, waits for them, and re-layouts, per_device(): codes.append(rests[o][s * span + slots * block, :slots])  5.14 us
    squeeze x7, local copies, waits for them, and re-layouts, per_device(): codes.append(owns[o][slots * block, :slots])  3.81 us
  transfers between devices with their start and end apart: 23, of which 9 were waited for; matrix products, arithmetic and copies ran while one was open for 24% of the time, Pallas kernels for 14%

profile of v1, /device:TPU:0, one launch (start us, length us, event | category | flops | bytes accessed | tf_op | source)
XLA Modules:
  0.0 131.0 jit_solution(17475351894779063677)
XLA Ops:
  0.9 1.0 constant_dynamic-slice_fusion
  1.9 4.1 %collective-permute-start.9 = (bf16[272,128]{1,0:T(8,128)(2,1)S(1)}, bf16[272,128]{1,0:T(8,128)(2,1)S(1)}, u32[]{:S(2)}, u32[]{:S(2)}) collective-permute-start(bf16[272,128]{1,0:T(8,128)(2,1)S(1)} %pad_maximum_fusion.3.refs_0_), channel_id=1, source_target_pairs={{0,4},{1,5},{2,6},{3,7},{4,0},{5,1},{6,2},{7,3},{8,12},{9,13},{10,... | collective-permute-start | bytes 208904 | tf_op jit(solution)/shard_map/ppermute | solution.py:16
  6.0 1.6 %collective-permute-start.5 = (bf16[272,128]{1,0:T(8,128)(2,1)S(1)}, bf16[272,128]{1,0:T(8,128)(2,1)S(1)}, u32[]{:S(2)}, u32[]{:S(2)}) collective-permute-start(bf16[272,128]{1,0:T(8,128)(2,1)S(1)} %pad_maximum_fusion.3.refs_0_), channel_id=1, source_target_pairs={{0,2},{1,3},{2,0},{3,1},{4,6},{5,7},{6,4},{7,5},{8,10},{9,11},{10,... | collective-permute-start | bytes 208904 | tf_op jit(solution)/shard_map/ppermute | solution.py:16
  7.6 2.3 %slice_bitcast_fusion = (bf16[256,1024]{1,0:T(8,128)(2,1)}, bf16[256,1024]{1,0:T(8,128)(2,1)}) fusion(bf16[2,256,1024]{2,1,0:T(8,128)(2,1)} %param.9), kind=kLoop, calls=%fused_computation | loop fusion | bytes 2097152 | tf_op jit(solution)/shard_map/squeeze | solution.py:130
  9.8 1.7 %collective-permute-start.20 = (bf16[256,1024]{1,0:T(8,128)(2,1)}, bf16[256,1024]{1,0:T(8,128)(2,1)S(1)}, u32[]{:S(2)}, u32[]{:S(2)}) collective-permute-start(bf16[256,1024]{1,0:T(8,128)(2,1)} %get-tuple-element.13), channel_id=1, source_target_pairs={{0,16},{8,24},{16,0},{24,8},{1,17},{9,25},{17,1},{25,9},{2,18},{10... | collective-permute-start | bytes 1572872 | tf_op jit(solution)/shard_map/ppermute | solution.py:16
  12.3 0.8 copy.8.keep
  13.2 1.5 %collective-permute-start.18 = (bf16[256,1024]{1,0:T(8,128)(2,1)}, bf16[256,1024]{1,0:T(8,128)(2,1)S(1)}, u32[]{:S(2)}, u32[]{:S(2)}) collective-permute-start(bf16[256,1024]{1,0:T(8,128)(2,1)} %get-tuple-element.13), channel_id=1, source_target_pairs={{0,8},{8,0},{16,24},{24,16},{1,9},{9,1},{17,25},{25,17},{2,10},{10... | collective-permute-start | bytes 1572872 | tf_op jit(solution)/shard_map/ppermute | solution.py:16
  16.3 1.4 %collective-permute-start.2 = (bf16[272,128]{1,0:T(8,128)(2,1)S(1)}, bf16[272,128]{1,0:T(8,128)(2,1)S(1)}, u32[]{:S(2)}, u32[]{:S(2)}) collective-permute-start(bf16[272,128]{1,0:T(8,128)(2,1)S(1)} %pad_maximum_fusion.2), channel_id=1, source_target_pairs={{0,24},{8,16},{16,8},{24,0},{1,25},{9,17},{17,9},{25,1},{2,26},{10... | collective-permute-start | bytes 208904 | tf_op jit(solution)/shard_map/ppermute | solution.py:16
  18.9 11.3 %collective-permute-done.2 = bf16[272,128]{1,0:T(8,128)(2,1)S(1)} collective-permute-done((bf16[272,128]{1,0:T(8,128)(2,1)S(1)}, bf16[272,128]{1,0:T(8,128)(2,1)S(1)}, u32[]{:S(2)}, u32[]{:S(2)}) %collective-permute-start.2) | collective-permute-done | bytes 69664 | tf_op jit(solution)/shard_map/ppermute | solution.py:16
  30.2 1.7 %collective-permute-start.1 = (bf16[272,128]{1,0:T(8,128)(2,1)S(1)}, bf16[272,128]{1,0:T(8,128)(2,1)S(1)}, u32[]{:S(2)}, u32[]{:S(2)}) collective-permute-start(bf16[272,128]{1,0:T(8,128)(2,1)S(1)} %pad_maximum_fusion.1), channel_id=1, source_target_pairs={{0,16},{8,24},{16,0},{24,8},{1,17},{9,25},{17,1},{25,9},{2,18},{10... | collective-permute-start | bytes 208904 | tf_op jit(solution)/shard_map/ppermute | solution.py:16
  32.4 1.5 %collective-permute-start.17 = (bf16[256,1024]{1,0:T(8,128)(2,1)}, bf16[256,1024]{1,0:T(8,128)(2,1)S(1)}, u32[]{:S(2)}, u32[]{:S(2)}) collective-permute-start(bf16[256,1024]{1,0:T(8,128)(2,1)} %get-tuple-element.14), channel_id=1, source_target_pairs={{0,8},{8,0},{16,24},{24,16},{1,9},{9,1},{17,25},{25,17},{2,10},{10... | collective-permute-start | bytes 1572872 | tf_op jit(solution)/shard_map/ppermute | solution.py:16
  34.5 1.7 %collective-permute-start.19 = (bf16[256,1024]{1,0:T(8,128)(2,1)}, bf16[256,1024]{1,0:T(8,128)(2,1)}, u32[]{:S(2)}, u32[]{:S(2)}) collective-permute-start(bf16[256,1024]{1,0:T(8,128)(2,1)} %get-tuple-element.14), channel_id=1, source_target_pairs={{0,16},{8,24},{16,0},{24,8},{1,17},{9,25},{17,1},{25,9},{2,18},{10... | collective-permute-start | bytes 1572872 | tf_op jit(solution)/shard_map/ppermute | solution.py:16
  41.0 3.6 %collective-permute-start.14 = (bf16[816,128]{1,0:T(8,128)(2,1)S(1)}, bf16[816,128]{1,0:T(8,128)(2,1)S(1)}, u32[]{:S(2)}, u32[]{:S(2)}) collective-permute-start(bf16[816,128]{1,0:T(8,128)(2,1)S(1)} %constant_dynamic-update-slice_fusion.refs_8_), channel_id=1, source_target_pairs={{0,6},{1,7},{2,4},{3,5},{4,2},{5,3},{6,0},{7,1},{8,14},{9,15},{10,... | collective-permute-start | bytes 626696 | tf_op jit(solution)/shard_map/ppermute | solution.py:16
  45.8 4.4 %collective-permute-done.14.refs_14_ = bf16[816,128]{1,0:T(8,128)(2,1)S(1)} collective-permute-done((bf16[816,128]{1,0:T(8,128)(2,1)S(1)}, bf16[816,128]{1,0:T(8,128)(2,1)S(1)}, u32[]{:S(2)}, u32[]{:S(2)}) %collective-permute-start.14) | collective-permute-done | bytes 208928 | tf_op jit(solution)/shard_map/ppermute | solution.py:16
  50.2 4.2 %collective-permute-start.10 = (bf16[816,128]{1,0:T(8,128)(2,1)S(1)}, bf16[816,128]{1,0:T(8,128)(2,1)S(1)}, u32[]{:S(2)}, u32[]{:S(2)}) collective-permute-start(bf16[816,128]{1,0:T(8,128)(2,1)S(1)} %constant_dynamic-update-slice_fusion.refs_8_), channel_id=1, source_target_pairs={{0,4},{1,5},{2,6},{3,7},{4,0},{5,1},{6,2},{7,3},{8,12},{9,13},{10,... | collective-permute-start | bytes 626696 | tf_op jit(solution)/shard_map/ppermute | solution.py:16
  54.4 9.1 %collective-permute-done.10.refs_12_ = bf16[816,128]{1,0:T(8,128)(2,1)S(1)} collective-permute-done((bf16[816,128]{1,0:T(8,128)(2,1)S(1)}, bf16[816,128]{1,0:T(8,128)(2,1)S(1)}, u32[]{:S(2)}, u32[]{:S(2)}) %collective-permute-start.10) | collective-permute-done | bytes 208928 | tf_op jit(solution)/shard_map/ppermute | solution.py:16
  64.1 5.4 %collective-permute-done.6.refs_10_ = bf16[816,128]{1,0:T(8,128)(2,1)S(1)} collective-permute-done((bf16[816,128]{1,0:T(8,128)(2,1)S(1)}, bf16[816,128]{1,0:T(8,128)(2,1)S(1)}, u32[]{:S(2)}, u32[]{:S(2)}) %collective-permute-start.6) | collective-permute-done | bytes 208928 | tf_op jit(solution)/shard_map/ppermute | solution.py:16
  70.1 0.9 collective-permute-done.4.refs_9_
  71.6 0.8 collective-permute-done.16.refs_15_
  73.1 0.8 collective-permute-done.12.refs_13_
  74.6 0.7 collective-permute-done.8.refs_11_
  75.9 18.2 %concatenate.23 = bf16[64]{0:T(256)(128)(2,1)} concatenate(bf16[2]{0:T(256)(128)(2,1)} %fusion.5, bf16[2]{0:T(256)(128)(2,1)} %slice_bitcast_fusion.32, bf16[2]{0:T(256)(128)(2,1)} %slice_bitcast_fusion.31, bf16[2]{0:T(256)(128)(2,1)} %slice_bitcast_fusion.30, bf16[2]{0:T(256)(128)(2,1)} %slice_bitcast_fusion.29, bf16[2]{0:T(256)(128)(2,1)} %get-tuple-element.39, ...), dimensions={0} | concatenate | bytes 256 | tf_op jit(solution)/shard_map/concatenate | solution.py:159
  95.3 1.5 %collective-permute-start.22 = (bf16[256,1024]{1,0:T(8,128)(2,1)S(1)}, bf16[256,1024]{1,0:T(8,128)(2,1)S(1)}, u32[]{:S(2)}, u32[]{:S(2)}) collective-permute-start(bf16[256,1024]{1,0:T(8,128)(2,1)S(1)} %collective-permute-done.20.refs_20_), channel_id=1, source_target_pairs={{0,8},{8,0},{16,24},{24,16},{1,9},{9,1},{17,25},{25,17},{2,10},{10... | collective-permute-start | bytes 1572872 | tf_op jit(solution)/shard_map/ppermute | solution.py:16
  96.8 1.2 copy-done.2
  98.0 0.9 copy-done.4
  98.9 0.9 copy-done.6
  99.8 0.9 copy-done.8
  100.7 0.9 copy-done.10
  101.6 18.1 %early_product.1 = (f32[2048,1024]{1,0:T(8,128)}, bf16[4,2048,128]{2,1,0:T(8,128)(2,1)}) custom-call(s32[64]{0:T(128)S(1)} %convert_element_type.9.codes, s32[2]{0:T(128)S(1)} %pad_add_fusion.spot, bf16[272,128]{1,0:T(8,128)(2,1)S(1)} %pad_maximum_fusion.3.refs_0_, bf16[272,128]{1,0:T(8,128)(2,1)S(1)} %copy-done.4, ...), custom_call_target="tpu_custom_call" | custom-call | flops 6442450944 | bytes 12582912 | tf_op jit(solution)/shard_map/early_product/pallas_call | solution.py:169
  119.7 3.4 %copy-done = f32[2048,1024]{1,0:T(8,128)S(1)} copy-done((f32[2048,1024]{1,0:T(8,128)S(1)}, f32[2048,1024]{1,0:T(8,128)}, u32[]{:S(2)}) %copy-start) | copy-done | bytes 8388632
  123.1 1.6 %copy-done.1 = bf16[4,2048,128]{2,1,0:T(8,128)(2,1)S(1)} copy-done((bf16[4,2048,128]{2,1,0:T(8,128)(2,1)S(1)}, bf16[4,2048,128]{2,1,0:T(8,128)(2,1)}, u32[]{:S(2)}) %copy-start.1) | copy-done | bytes 2097176
  124.7 6.3 %late_product.1 = bf16[2048,1024]{1,0:T(8,128)(2,1)} custom-call(s32[16,8]{1,0:T(8,128)S(1)} %copy.8.keep, f32[2048,1024]{1,0:T(8,128)S(1)} %copy-done, bf16[4,2048,128]{2,1,0:T(8,128)(2,1)S(1)} %copy-done.1, bf16[256,1024]{1,0:T(8,128)(2,1)S(1)} %collective-permute-done.21.refs_0_, bf16[256,1024]{1,0:T(8,128)(2,1)S(1)} %collective-permute-done.22.refs_1_), custom_call_target="tpu_custom_call" | custom-call | flops 2147483648 | bytes 12582912 | tf_op jit(solution)/shard_map/late_product/pallas_call | solution.py:204
  (75 shorter events, 16.6 us)
Async XLA Ops:
  1.9 11.3 %collective-permute-start.9 = (bf16[272,128]{1,0:T(8,128)(2,1)S(1)}, bf16[272,128]{1,0:T(8,128)(2,1)S(1)}, u32[]{:S(2)}, u32[]{:S(2)}) collective-permute-start(bf16[272,128]{1,0:T(8,128)(2,1)S(1)} %pad_maximum_fusion.3.refs_0_), channel_id=1, source_target_pairs={{0,4},{1,5},{2,6},{3,7},{4,0},{5,1},{6,2},{7,3},{8,12},{9,13},{10,... | collective-permute-start | bytes 208904 | tf_op jit(solution)/shard_map/ppermute | solution.py:16
  6.0 9.2 %collective-permute-start.5 = (bf16[272,128]{1,0:T(8,128)(2,1)S(1)}, bf16[272,128]{1,0:T(8,128)(2,1)S(1)}, u32[]{:S(2)}, u32[]{:S(2)}) collective-permute-start(bf16[272,128]{1,0:T(8,128)(2,1)S(1)} %pad_maximum_fusion.3.refs_0_), channel_id=1, source_target_pairs={{0,2},{1,3},{2,0},{3,1},{4,6},{5,7},{6,4},{7,5},{8,10},{9,11},{10,... | collective-permute-start | bytes 208904 | tf_op jit(solution)/shard_map/ppermute | solution.py:16
  7.6 29.2 %collective-permute-start.13 = (bf16[272,128]{1,0:T(8,128)(2,1)S(1)}, bf16[272,128]{1,0:T(8,128)(2,1)S(1)}, u32[]{:S(2)}, u32[]{:S(2)}) collective-permute-start(bf16[272,128]{1,0:T(8,128)(2,1)S(1)} %pad_maximum_fusion.3.refs_0_), channel_id=1, source_target_pairs={{0,6},{1,7},{2,4},{3,5},{4,2},{5,3},{6,0},{7,1},{8,14},{9,15},{10,... | collective-permute-start | bytes 208904 | tf_op jit(solution)/shard_map/ppermute | solution.py:16
  7.6 8.7 %collective-permute-start.3 = (bf16[272,128]{1,0:T(8,128)(2,1)S(1)}, bf16[272,128]{1,0:T(8,128)(2,1)S(1)}, u32[]{:S(2)}, u32[]{:S(2)}) collective-permute-start(bf16[272,128]{1,0:T(8,128)(2,1)S(1)} %pad_maximum_fusion.3.refs_0_), channel_id=1, source_target_pairs={{0,1},{1,0},{2,3},{3,2},{4,5},{5,4},{6,7},{7,6},{8,9},{9,8},{10,11... | collective-permute-start | bytes 208904 | tf_op jit(solution)/shard_map/ppermute | solution.py:16
  9.8 85.5 %collective-permute-start.20 = (bf16[256,1024]{1,0:T(8,128)(2,1)}, bf16[256,1024]{1,0:T(8,128)(2,1)S(1)}, u32[]{:S(2)}, u32[]{:S(2)}) collective-permute-start(bf16[256,1024]{1,0:T(8,128)(2,1)} %get-tuple-element.13), channel_id=1, source_target_pairs={{0,16},{8,24},{16,0},{24,8},{1,17},{9,25},{17,1},{25,9},{2,18},{10... | collective-permute-start | bytes 1572872 | tf_op jit(solution)/shard_map/ppermute | solution.py:16
  13.2 83.6 %collective-permute-start.18 = (bf16[256,1024]{1,0:T(8,128)(2,1)}, bf16[256,1024]{1,0:T(8,128)(2,1)S(1)}, u32[]{:S(2)}, u32[]{:S(2)}) collective-permute-start(bf16[256,1024]{1,0:T(8,128)(2,1)} %get-tuple-element.13), channel_id=1, source_target_pairs={{0,8},{8,0},{16,24},{24,16},{1,9},{9,1},{17,25},{25,17},{2,10},{10... | collective-permute-start | bytes 1572872 | tf_op jit(solution)/shard_map/ppermute | solution.py:16
  15.2 17.3 %collective-permute-start = (bf16[272,128]{1,0:T(8,128)(2,1)S(1)}, bf16[272,128]{1,0:T(8,128)(2,1)S(1)}, u32[]{:S(2)}, u32[]{:S(2)}) collective-permute-start(bf16[272,128]{1,0:T(8,128)(2,1)S(1)} %pad_maximum_fusion), channel_id=1, source_target_pairs={{0,8},{8,0},{16,24},{24,16},{1,9},{9,1},{17,25},{25,17},{2,10},{10... | collective-permute-start | bytes 208904 | tf_op jit(solution)/shard_map/ppermute | solution.py:16
  16.3 13.9 %collective-permute-start.2 = (bf16[272,128]{1,0:T(8,128)(2,1)S(1)}, bf16[272,128]{1,0:T(8,128)(2,1)S(1)}, u32[]{:S(2)}, u32[]{:S(2)}) collective-permute-start(bf16[272,128]{1,0:T(8,128)(2,1)S(1)} %pad_maximum_fusion.2), channel_id=1, source_target_pairs={{0,24},{8,16},{16,8},{24,0},{1,25},{9,17},{17,9},{25,1},{2,26},{10... | collective-permute-start | bytes 208904 | tf_op jit(solution)/shard_map/ppermute | solution.py:16
  30.2 4.3 %collective-permute-start.1 = (bf16[272,128]{1,0:T(8,128)(2,1)S(1)}, bf16[272,128]{1,0:T(8,128)(2,1)S(1)}, u32[]{:S(2)}, u32[]{:S(2)}) collective-permute-start(bf16[272,128]{1,0:T(8,128)(2,1)S(1)} %pad_maximum_fusion.1), channel_id=1, source_target_pairs={{0,16},{8,24},{16,0},{24,8},{1,17},{9,25},{17,1},{25,9},{2,18},{10... | collective-permute-start | bytes 208904 | tf_op jit(solution)/shard_map/ppermute | solution.py:16
  32.4 62.3 %collective-permute-start.17 = (bf16[256,1024]{1,0:T(8,128)(2,1)}, bf16[256,1024]{1,0:T(8,128)(2,1)S(1)}, u32[]{:S(2)}, u32[]{:S(2)}) collective-permute-start(bf16[256,1024]{1,0:T(8,128)(2,1)} %get-tuple-element.14), channel_id=1, source_target_pairs={{0,8},{8,0},{16,24},{24,16},{1,9},{9,1},{17,25},{25,17},{2,10},{10... | collective-permute-start | bytes 1572872 | tf_op jit(solution)/shard_map/ppermute | solution.py:16
  34.5 62.3 %collective-permute-start.19 = (bf16[256,1024]{1,0:T(8,128)(2,1)}, bf16[256,1024]{1,0:T(8,128)(2,1)}, u32[]{:S(2)}, u32[]{:S(2)}) collective-permute-start(bf16[256,1024]{1,0:T(8,128)(2,1)} %get-tuple-element.14), channel_id=1, source_target_pairs={{0,16},{8,24},{16,0},{24,8},{1,17},{9,25},{17,1},{25,9},{2,18},{10... | collective-permute-start | bytes 1572872 | tf_op jit(solution)/shard_map/ppermute | solution.py:16
  36.8 1.3 %collective-permute-start.11 = (bf16[272,128]{1,0:T(8,128)(2,1)S(1)}, bf16[272,128]{1,0:T(8,128)(2,1)S(1)}, u32[]{:S(2)}, u32[]{:S(2)}) collective-permute-start(bf16[272,128]{1,0:T(8,128)(2,1)S(1)} %collective-permute-done.9.refs_4_), channel_id=1, source_target_pairs={{0,1},{1,0},{2,3},{3,2},{4,5},{5,4},{6,7},{7,6},{8,9},{9,8},{10,11... | collective-permute-start | bytes 208904 | tf_op jit(solution)/shard_map/ppermute | solution.py:16
  38.1 1.3 %collective-permute-start.7 = (bf16[272,128]{1,0:T(8,128)(2,1)S(1)}, bf16[272,128]{1,0:T(8,128)(2,1)S(1)}, u32[]{:S(2)}, u32[]{:S(2)}) collective-permute-start(bf16[272,128]{1,0:T(8,128)(2,1)S(1)} %collective-permute-done.5.refs_2_), channel_id=1, source_target_pairs={{0,1},{1,0},{2,3},{3,2},{4,5},{5,4},{6,7},{7,6},{8,9},{9,8},{10,11... | collective-permute-start | bytes 208904 | tf_op jit(solution)/shard_map/ppermute | solution.py:16
  38.8 0.6 copy-start.5
  39.5 1.6 %collective-permute-start.15 = (bf16[272,128]{1,0:T(8,128)(2,1)S(1)}, bf16[272,128]{1,0:T(8,128)(2,1)S(1)}, u32[]{:S(2)}, u32[]{:S(2)}) collective-permute-start(bf16[272,128]{1,0:T(8,128)(2,1)S(1)} %collective-permute-done.13.refs_6_), channel_id=1, source_target_pairs={{0,1},{1,0},{2,3},{3,2},{4,5},{5,4},{6,7},{7,6},{8,9},{9,8},{10,11... | collective-permute-start | bytes 208904 | tf_op jit(solution)/shard_map/ppermute | solution.py:16
  41.0 9.2 %collective-permute-start.14 = (bf16[816,128]{1,0:T(8,128)(2,1)S(1)}, bf16[816,128]{1,0:T(8,128)(2,1)S(1)}, u32[]{:S(2)}, u32[]{:S(2)}) collective-permute-start(bf16[816,128]{1,0:T(8,128)(2,1)S(1)} %constant_dynamic-update-slice_fusion.refs_8_), channel_id=1, source_target_pairs={{0,6},{1,7},{2,4},{3,5},{4,2},{5,3},{6,0},{7,1},{8,14},{9,15},{10,... | collective-permute-start | bytes 626696 | tf_op jit(solution)/shard_map/ppermute | solution.py:16
  45.1 0.6 copy-start.9
  50.2 13.3 %collective-permute-start.10 = (bf16[816,128]{1,0:T(8,128)(2,1)S(1)}, bf16[816,128]{1,0:T(8,128)(2,1)S(1)}, u32[]{:S(2)}, u32[]{:S(2)}) collective-permute-start(bf16[816,128]{1,0:T(8,128)(2,1)S(1)} %constant_dynamic-update-slice_fusion.refs_8_), channel_id=1, source_target_pairs={{0,4},{1,5},{2,6},{3,7},{4,0},{5,1},{6,2},{7,3},{8,12},{9,13},{10,... | collective-permute-start | bytes 626696 | tf_op jit(solution)/shard_map/ppermute | solution.py:16
  63.5 6.0 %collective-permute-start.6 = (bf16[816,128]{1,0:T(8,128)(2,1)S(1)}, bf16[816,128]{1,0:T(8,128)(2,1)S(1)}, u32[]{:S(2)}, u32[]{:S(2)}) collective-permute-start(bf16[816,128]{1,0:T(8,128)(2,1)S(1)} %constant_dynamic-update-slice_fusion.refs_8_), channel_id=1, source_target_pairs={{0,2},{1,3},{2,0},{3,1},{4,6},{5,7},{6,4},{7,5},{8,10},{9,11},{10,... | collective-permute-start | bytes 626696 | tf_op jit(solution)/shard_map/ppermute | solution.py:16
  69.5 1.5 %collective-permute-start.4 = (bf16[816,128]{1,0:T(8,128)(2,1)S(1)}, bf16[816,128]{1,0:T(8,128)(2,1)S(1)}, u32[]{:S(2)}, u32[]{:S(2)}) collective-permute-start(bf16[816,128]{1,0:T(8,128)(2,1)S(1)} %constant_dynamic-update-slice_fusion.refs_8_), channel_id=1, source_target_pairs={{0,1},{1,0},{2,3},{3,2},{4,5},{5,4},{6,7},{7,6},{8,9},{9,8},{10,11... | collective-permute-start | bytes 626696 | tf_op jit(solution)/shard_map/ppermute | solution.py:16
  71.0 1.5 %collective-permute-start.16 = (bf16[816,128]{1,0:T(8,128)(2,1)S(1)}, bf16[816,128]{1,0:T(8,128)(2,1)S(1)}, u32[]{:S(2)}, u32[]{:S(2)}) collective-permute-start(bf16[816,128]{1,0:T(8,128)(2,1)S(1)} %collective-permute-done.14.refs_14_), channel_id=1, source_target_pairs={{0,1},{1,0},{2,3},{3,2},{4,5},{5,4},{6,7},{7,6},{8,9},{9,8},{10,11... | collective-permute-start | bytes 626696 | tf_op jit(solution)/shard_map/ppermute | solution.py:16
  72.4 1.5 %collective-permute-start.12 = (bf16[816,128]{1,0:T(8,128)(2,1)S(1)}, bf16[816,128]{1,0:T(8,128)(2,1)S(1)}, u32[]{:S(2)}, u32[]{:S(2)}) collective-permute-start(bf16[816,128]{1,0:T(8,128)(2,1)S(1)} %collective-permute-done.10.refs_12_), channel_id=1, source_target_pairs={{0,1},{1,0},{2,3},{3,2},{4,5},{5,4},{6,7},{7,6},{8,9},{9,8},{10,11... | collective-permute-start | bytes 626696 | tf_op jit(solution)/shard_map/ppermute | solution.py:16
  73.9 1.5 %collective-permute-start.8 = (bf16[816,128]{1,0:T(8,128)(2,1)S(1)}, bf16[816,128]{1,0:T(8,128)(2,1)S(1)}, u32[]{:S(2)}, u32[]{:S(2)}) collective-permute-start(bf16[816,128]{1,0:T(8,128)(2,1)S(1)} %collective-permute-done.6.refs_10_), channel_id=1, source_target_pairs={{0,1},{1,0},{2,3},{3,2},{4,5},{5,4},{6,7},{7,6},{8,9},{9,8},{10,11... | collective-permute-start | bytes 626696 | tf_op jit(solution)/shard_map/ppermute | solution.py:16
  94.8 24.9 %collective-permute-start.21 = (bf16[256,1024]{1,0:T(8,128)(2,1)S(1)}, bf16[256,1024]{1,0:T(8,128)(2,1)S(1)}, u32[]{:S(2)}, u32[]{:S(2)}) collective-permute-start(bf16[256,1024]{1,0:T(8,128)(2,1)S(1)} %collective-permute-done.17.refs_17_), channel_id=1, source_target_pairs={{0,16},{8,24},{16,0},{24,8},{1,17},{9,25},{17,1},{25,9},{2,18},{10... | collective-permute-start | bytes 1572872 | tf_op jit(solution)/shard_map/ppermute | solution.py:16
  95.3 24.4 %collective-permute-start.22 = (bf16[256,1024]{1,0:T(8,128)(2,1)S(1)}, bf16[256,1024]{1,0:T(8,128)(2,1)S(1)}, u32[]{:S(2)}, u32[]{:S(2)}) collective-permute-start(bf16[256,1024]{1,0:T(8,128)(2,1)S(1)} %collective-permute-done.20.refs_20_), channel_id=1, source_target_pairs={{0,8},{8,0},{16,24},{24,16},{1,9},{9,1},{17,25},{25,17},{2,10},{10... | collective-permute-start | bytes 1572872 | tf_op jit(solution)/shard_map/ppermute | solution.py:16
  96.8 1.2 copy-start.2
  98.0 0.9 copy-start.4
  98.9 0.9 copy-start.6
  99.8 0.9 copy-start.8
  100.7 0.9 copy-start.10
  119.7 3.4 %copy-start = (f32[2048,1024]{1,0:T(8,128)S(1)}, f32[2048,1024]{1,0:T(8,128)}, u32[]{:S(2)}) copy-start(f32[2048,1024]{1,0:T(8,128)} %get-tuple-element.7.acc) | copy-start | bytes 25165828
  123.1 1.6 %copy-start.1 = (bf16[4,2048,128]{2,1,0:T(8,128)(2,1)S(1)}, bf16[4,2048,128]{2,1,0:T(8,128)(2,1)}, u32[]{:S(2)}) copy-start(bf16[4,2048,128]{2,1,0:T(8,128)(2,1)} %get-tuple-element.8.late) | copy-start | bytes 6291460
  (2 other events, 1.2 us)

commit v2 on v0

v2 whole, which is shorter than its diff:
```python
import functools

import jax
import jax.numpy as jnp
from jax import lax
from jax.experimental import pallas as pl
from jax.experimental.pallas import tpu as pltpu
from jax.sharding import PartitionSpec as P

SLACK = 5 * 1024 * 1024
SMALL = 1024 * 1024
PAD = 16
TILE = 256


def swap(x, axis, offset):
    size = lax.axis_size(axis)
    return lax.ppermute(x, axis, [(i, i ^ offset) for i in range(size)])


def mark_kernel(*refs):
    refs[-1][...] = jnp.zeros_like(refs[-1])


def mark(arrays):
    return pl.pallas_call(
        mark_kernel,
        out_shape=jax.ShapeDtypeStruct((PAD, 128), jnp.bfloat16),
        in_specs=[pl.BlockSpec(memory_space=pl.ANY)] * len(arrays),
        compiler_params=pltpu.CompilerParams(vmem_limit_bytes=SMALL),
        name="mark",
    )(*arrays)


def hold_kernel(*refs):
    pass


def hold(array, others):
    return pl.pallas_call(
        hold_kernel,
        out_shape=jax.ShapeDtypeStruct(array.shape, array.dtype),
        in_specs=[pl.BlockSpec(memory_space=pl.ANY)] * (1 + len(others)),
        out_specs=pl.BlockSpec(memory_space=pl.ANY),
        input_output_aliases={0: 0},
        compiler_params=pltpu.CompilerParams(vmem_limit_bytes=SMALL),
        name="hold",
    )(array, *others)


def early_kernel(dims, arrays, early, spot, offsets, *refs):
    grid_rows, grid_cols, slots, panels, block = dims
    span = slots * block + PAD
    per_row = grid_cols // grid_rows
    record_refs = refs[:arrays]
    term_refs = refs[arrays:-12]
    previous, acc, late, terms, held, before, code_rows, codes, counts, firsts, depths, sems = refs[-12:]
    row_blocks = acc.shape[0] // block
    count = grid_rows * grid_cols
    nothing = count * span

    def fetch(sources, target, sem):
        copies, at = [], 0
        for ref in sources:
            rows = ref.shape[0]
            copies.append(pltpu.make_async_copy(ref, target.at[pl.ds(at, rows)], sem))
            at += rows
        for copy in copies:
            copy.start()
        return copies

    first = fetch(record_refs, held, sems.at[0])
    second = fetch(term_refs, terms, sems.at[1])
    third = fetch([previous], before, sems.at[2])
    late[...] = jnp.zeros_like(late)
    held[pl.ds(nothing, block), :] = jnp.zeros((block, held.shape[1]), held.dtype)

    def clear(i, carry):
        counts[i] = 0
        for n in range(early):
            firsts[i, n] = nothing
            depths[i, n] = 0
        return carry

    lax.fori_loop(0, row_blocks, clear, 0)
    for copy in first:
        copy.wait()
    for n in range(count):
        row = held[pl.ds(n * span + slots * block, PAD), :].astype(jnp.float32)
        code_rows[pl.ds(n, 1), :] = row[:1].astype(jnp.int32)
    to_scalars = pltpu.make_async_copy(code_rows, codes, sems.at[3])
    to_scalars.start()
    to_scalars.wait()
    my_row, my_col = spot[0], spot[1]

    def place(n, carry):
        col = my_col ^ offsets[n // grid_rows]
        source = (col // per_row) ^ my_row
        inner = col % per_row
        for j in range(slots):
            code = codes[n, j]
            row = code // panels
            k = (source * panels + code % panels) * per_row + inner
            start = pl.multiple_of(n * span + j * block, PAD)

            @pl.when((code >= 0) & (k < early))
            def _():
                at = counts[row]
                firsts[row, at] = start
                depths[row, at] = k * block
                counts[row] = at + 1

            @pl.when((code >= 0) & (k >= early))
            def _():
                to = pl.ds(pl.multiple_of(row * block, block), block)
                late[k - early, to, :] = held[pl.ds(start, block), :]

        return carry

    lax.fori_loop(0, count, place, 0)
    for copy in second + third:
        copy.wait()

    def pair(i, n):
        def one(m):
            left = held[pl.ds(pl.multiple_of(firsts[i, m], PAD), block), :]
            right = terms[pl.ds(pl.multiple_of(depths[i, m], block), block), :]
            return left, right

        (left0, right0), (left1, right1) = one(2 * n), one(2 * n + 1)
        return jnp.dot(
            jnp.concatenate([left0, left1], axis=1),
            jnp.concatenate([right0, right1], axis=0),
            preferred_element_type=jnp.float32,
        )

    for i in range(row_blocks):
        rows = pl.ds(i * block, block)
        product = pair(i, 0) + pair(i, 1)
        acc[rows, :] = 2.0 * product - before[rows, :].astype(jnp.float32)

    def more(i, carry):
        rows = pl.ds(pl.multiple_of(i * block, block), block)

        def step(n, inner):
            acc[rows, :] += 2.0 * pair(i, n)
            return inner

        return lax.fori_loop(2, (counts[i] + 1) // 2, step, carry)

    lax.fori_loop(0, row_blocks, more, 0)


def late_kernel(dims, keep, acc, late, *refs):
    block = dims[-1]
    term_refs, out, staged, sem = refs[:-3], refs[-3], refs[-2], refs[-1]
    blocks = late.shape[0]
    right = jnp.concatenate([ref[...] for ref in term_refs], axis=0)
    copies = []
    for t in range(acc.shape[0] // TILE):
        rows = pl.ds(t * TILE, TILE)
        left = jnp.concatenate([late[k, rows, :] for k in range(blocks)], axis=1)
        product = jnp.dot(left, right, preferred_element_type=jnp.float32)
        update = acc[rows, :] + 2.0 * product
        for i in range(TILE // block):
            for j in range(out.shape[1] // block):
                wanted = keep[t * (TILE // block) + i, j] > 0
                part = update[i * block : (i + 1) * block, j * block : (j + 1) * block]
                staged[pl.ds(t * TILE + i * block, block), pl.ds(j * block, block)] = jnp.where(
                    wanted, part, jnp.zeros_like(part)
                ).astype(out.dtype)
        copies.append(pltpu.make_async_copy(staged.at[rows], out.at[rows], sem))
        copies[-1].start()
    for copy in copies:
        copy.wait()


def per_device(send_blocks, send_count, send_place, term_current, term_previous, keep_mask):
    grid_rows, grid_cols = lax.axis_size("row"), lax.axis_size("col")
    my_row, my_col = lax.axis_index("row"), lax.axis_index("col")
    block = send_blocks.shape[-1]
    slots = send_blocks.shape[1]
    panels = term_current.shape[0]
    tile_rows, tile_cols = term_previous.shape
    row_blocks = tile_rows // block
    per_row = grid_cols // grid_rows
    dims = (grid_rows, grid_cols, slots, panels, block)

    lane = jnp.arange(slots, dtype=jnp.int32)
    places = jnp.where(lane[None, :] < send_count, send_place, -1).astype(jnp.bfloat16)
    pad = jnp.broadcast_to(
        jnp.pad(places, ((0, 0), (0, block - slots)))[:, None, :], (grid_rows, PAD, block)
    )

    def payload(offset):
        to = my_row ^ offset
        records = lax.dynamic_index_in_dim(send_blocks, to, 0, keepdims=False)
        tail = lax.dynamic_index_in_dim(pad, to, 0, keepdims=False)
        return jnp.concatenate([records.reshape(slots * block, block), tail], axis=0)

    mine = [term_current[p] for p in range(panels)]
    term = {}
    last = grid_rows - 1
    if grid_rows == 4 and panels == 2:
        term[1, 0] = swap(mine[0], "row", 1)
        term[2, 1] = swap(mine[1], "row", 2)
        term[1, 1] = swap(mine[1], "row", 1)
        term[2, 0] = swap(mine[0], "row", 2)
        term[3, 0] = swap(term[1, 0], "row", 2)
        term[3, 1] = swap(term[2, 1], "row", 1)
    else:
        for o in range(1, grid_rows):
            for p in range(panels):
                term[o, p] = swap(mine[p], "row", o)

    own = jnp.concatenate(
        [payload(0)] + [swap(payload(o), "row", o) for o in range(1, grid_rows)], axis=0
    )
    if grid_cols == 8:
        far, near = swap(own, "col", 6), swap(own, "col", 2)
        if grid_rows == 4:
            far = hold(far, [swap(mark([term[1, 0], term[2, 1]]), "col", 1)])
        middle = swap(far, "col", 2)
        if grid_rows == 4:
            token = swap(mark([term[1, 1], term[2, 0]]), "col", 1)
            middle = hold(middle, [swap(token, "col", 1)])
        offsets = [0, 2, 6, 4]
        parts = [own, near, far, middle]
        groups = [jnp.concatenate(parts[:3], axis=0), middle]
        others = [swap(group, "col", 1) for group in groups]
    else:
        offsets = list(range(0, grid_cols, 2))
        parts = [own] + [swap(own, "col", o) for o in offsets[1:]]
        others = [swap(part, "col", 1) for part in parts]
    offsets = offsets + [o ^ 1 for o in offsets]
    record_arrays = parts + others
    span = slots * block + PAD

    early = (grid_rows - 1) * panels * per_row
    anywhere = pl.BlockSpec(memory_space=pl.ANY)
    smem = pl.BlockSpec(memory_space=pltpu.SMEM)
    vmem = pl.BlockSpec(memory_space=pltpu.VMEM)
    early_terms = [term_current.reshape(-1, tile_cols)] + [
        term[o, p] for o in range(1, last) for p in range(panels)
    ]
    late_blocks = panels * per_row
    count = grid_cols * grid_rows
    early_bytes = 2 * (early * block * tile_cols + count * span * block + tile_rows * tile_cols)
    passed_bytes = 4 * tile_rows * tile_cols + 2 * late_blocks * tile_rows * block
    acc, late = pl.pallas_call(
        functools.partial(early_kernel, dims, len(record_arrays), early),
        out_shape=[
            jax.ShapeDtypeStruct((tile_rows, tile_cols), jnp.float32),
            jax.ShapeDtypeStruct((late_blocks, tile_rows, block), jnp.bfloat16),
        ],
        in_specs=[smem, smem] + [anywhere] * (len(record_arrays) + len(early_terms) + 1),
        out_specs=[vmem, vmem],
        scratch_shapes=[
            pltpu.VMEM((early * block, tile_cols), jnp.bfloat16),
            pltpu.VMEM((count * span + block, block), jnp.bfloat16),
            pltpu.VMEM((tile_rows, tile_cols), jnp.bfloat16),
            pltpu.VMEM((count, block), jnp.int32),
            pltpu.SMEM((count, block), jnp.int32),
            pltpu.SMEM((row_blocks,), jnp.int32),
            pltpu.SMEM((row_blocks, early), jnp.int32),
            pltpu.SMEM((row_blocks, early), jnp.int32),
            pltpu.SemaphoreType.DMA((4,)),
        ],
        compiler_params=pltpu.CompilerParams(vmem_limit_bytes=early_bytes + passed_bytes + SLACK),
        name="early_product",
    )(
        jnp.stack([my_row, my_col]).astype(jnp.int32),
        jnp.array(offsets, jnp.int32),
        *record_arrays,
        *early_terms,
        term_previous,
    )
    return pl.pallas_call(
        functools.partial(late_kernel, dims),
        out_shape=jax.ShapeDtypeStruct((tile_rows, tile_cols), term_previous.dtype),
        in_specs=[smem, vmem, vmem] + [vmem] * panels,
        out_specs=anywhere,
        scratch_shapes=[
            pltpu.VMEM((tile_rows, tile_cols), term_previous.dtype),
            pltpu.SemaphoreType.DMA,
        ],
        compiler_params=pltpu.CompilerParams(vmem_limit_bytes=passed_bytes + 2 * tile_rows * tile_cols + SLACK),
        name="late_product",
    )(keep_mask, acc, late, *[term[last, p] for p in range(panels)])


def solution(mesh):
    placed = (
        P("row", "col", None, None),
        P("row", "col"),
        P("row", "col"),
        P(None, "row", "col"),
        P("row", "col"),
        P("row", "col"),
    )
    return jax.shard_map(
        per_device, mesh=mesh, in_specs=placed, out_specs=P("row", "col"), check_vma=False
    )
```

time: 206 us -> 66.5 us (0.32)
  waiting for transfers between devices: 149 us -> 26.3 us
  matrix products: 25.4 us -> 0 us
  between operations: 13.2 us -> 0.11 us
  Pallas kernels: 0 us -> 12.5 us
  starting transfers between devices: 3.53 us -> 15 us
  blocking collectives: 9.6 us -> 0 us
  local copies, waits for them, and re-layouts: 4.4 us -> 11.3 us
    all_gather x4 -> x0, waiting for transfers between devices: 140 us -> none  [the longest x2 98.7 us: per_device(): lax.all_gather(own_part, 'col', axis=1, tiled=True)]
    ppermute x0 -> x17, waiting for transfers between devices: none -> 26.3 us  [swap(): return lax.ppermute(x, axis, [(i, i ^ offset) for i in range(size)])]
    dot_general x3 -> x0, matrix products: 25.4 us -> none  [the longest x2 24.9 us: add_portion(): jnp.dot(portion, term_panel, preferred_element_type=jnp.float32)]
    ppermute x0 -> x17, starting transfers between devices: none -> 15 us  [swap(): return lax.ppermute(x, axis, [(i, i ^ offset) for i in range(size)])]
    pallas_call x0 -> x6, Pallas kernels: none -> 12.5 us  [the longest x1 7.94 us: per_device(): pl.pallas_call(functools.partial(early_kernel, dims, len(record_arrays),...]
    all_to_all x1 -> x0, blocking collectives: 9.6 us -> none  [per_device(): lax.all_to_all(slot_codes, 'row', split_axis=0, concat_axis=0, tiled=True)]
    unnamed x3 -> x23, local copies, waits for them, and re-layouts: 0.24 us -> 8.15 us
    all_to_all x1 -> x0, waiting for transfers between devices: 7.8 us -> none  [per_device(): lax.all_to_all(send_blocks, 'row', split_axis=0, concat_axis=0, tiled=True)]
  transfers between devices with their start and end apart: 5 -> 17, of which waited for: 5 -> 8; matrix products, arithmetic and copies ran while one was open for 6% -> 9% of each run, Pallas kernels for 0% -> 12%
where the time goes in v2:
time: 66.5 us; the launch traced here: 66.2 us
  waiting for transfers between devices  26.3 us (40%)
  starting transfers between devices  15 us (23%)
  Pallas kernels  12.5 us (19%)
  local copies, waits for them, and re-layouts  11.3 us (17%)
  other arithmetic  0.88 us (1%)
    ppermute x17, waiting for transfers between devices, swap(): return lax.ppermute(x, axis, [(i, i ^ offset) for i in range(size)])  26.3 us
    ppermute x17, starting transfers between devices, swap(): return lax.ppermute(x, axis, [(i, i ^ offset) for i in range(size)])  15 us
    unnamed x23, local copies, waits for them, and re-layouts  8.15 us
    pallas_call x1, Pallas kernels, per_device(): pl.pallas_call(functools.partial(early_kernel, dims, len(record_arrays),...  7.94 us
    pallas_call x1, Pallas kernels, per_device(): pl.pallas_call(functools.partial(late_kernel, dims), out_shape=jax.ShapeD...  4.58 us
  transfers between devices with their start and end apart: 17, of which 8 were waited for; matrix products, arithmetic and copies ran while one was open for 9% of the time, Pallas kernels for 12%

profile of v2, /device:TPU:0, one launch (start us, length us, event | category | flops | bytes accessed | tf_op | source)
XLA Modules:
  0.0 66.2 jit_solution(15623395371306203343)
XLA Ops:
  0.0 0.8 %fusion.4 = bf16[4,2]{0,1:T(2,128)(2,1)S(1)} fusion(s32[4,2]{0,1:T(2,128)} %param.9, s32[4]{0:T(128)} %bitcast.17), kind=kLoop, calls=%fused_computation.30 | loop fusion | flops 24 | bytes 64 | tf_op jit(solution)/shard_map/convert_element_type | solution.py:190
  0.8 1.0 %constant_dynamic-slice_fusion = (bf16[1,2,128,128]{3,2,1,0:T(8,128)(2,1)S(1)}, bf16[1,2,128,128]{3,2,1,0:T(8,128)(2,1)S(1)}, bf16[1,2,128,128]{3,2,1,0:T(8,128)(2,1)S(1)}, bf16[1,2,128,128]{3,2,1,0:T(8,128)(2,1)S(1)}) fusion(bf16[4,2,128,128]{3,2,1,0:T(8,128)(2,1)} %param.7, s32[]{:T(128)S(6)} %select_n.26, s32[]{:T(128)S(6)} %select_n.24, ...), kind=kLoop, calls=%fused_computation.25 | loop fusion | bytes 524304 | tf_op jit(solution)/shard_map/jit(dynamic_index_in_dim)/dynamic_slice | solution.py:197
  2.0 3.0 %collective-permute-start = (bf16[272,128]{1,0:T(8,128)(2,1)S(1)}, bf16[272,128]{1,0:T(8,128)(2,1)S(1)}, u32[]{:S(2)}, u32[]{:S(2)}) collective-permute-start(bf16[272,128]{1,0:T(8,128)(2,1)S(1)} %pad_maximum_fusion), channel_id=1, source_target_pairs={{0,8},{8,0},{16,24},{24,16},{1,9},{9,1},{17,25},{25,17},{2,10},{10... | collective-permute-start | bytes 208904 | tf_op jit(solution)/shard_map/ppermute | solution.py:18
  5.0 1.6 %collective-permute-start.1 = (bf16[272,128]{1,0:T(8,128)(2,1)S(1)}, bf16[272,128]{1,0:T(8,128)(2,1)S(1)}, u32[]{:S(2)}, u32[]{:S(2)}) collective-permute-start(bf16[272,128]{1,0:T(8,128)(2,1)S(1)} %pad_maximum_fusion.1), channel_id=1, source_target_pairs={{0,16},{8,24},{16,0},{24,8},{1,17},{9,25},{17,1},{25,9},{2,18},{10... | collective-permute-start | bytes 208904 | tf_op jit(solution)/shard_map/ppermute | solution.py:18
  6.7 1.3 %slice_bitcast_fusion = (bf16[256,1024]{1,0:T(8,128)(2,1)S(1)}, bf16[256,1024]{1,0:T(8,128)(2,1)S(1)}) fusion(bf16[2,256,1024]{2,1,0:T(8,128)(2,1)} %param.10), kind=kLoop, calls=%fused_computation | loop fusion | bytes 2097152 | tf_op jit(solution)/shard_map/squeeze | solution.py:201
  8.0 2.0 %collective-permute-start.5 = (bf16[256,1024]{1,0:T(8,128)(2,1)S(1)}, bf16[256,1024]{1,0:T(8,128)(2,1)S(1)}, u32[]{:S(2)}, u32[]{:S(2)}) collective-permute-start(bf16[256,1024]{1,0:T(8,128)(2,1)S(1)} %get-tuple-element.14), channel_id=1, source_target_pairs={{0,8},{8,0},{16,24},{24,16},{1,9},{9,1},{17,25},{25,17},{2,10},{10... | collective-permute-start | bytes 1572872 | tf_op jit(solution)/shard_map/ppermute | solution.py:18
  10.0 1.5 %collective-permute-start.6 = (bf16[256,1024]{1,0:T(8,128)(2,1)S(1)}, bf16[256,1024]{1,0:T(8,128)(2,1)S(1)}, u32[]{:S(2)}, u32[]{:S(2)}) collective-permute-start(bf16[256,1024]{1,0:T(8,128)(2,1)S(1)} %get-tuple-element.13), channel_id=1, source_target_pairs={{0,16},{8,24},{16,0},{24,8},{1,17},{9,25},{17,1},{25,9},{2,18},{10... | collective-permute-start | bytes 1572872 | tf_op jit(solution)/shard_map/ppermute | solution.py:18
  11.5 0.6 constant_dynamic-update-slice_fusion.11
  12.1 0.6 constant_dynamic-update-slice_fusion.10
  12.7 0.6 constant_dynamic-update-slice_fusion.9
  13.4 0.6 constant_dynamic-update-slice_fusion.8
  14.0 0.6 constant_dynamic-update-slice_fusion.7
  14.7 1.6 %collective-permute-start.3 = (bf16[1088,128]{1,0:T(8,128)(2,1)S(1)}, bf16[1088,128]{1,0:T(8,128)(2,1)S(1)}, u32[]{:S(2)}, u32[]{:S(2)}) collective-permute-start(bf16[1088,128]{1,0:T(8,128)(2,1)S(1)} %get-tuple-element.20.refs_0_), channel_id=1, source_target_pairs={{0,2},{1,3},{2,0},{3,1},{4,6},{5,7},{6,4},{7,5},{8,10},{9,11},{10,... | collective-permute-start | bytes 835592 | tf_op jit(solution)/shard_map/ppermute | solution.py:18
  16.2 2.5 %collective-permute-start.4 = (bf16[1088,128]{1,0:T(8,128)(2,1)S(1)}, bf16[1088,128]{1,0:T(8,128)(2,1)S(1)}, u32[]{:S(2)}, u32[]{:S(2)}) collective-permute-start(bf16[1088,128]{1,0:T(8,128)(2,1)S(1)} %get-tuple-element.20.refs_0_), channel_id=1, source_target_pairs={{0,6},{1,7},{2,4},{3,5},{4,2},{5,3},{6,0},{7,1},{8,14},{9,15},{10,... | collective-permute-start | bytes 835592 | tf_op jit(solution)/shard_map/ppermute | solution.py:18
  18.7 0.5 collective-permute-start.10
  19.2 2.6 %collective-permute-done.5.refs_0_.refs_7_ = bf16[256,1024]{1,0:T(8,128)(2,1)S(1)} collective-permute-done((bf16[256,1024]{1,0:T(8,128)(2,1)S(1)}, bf16[256,1024]{1,0:T(8,128)(2,1)S(1)}, u32[]{:S(2)}, u32[]{:S(2)}) %collective-permute-start.5) | collective-permute-done | bytes 524320 | tf_op jit(solution)/shard_map/ppermute | solution.py:18
  21.9 3.0 %collective-permute-done.6.refs_1_.refs_10_ = bf16[256,1024]{1,0:T(8,128)(2,1)S(1)} collective-permute-done((bf16[256,1024]{1,0:T(8,128)(2,1)S(1)}, bf16[256,1024]{1,0:T(8,128)(2,1)S(1)}, u32[]{:S(2)}, u32[]{:S(2)}) %collective-permute-start.6) | collective-permute-done | bytes 524320 | tf_op jit(solution)/shard_map/ppermute | solution.py:18
  24.9 0.8 %constant_dynamic-update-slice_fusion.6 = bf16[3264,128]{1,0:T(8,128)(2,1)} fusion(bf16[3264,128]{1,0:T(8,128)(2,1)} %get-tuple-element.19, bf16[1088,128]{1,0:T(8,128)(2,1)S(1)} %collective-permute-done.3.refs_1_), kind=kLoop, calls=%fused_computation.19 | loop fusion | bytes 557056
  25.7 4.1 %collective-permute-done.4.refs_0_ = bf16[1088,128]{1,0:T(8,128)(2,1)S(1)} collective-permute-done((bf16[1088,128]{1,0:T(8,128)(2,1)S(1)}, bf16[1088,128]{1,0:T(8,128)(2,1)S(1)}, u32[]{:S(2)}, u32[]{:S(2)}) %collective-permute-start.4) | collective-permute-done | bytes 278560 | tf_op jit(solution)/shard_map/ppermute | solution.py:18
  29.8 0.7 %constant_dynamic-update-slice_fusion.5 = bf16[3264,128]{1,0:T(8,128)(2,1)} fusion(bf16[3264,128]{1,0:T(8,128)(2,1)} %constant_dynamic-update-slice_fusion.6, bf16[1088,128]{1,0:T(8,128)(2,1)S(1)} %hold.2.refs_2_), kind=kLoop, calls=%fused_computation.18 | loop fusion | bytes 557056 | tf_op jit(solution)/shard_map/concatenate | solution.py:229
  30.5 0.5 collective-permute-start.9
  31.0 0.6 collective-permute-start.8
  32.1 2.5 %collective-permute-done.10.refs_1_.refs_9_ = bf16[256,1024]{1,0:T(8,128)(2,1)S(1)} collective-permute-done((bf16[256,1024]{1,0:T(8,128)(2,1)S(1)}, bf16[256,1024]{1,0:T(8,128)(2,1)S(1)}, u32[]{:S(2)}, u32[]{:S(2)}) %collective-permute-start.10) | collective-permute-done | bytes 524320 | tf_op jit(solution)/shard_map/ppermute | solution.py:18
  34.9 10.4 %collective-permute-done.9.refs_0_.refs_8_ = bf16[256,1024]{1,0:T(8,128)(2,1)S(1)} collective-permute-done((bf16[256,1024]{1,0:T(8,128)(2,1)S(1)}, bf16[256,1024]{1,0:T(8,128)(2,1)S(1)}, u32[]{:S(2)}, u32[]{:S(2)}) %collective-permute-start.9) | collective-permute-done | bytes 524320 | tf_op jit(solution)/shard_map/ppermute | solution.py:18
  45.2 1.2 %collective-permute-done.11 = bf16[16,128]{1,0:T(8,128)(2,1)S(1)} collective-permute-done((bf16[16,128]{1,0:T(8,128)(2,1)S(1)}, bf16[16,128]{1,0:T(8,128)(2,1)S(1)}, u32[]{:S(2)}, u32[]{:S(2)}) %collective-permute-start.11) | collective-permute-done | bytes 4128 | tf_op jit(solution)/shard_map/ppermute | solution.py:18
  46.6 1.0 %collective-permute-done.12.refs_1_ = bf16[16,128]{1,0:T(8,128)(2,1)S(1)} collective-permute-done((bf16[16,128]{1,0:T(8,128)(2,1)S(1)}, bf16[16,128]{1,0:T(8,128)(2,1)S(1)}, u32[]{:S(2)}, u32[]{:S(2)}) %collective-permute-start.12) | collective-permute-done | bytes 4128 | tf_op jit(solution)/shard_map/ppermute | solution.py:18
  48.0 1.6 %collective-permute-done.14.refs_5_ = bf16[1088,128]{1,0:T(8,128)(2,1)} collective-permute-done((bf16[1088,128]{1,0:T(8,128)(2,1)}, bf16[1088,128]{1,0:T(8,128)(2,1)}, u32[]{:S(2)}, u32[]{:S(2)}) %collective-permute-start.14) | collective-permute-done | bytes 278560 | tf_op jit(solution)/shard_map/ppermute | solution.py:18
  49.6 2.2 %copy-done = bf16[2048,1024]{1,0:T(8,128)(2,1)S(1)} copy-done((bf16[2048,1024]{1,0:T(8,128)(2,1)S(1)}, bf16[2048,1024]{1,0:T(8,128)(2,1)}, u32[]{:S(2)}) %copy-start) | copy-done | bytes 4194328
  51.7 1.0 %copy-done.3 = bf16[1088,128]{1,0:T(8,128)(2,1)S(1)} copy-done((bf16[1088,128]{1,0:T(8,128)(2,1)S(1)}, bf16[1088,128]{1,0:T(8,128)(2,1)}, u32[]{:S(2)}) %copy-start.3) | copy-done | bytes 278552
  52.7 1.0 %copy-done.5 = bf16[1088,128]{1,0:T(8,128)(2,1)S(1)} copy-done((bf16[1088,128]{1,0:T(8,128)(2,1)S(1)}, bf16[1088,128]{1,0:T(8,128)(2,1)}, u32[]{:S(2)}) %copy-start.5) | copy-done | bytes 278552
  53.7 7.9 %early_product.1 = (f32[2048,1024]{1,0:T(8,128)S(1)}, bf16[4,2048,128]{2,1,0:T(8,128)(2,1)S(1)}) custom-call(s32[2]{0:T(128)S(1)} %pad_add_fusion.spot, s32[8]{0:T(128)S(1)} %copy-done.6, bf16[1088,128]{1,0:T(8,128)(2,1)S(1)} %copy-done.5, bf16[1088,128]{1,0:T(8,128)(2,1)S(1)} %copy-done.3, bf16[1088,128]{1,0:T(8,128)(2,1)S(1)} %hold.2.refs_2_, ...), custom_call_target="tpu_custom_call" | custom-call | tf_op jit(solution)/shard_map/early_product/pallas_call | solution.py:250
  61.6 4.6 %late_product.1 = bf16[2048,1024]{1,0:T(8,128)(2,1)} custom-call(s32[16,8]{1,0:T(8,128)S(1)} %copy.11.keep, f32[2048,1024]{1,0:T(8,128)S(1)} %get-tuple-element.7.acc, bf16[4,2048,128]{2,1,0:T(8,128)(2,1)S(1)} %get-tuple-element.8.late, bf16[256,1024]{1,0:T(8,128)(2,1)} %collective-permute-done.15.refs_0_, bf16[256,1024]{1,0:T(8,128)(2,1)} %collective-permute-done.16.refs_1_), custom_call_target="tpu_custom_call" | custom-call | tf_op jit(solution)/shard_map/late_product/pallas_call | solution.py:278
  (43 shorter events, 1.7 us)
Async XLA Ops:
  0.0 49.5 %copy-start.6 = (s32[8]{0:T(128)S(1)}, s32[8]{0:T(128)}, u32[]{:S(2)}) copy-start(s32[8]{0:T(128)} %constant.44.clone.offsets) | copy-start | bytes 100
  0.0 49.5 %copy-start.1 = (bf16[2,256,1024]{2,1,0:T(8,128)(2,1)S(1)}, bf16[2,256,1024]{2,1,0:T(8,128)(2,1)}, u32[]{:S(2)}) copy-start(bf16[2,256,1024]{2,1,0:T(8,128)(2,1)} %param.10) | copy-start | bytes 3145732
  0.0 47.8 %copy-start.7 = (s32[16,8]{0,1:T(8,128)S(1)}, s32[16,8]{0,1:T(8,128)}, u32[]{:S(2)}) copy-start(s32[16,8]{0,1:T(8,128)} %param.12) | copy-start | bytes 1540
  2.0 10.8 %collective-permute-start = (bf16[272,128]{1,0:T(8,128)(2,1)S(1)}, bf16[272,128]{1,0:T(8,128)(2,1)S(1)}, u32[]{:S(2)}, u32[]{:S(2)}) collective-permute-start(bf16[272,128]{1,0:T(8,128)(2,1)S(1)} %pad_maximum_fusion), channel_id=1, source_target_pairs={{0,8},{8,0},{16,24},{24,16},{1,9},{9,1},{17,25},{25,17},{2,10},{10... | collective-permute-start | bytes 208904 | tf_op jit(solution)/shard_map/ppermute | solution.py:18
  5.0 8.4 %collective-permute-start.1 = (bf16[272,128]{1,0:T(8,128)(2,1)S(1)}, bf16[272,128]{1,0:T(8,128)(2,1)S(1)}, u32[]{:S(2)}, u32[]{:S(2)}) collective-permute-start(bf16[272,128]{1,0:T(8,128)(2,1)S(1)} %pad_maximum_fusion.1), channel_id=1, source_target_pairs={{0,16},{8,24},{16,0},{24,8},{1,17},{9,25},{17,1},{25,9},{2,18},{10... | collective-permute-start | bytes 208904 | tf_op jit(solution)/shard_map/ppermute | solution.py:18
  6.6 7.4 %collective-permute-start.2 = (bf16[272,128]{1,0:T(8,128)(2,1)S(1)}, bf16[272,128]{1,0:T(8,128)(2,1)S(1)}, u32[]{:S(2)}, u32[]{:S(2)}) collective-permute-start(bf16[272,128]{1,0:T(8,128)(2,1)S(1)} %pad_maximum_fusion.2), channel_id=1, source_target_pairs={{0,24},{8,16},{16,8},{24,0},{1,25},{9,17},{17,9},{25,1},{2,26},{10... | collective-permute-start | bytes 208904 | tf_op jit(solution)/shard_map/ppermute | solution.py:18
  8.0 13.9 %collective-permute-start.5 = (bf16[256,1024]{1,0:T(8,128)(2,1)S(1)}, bf16[256,1024]{1,0:T(8,128)(2,1)S(1)}, u32[]{:S(2)}, u32[]{:S(2)}) collective-permute-start(bf16[256,1024]{1,0:T(8,128)(2,1)S(1)} %get-tuple-element.14), channel_id=1, source_target_pairs={{0,8},{8,0},{16,24},{24,16},{1,9},{9,1},{17,25},{25,17},{2,10},{10... | collective-permute-start | bytes 1572872 | tf_op jit(solution)/shard_map/ppermute | solution.py:18
  10.0 14.9 %collective-permute-start.6 = (bf16[256,1024]{1,0:T(8,128)(2,1)S(1)}, bf16[256,1024]{1,0:T(8,128)(2,1)S(1)}, u32[]{:S(2)}, u32[]{:S(2)}) collective-permute-start(bf16[256,1024]{1,0:T(8,128)(2,1)S(1)} %get-tuple-element.13), channel_id=1, source_target_pairs={{0,16},{8,24},{16,0},{24,8},{1,17},{9,25},{17,1},{25,9},{2,18},{10... | collective-permute-start | bytes 1572872 | tf_op jit(solution)/shard_map/ppermute | solution.py:18
  14.7 32.9 %copy-start.4 = (bf16[1088,128]{1,0:T(8,128)(2,1)}, bf16[1088,128]{1,0:T(8,128)(2,1)S(1)}, u32[]{:S(2)}) copy-start(bf16[1088,128]{1,0:T(8,128)(2,1)S(1)} %get-tuple-element.20.refs_0_) | copy-start | bytes 835588
  14.7 10.2 %collective-permute-start.3 = (bf16[1088,128]{1,0:T(8,128)(2,1)S(1)}, bf16[1088,128]{1,0:T(8,128)(2,1)S(1)}, u32[]{:S(2)}, u32[]{:S(2)}) collective-permute-start(bf16[1088,128]{1,0:T(8,128)(2,1)S(1)} %get-tuple-element.20.refs_0_), channel_id=1, source_target_pairs={{0,2},{1,3},{2,0},{3,1},{4,6},{5,7},{6,4},{7,5},{8,10},{9,11},{10,... | collective-permute-start | bytes 835592 | tf_op jit(solution)/shard_map/ppermute | solution.py:18
  16.2 13.5 %collective-permute-start.4 = (bf16[1088,128]{1,0:T(8,128)(2,1)S(1)}, bf16[1088,128]{1,0:T(8,128)(2,1)S(1)}, u32[]{:S(2)}, u32[]{:S(2)}) collective-permute-start(bf16[1088,128]{1,0:T(8,128)(2,1)S(1)} %get-tuple-element.20.refs_0_), channel_id=1, source_target_pairs={{0,6},{1,7},{2,4},{3,5},{4,2},{5,3},{6,0},{7,1},{8,14},{9,15},{10,... | collective-permute-start | bytes 835592 | tf_op jit(solution)/shard_map/ppermute | solution.py:18
  18.7 15.9 %collective-permute-start.10 = (bf16[256,1024]{1,0:T(8,128)(2,1)S(1)}, bf16[256,1024]{1,0:T(8,128)(2,1)S(1)}, u32[]{:S(2)}, u32[]{:S(2)}) collective-permute-start(bf16[256,1024]{1,0:T(8,128)(2,1)S(1)} %get-tuple-element.14), channel_id=1, source_target_pairs={{0,16},{8,24},{16,0},{24,8},{1,17},{9,25},{17,1},{25,9},{2,18},{10... | collective-permute-start | bytes 1572872 | tf_op jit(solution)/shard_map/ppermute | solution.py:18
  24.8 4.9 %collective-permute-start.7 = (bf16[16,128]{1,0:T(8,128)(2,1)S(1)}, bf16[16,128]{1,0:T(8,128)(2,1)S(1)}, u32[]{:S(2)}, u32[]{:S(2)}) collective-permute-start(bf16[16,128]{1,0:T(8,128)(2,1)S(1)} %mark.2), channel_id=1, source_target_pairs={{0,1},{1,0},{2,3},{3,2},{4,5},{5,4},{6,7},{7,6},{8,9},{9,8},{10,11... | collective-permute-start | bytes 12296 | tf_op jit(solution)/shard_map/ppermute | solution.py:18
  24.8 22.7 %copy-start.2 = (bf16[1088,128]{1,0:T(8,128)(2,1)}, bf16[1088,128]{1,0:T(8,128)(2,1)S(1)}, u32[]{:S(2)}) copy-start(bf16[1088,128]{1,0:T(8,128)(2,1)S(1)} %collective-permute-done.3.refs_1_) | copy-start | bytes 835588
  30.5 19.0 %collective-permute-start.13 = (bf16[3264,128]{1,0:T(8,128)(2,1)}, bf16[3264,128]{1,0:T(8,128)(2,1)}, u32[]{:S(2)}, u32[]{:S(2)}) collective-permute-start(bf16[3264,128]{1,0:T(8,128)(2,1)} %constant_dynamic-update-slice_fusion.5), channel_id=1, source_target_pairs={{0,1},{1,0},{2,3},{3,2},{4,5},{5,4},{6,7},{7,6},{8,9},{9,8},{10,11... | collective-permute-start | bytes 2506760 | tf_op jit(solution)/shard_map/ppermute | solution.py:18
  30.5 14.7 %collective-permute-start.9 = (bf16[256,1024]{1,0:T(8,128)(2,1)S(1)}, bf16[256,1024]{1,0:T(8,128)(2,1)S(1)}, u32[]{:S(2)}, u32[]{:S(2)}) collective-permute-start(bf16[256,1024]{1,0:T(8,128)(2,1)S(1)} %get-tuple-element.13), channel_id=1, source_target_pairs={{0,8},{8,0},{16,24},{24,16},{1,9},{9,1},{17,25},{25,17},{2,10},{10... | collective-permute-start | bytes 1572872 | tf_op jit(solution)/shard_map/ppermute | solution.py:18
  31.0 16.5 %collective-permute-start.8 = (bf16[1088,128]{1,0:T(8,128)(2,1)S(1)}, bf16[1088,128]{1,0:T(8,128)(2,1)}, u32[]{:S(2)}, u32[]{:S(2)}) collective-permute-start(bf16[1088,128]{1,0:T(8,128)(2,1)S(1)} %hold.2.refs_2_), channel_id=1, source_target_pairs={{0,2},{1,3},{2,0},{3,1},{4,6},{5,7},{6,4},{7,5},{8,10},{9,11},{10,... | collective-permute-start | bytes 835592 | tf_op jit(solution)/shard_map/ppermute | solution.py:18
  31.6 30.0 %collective-permute-start.15 = (bf16[256,1024]{1,0:T(8,128)(2,1)S(1)}, bf16[256,1024]{1,0:T(8,128)(2,1)}, u32[]{:S(2)}, u32[]{:S(2)}) collective-permute-start(bf16[256,1024]{1,0:T(8,128)(2,1)S(1)} %collective-permute-done.5.refs_0_.refs_7_), channel_id=1, source_target_pairs={{0,16},{8,24},{16,0},{24,8},{1,17},{9,25},{17,1},{25,9},{2,18},{10... | collective-permute-start | bytes 1572872 | tf_op jit(solution)/shard_map/ppermute | solution.py:18
  34.6 27.0 %collective-permute-start.16 = (bf16[256,1024]{1,0:T(8,128)(2,1)S(1)}, bf16[256,1024]{1,0:T(8,128)(2,1)}, u32[]{:S(2)}, u32[]{:S(2)}) collective-permute-start(bf16[256,1024]{1,0:T(8,128)(2,1)S(1)} %collective-permute-done.6.refs_1_.refs_10_), channel_id=1, source_target_pairs={{0,8},{8,0},{16,24},{24,16},{1,9},{9,1},{17,25},{25,17},{2,10},{10... | collective-permute-start | bytes 1572872 | tf_op jit(solution)/shard_map/ppermute | solution.py:18
  45.2 1.2 %collective-permute-start.11 = (bf16[16,128]{1,0:T(8,128)(2,1)S(1)}, bf16[16,128]{1,0:T(8,128)(2,1)S(1)}, u32[]{:S(2)}, u32[]{:S(2)}) collective-permute-start(bf16[16,128]{1,0:T(8,128)(2,1)S(1)} %mark.3), channel_id=1, source_target_pairs={{0,1},{1,0},{2,3},{3,2},{4,5},{5,4},{6,7},{7,6},{8,9},{9,8},{10,11... | collective-permute-start | bytes 12296 | tf_op jit(solution)/shard_map/ppermute | solution.py:18
  46.4 1.2 %collective-permute-start.12 = (bf16[16,128]{1,0:T(8,128)(2,1)S(1)}, bf16[16,128]{1,0:T(8,128)(2,1)S(1)}, u32[]{:S(2)}, u32[]{:S(2)}) collective-permute-start(bf16[16,128]{1,0:T(8,128)(2,1)S(1)} %collective-permute-done.11), channel_id=1, source_target_pairs={{0,1},{1,0},{2,3},{3,2},{4,5},{5,4},{6,7},{7,6},{8,9},{9,8},{10,11... | collective-permute-start | bytes 12296 | tf_op jit(solution)/shard_map/ppermute | solution.py:18
  47.6 2.0 %collective-permute-start.14 = (bf16[1088,128]{1,0:T(8,128)(2,1)}, bf16[1088,128]{1,0:T(8,128)(2,1)}, u32[]{:S(2)}, u32[]{:S(2)}) collective-permute-start(bf16[1088,128]{1,0:T(8,128)(2,1)} %hold.3.refs_3_), channel_id=1, source_target_pairs={{0,1},{1,0},{2,3},{3,2},{4,5},{5,4},{6,7},{7,6},{8,9},{9,8},{10,11... | collective-permute-start | bytes 835592 | tf_op jit(solution)/shard_map/ppermute | solution.py:18
  49.6 2.2 %copy-start = (bf16[2048,1024]{1,0:T(8,128)(2,1)S(1)}, bf16[2048,1024]{1,0:T(8,128)(2,1)}, u32[]{:S(2)}) copy-start(bf16[2048,1024]{1,0:T(8,128)(2,1)} %refs_11_.1) | copy-start | bytes 12582916
  51.7 1.0 %copy-start.3 = (bf16[1088,128]{1,0:T(8,128)(2,1)S(1)}, bf16[1088,128]{1,0:T(8,128)(2,1)}, u32[]{:S(2)}) copy-start(bf16[1088,128]{1,0:T(8,128)(2,1)} %copy-done.2) | copy-start | bytes 835588
  52.7 1.0 %copy-start.5 = (bf16[1088,128]{1,0:T(8,128)(2,1)S(1)}, bf16[1088,128]{1,0:T(8,128)(2,1)}, u32[]{:S(2)}) copy-start(bf16[1088,128]{1,0:T(8,128)(2,1)} %copy-done.4) | copy-start | bytes 835588

commit v3 on v2

--- a/solution.py
+++ b/solution.py
@@ -8,7 +8,6 @@
 from jax.sharding import PartitionSpec as P
 
 SLACK = 5 * 1024 * 1024
-SMALL = 1024 * 1024
 PAD = 16
 TILE = 256
 
@@ -18,60 +17,34 @@
     return lax.ppermute(x, axis, [(i, i ^ offset) for i in range(size)])
 
 
-def mark_kernel(*refs):
-    refs[-1][...] = jnp.zeros_like(refs[-1])
-
-
-def mark(arrays):
-    return pl.pallas_call(
-        mark_kernel,
-        out_shape=jax.ShapeDtypeStruct((PAD, 128), jnp.bfloat16),
-        in_specs=[pl.BlockSpec(memory_space=pl.ANY)] * len(arrays),
-        compiler_params=pltpu.CompilerParams(vmem_limit_bytes=SMALL),
-        name="mark",
-    )(*arrays)
-
-
-def hold_kernel(*refs):
-    pass
-
-
-def hold(array, others):
-    return pl.pallas_call(
-        hold_kernel,
-        out_shape=jax.ShapeDtypeStruct(array.shape, array.dtype),
-        in_specs=[pl.BlockSpec(memory_space=pl.ANY)] * (1 + len(others)),
-        out_specs=pl.BlockSpec(memory_space=pl.ANY),
-        input_output_aliases={0: 0},
-        compiler_params=pltpu.CompilerParams(vmem_limit_bytes=SMALL),
-        name="hold",
-    )(array, *others)
-
-
-def early_kernel(dims, arrays, early, spot, offsets, *refs):
+def early_kernel(dims, arrays, early, routes, spot, offsets, *refs):
     grid_rows, grid_cols, slots, panels, block = dims
     span = slots * block + PAD
     per_row = grid_cols // grid_rows
     record_refs = refs[:arrays]
-    term_refs = refs[arrays:-12]
-    previous, acc, late, terms, held, before, code_rows, codes, counts, firsts, depths, sems = refs[-12:]
+    term_refs = refs[arrays:-11]
+    previous, acc, late, terms, held, code_rows, codes, counts, firsts, depths, sems = refs[-11:]
     row_blocks = acc.shape[0] // block
     count = grid_rows * grid_cols
     nothing = count * span
 
-    def fetch(sources, target, sem):
-        copies, at = [], 0
-        for ref in sources:
-            rows = ref.shape[0]
-            copies.append(pltpu.make_async_copy(ref, target.at[pl.ds(at, rows)], sem))
-            at += rows
+    def fetch(copies):
         for copy in copies:
             copy.start()
         return copies
 
-    first = fetch(record_refs, held, sems.at[0])
-    second = fetch(term_refs, terms, sems.at[1])
-    third = fetch([previous], before, sems.at[2])
+    at, first = 0, []
+    for ref in record_refs:
+        rows = pl.ds(at, ref.shape[0])
+        first.append(pltpu.make_async_copy(ref, held.at[rows], sems.at[0]))
+        at += ref.shape[0]
+    first = fetch(first)
+    second = []
+    for ref, route in zip(term_refs, routes):
+        for source, target, size in route:
+            here, there = pl.ds(source, size), pl.ds(target, size)
+            second.append(pltpu.make_async_copy(ref.at[here], terms.at[there], sems.at[1]))
+    second = fetch(second)
     late[...] = jnp.zeros_like(late)
     held[pl.ds(nothing, block), :] = jnp.zeros((block, held.shape[1]), held.dtype)
 
@@ -88,7 +61,7 @@
     for n in range(count):
         row = held[pl.ds(n * span + slots * block, PAD), :].astype(jnp.float32)
         code_rows[pl.ds(n, 1), :] = row[:1].astype(jnp.int32)
-    to_scalars = pltpu.make_async_copy(code_rows, codes, sems.at[3])
+    to_scalars = pltpu.make_async_copy(code_rows, codes, sems.at[2])
     to_scalars.start()
     to_scalars.wait()
     my_row, my_col = spot[0], spot[1]
@@ -101,24 +74,24 @@
             code = codes[n, j]
             row = code // panels
             k = (source * panels + code % panels) * per_row + inner
-            start = pl.multiple_of(n * span + j * block, PAD)
+            record = pl.multiple_of(n * span + j * block, PAD)
 
             @pl.when((code >= 0) & (k < early))
             def _():
                 at = counts[row]
-                firsts[row, at] = start
+                firsts[row, at] = record
                 depths[row, at] = k * block
                 counts[row] = at + 1
 
             @pl.when((code >= 0) & (k >= early))
             def _():
                 to = pl.ds(pl.multiple_of(row * block, block), block)
-                late[k - early, to, :] = held[pl.ds(start, block), :]
+                late[k - early, to, :] = held[pl.ds(record, block), :]
 
         return carry
 
     lax.fori_loop(0, count, place, 0)
-    for copy in second + third:
+    for copy in second:
         copy.wait()
 
     def pair(i, n):
@@ -137,7 +110,7 @@
     for i in range(row_blocks):
         rows = pl.ds(i * block, block)
         product = pair(i, 0) + pair(i, 1)
-        acc[rows, :] = 2.0 * product - before[rows, :].astype(jnp.float32)
+        acc[rows, :] = 2.0 * product - previous[rows, :].astype(jnp.float32)
 
     def more(i, carry):
         rows = pl.ds(pl.multiple_of(i * block, block), block)
@@ -198,35 +171,30 @@
         tail = lax.dynamic_index_in_dim(pad, to, 0, keepdims=False)
         return jnp.concatenate([records.reshape(slots * block, block), tail], axis=0)
 
-    mine = [term_current[p] for p in range(panels)]
-    term = {}
     last = grid_rows - 1
+    rows = term_current.shape[1]
+    flat = term_current.reshape(panels * rows, tile_cols)
+    pieces = [(flat, [(0, 0, panels * rows)])]
     if grid_rows == 4 and panels == 2:
-        term[1, 0] = swap(mine[0], "row", 1)
-        term[2, 1] = swap(mine[1], "row", 2)
-        term[1, 1] = swap(mine[1], "row", 1)
-        term[2, 0] = swap(mine[0], "row", 2)
-        term[3, 0] = swap(term[1, 0], "row", 2)
-        term[3, 1] = swap(term[2, 1], "row", 1)
+        size = panels * rows
+        up, down = swap(flat, "row", 1), swap(flat, "row", 2)
+        pieces += [(up, [(0, size, size)]), (down, [(0, 2 * size, size)])]
+        final = [swap(up[:rows], "row", 2), swap(down[rows:], "row", 1)]
     else:
-        for o in range(1, grid_rows):
-            for p in range(panels):
-                term[o, p] = swap(mine[p], "row", o)
+        for o in range(1, last):
+            pieces.append((swap(flat, "row", o), [(0, o * panels * rows, panels * rows)]))
+        final = [swap(flat[p * rows : (p + 1) * rows], "row", last) for p in range(panels)]
 
     own = jnp.concatenate(
         [payload(0)] + [swap(payload(o), "row", o) for o in range(1, grid_rows)], axis=0
     )
     if grid_cols == 8:
         far, near = swap(own, "col", 6), swap(own, "col", 2)
-        if grid_rows == 4:
-            far = hold(far, [swap(mark([term[1, 0], term[2, 1]]), "col", 1)])
         middle = swap(far, "col", 2)
-        if grid_rows == 4:
-            token = swap(mark([term[1, 1], term[2, 0]]), "col", 1)
-            middle = hold(middle, [swap(token, "col", 1)])
         offsets = [0, 2, 6, 4]
         parts = [own, near, far, middle]
         groups = [jnp.concatenate(parts[:3], axis=0), middle]
+        parts = groups
         others = [swap(group, "col", 1) for group in groups]
     else:
         offsets = list(range(0, grid_cols, 2))
@@ -240,31 +208,27 @@
     anywhere = pl.BlockSpec(memory_space=pl.ANY)
     smem = pl.BlockSpec(memory_space=pltpu.SMEM)
     vmem = pl.BlockSpec(memory_space=pltpu.VMEM)
-    early_terms = [term_current.reshape(-1, tile_cols)] + [
-        term[o, p] for o in range(1, last) for p in range(panels)
-    ]
     late_blocks = panels * per_row
     count = grid_cols * grid_rows
     early_bytes = 2 * (early * block * tile_cols + count * span * block + tile_rows * tile_cols)
     passed_bytes = 4 * tile_rows * tile_cols + 2 * late_blocks * tile_rows * block
     acc, late = pl.pallas_call(
-        functools.partial(early_kernel, dims, len(record_arrays), early),
+        functools.partial(early_kernel, dims, len(record_arrays), early, [p[1] for p in pieces]),
         out_shape=[
             jax.ShapeDtypeStruct((tile_rows, tile_cols), jnp.float32),
             jax.ShapeDtypeStruct((late_blocks, tile_rows, block), jnp.bfloat16),
         ],
-        in_specs=[smem, smem] + [anywhere] * (len(record_arrays) + len(early_terms) + 1),
+        in_specs=[smem, smem] + [anywhere] * (len(record_arrays) + len(pieces)) + [vmem],
         out_specs=[vmem, vmem],
         scratch_shapes=[
             pltpu.VMEM((early * block, tile_cols), jnp.bfloat16),
             pltpu.VMEM((count * span + block, block), jnp.bfloat16),
-            pltpu.VMEM((tile_rows, tile_cols), jnp.bfloat16),
             pltpu.VMEM((count, block), jnp.int32),
             pltpu.SMEM((count, block), jnp.int32),
             pltpu.SMEM((row_blocks,), jnp.int32),
             pltpu.SMEM((row_blocks, early), jnp.int32),
             pltpu.SMEM((row_blocks, early), jnp.int32),
-            pltpu.SemaphoreType.DMA((4,)),
+            pltpu.SemaphoreType.DMA((3,)),
         ],
         compiler_params=pltpu.CompilerParams(vmem_limit_bytes=early_bytes + passed_bytes + SLACK),
         name="early_product",
@@ -272,13 +236,13 @@
         jnp.stack([my_row, my_col]).astype(jnp.int32),
         jnp.array(offsets, jnp.int32),
         *record_arrays,
-        *early_terms,
+        *[p[0] for p in pieces],
         term_previous,
     )
     return pl.pallas_call(
         functools.partial(late_kernel, dims),
         out_shape=jax.ShapeDtypeStruct((tile_rows, tile_cols), term_previous.dtype),
-        in_specs=[smem, vmem, vmem] + [vmem] * panels,
+        in_specs=[smem, vmem, vmem] + [vmem] * len(final),
         out_specs=anywhere,
         scratch_shapes=[
             pltpu.VMEM((tile_rows, tile_cols), term_previous.dtype),
@@ -286,7 +250,7 @@
         ],
         compiler_params=pltpu.CompilerParams(vmem_limit_bytes=passed_bytes + 2 * tile_rows * tile_cols + SLACK),
         name="late_product",
-    )(keep_mask, acc, late, *[term[last, p] for p in range(panels)])
+    )(keep_mask, acc, late, *final)
 
 
 def solution(mesh):

time: 66.5 us -> 57.3 us (0.86)
  waiting for transfers between devices: 26.3 us -> 20.7 us
  starting transfers between devices: 15 us -> 13.2 us
  local copies, waits for them, and re-layouts: 11.3 us -> 9.74 us
    ppermute x17 -> x12, waiting for transfers between devices: 26.3 us -> 20.7 us  [swap(): return lax.ppermute(x, axis, [(i, i ^ offset) for i in range(size)])]
    unnamed x23 -> x14, local copies, waits for them, and re-layouts: 8.15 us -> 5.52 us
    ppermute x17 -> x12, starting transfers between devices: 15 us -> 13.2 us  [swap(): return lax.ppermute(x, axis, [(i, i ^ offset) for i in range(size)])]
    slice x0 -> x2, local copies, waits for them, and re-layouts: none -> 1.69 us  [per_device(): final = [swap(up[:rows], 'row', 2), swap(down[rows:], 'row', 1)]]
    squeeze x1 -> x0, local copies, waits for them, and re-layouts: 1.27 us -> none  [per_device(): mine = [term_current[p] for p in range(panels)]]
  transfers between devices with their start and end apart: 17 -> 12, of which waited for: 8 -> 6; matrix products, arithmetic and copies ran while one was open for 9% -> 10% of each run, Pallas kernels for 12% -> 14%
where the time goes in v3:
time: 57.3 us; the launch traced here: 57.1 us
  waiting for transfers between devices  20.7 us (36%)
  starting transfers between devices  13.2 us (23%)
  Pallas kernels  12.6 us (22%)
  local copies, waits for them, and re-layouts  9.74 us (17%)
  other arithmetic  0.88 us (2%)
    ppermute x12, waiting for transfers between devices, swap(): return lax.ppermute(x, axis, [(i, i ^ offset) for i in range(size)])  20.7 us
    ppermute x12, starting transfers between devices, swap(): return lax.ppermute(x, axis, [(i, i ^ offset) for i in range(size)])  13.2 us
    pallas_call x1, Pallas kernels, per_device(): pl.pallas_call(functools.partial(early_kernel, dims, len(record_arrays),...  8.03 us
    unnamed x14, local copies, waits for them, and re-layouts  5.52 us
    pallas_call x1, Pallas kernels, per_device(): pl.pallas_call(functools.partial(late_kernel, dims), out_shape=jax.ShapeD...  4.59 us
    slice x2, local copies, waits for them, and re-layouts, per_device(): final = [swap(up[:rows], 'row', 2), swap(down[rows:], 'row', 1)]  1.69 us
  transfers between devices with their start and end apart: 12, of which 6 were waited for; matrix products, arithmetic and copies ran while one was open for 10% of the time, Pallas kernels for 14%

profile of v3, /device:TPU:0, one launch (start us, length us, event | category | flops | bytes accessed | tf_op | source)
XLA Modules:
  0.0 57.1 jit_solution(8029874110617033253)
XLA Ops:
  0.0 0.8 %fusion.4 = bf16[4,2]{0,1:T(2,128)(2,1)S(1)} fusion(s32[4,2]{0,1:T(2,128)} %param.9, s32[4]{0:T(128)} %bitcast.15), kind=kLoop, calls=%fused_computation.28 | loop fusion | flops 24 | bytes 64 | tf_op jit(solution)/shard_map/convert_element_type | solution.py:163
  0.8 1.0 %constant_dynamic-slice_fusion = (bf16[1,2,128,128]{3,2,1,0:T(8,128)(2,1)S(1)}, bf16[1,2,128,128]{3,2,1,0:T(8,128)(2,1)S(1)}, bf16[1,2,128,128]{3,2,1,0:T(8,128)(2,1)S(1)}, bf16[1,2,128,128]{3,2,1,0:T(8,128)(2,1)S(1)}) fusion(bf16[4,2,128,128]{3,2,1,0:T(8,128)(2,1)} %param.7, s32[]{:T(128)S(6)} %select_n.26, s32[]{:T(128)S(6)} %select_n.24, ...), kind=kLoop, calls=%fused_computation.23 | loop fusion | bytes 524304 | tf_op jit(solution)/shard_map/jit(dynamic_index_in_dim)/dynamic_slice | solution.py:170
  1.8 0.2 fusion.3
  2.0 3.0 %collective-permute-start = (bf16[272,128]{1,0:T(8,128)(2,1)S(1)}, bf16[272,128]{1,0:T(8,128)(2,1)S(1)}, u32[]{:S(2)}, u32[]{:S(2)}) collective-permute-start(bf16[272,128]{1,0:T(8,128)(2,1)S(1)} %pad_maximum_fusion), channel_id=1, source_target_pairs={{0,8},{8,0},{16,24},{24,16},{1,9},{9,1},{17,25},{25,17},{2,10},{10... | collective-permute-start | bytes 208904 | tf_op jit(solution)/shard_map/ppermute | solution.py:17
  5.0 1.6 %collective-permute-start.1 = (bf16[272,128]{1,0:T(8,128)(2,1)S(1)}, bf16[272,128]{1,0:T(8,128)(2,1)S(1)}, u32[]{:S(2)}, u32[]{:S(2)}) collective-permute-start(bf16[272,128]{1,0:T(8,128)(2,1)S(1)} %pad_maximum_fusion.1), channel_id=1, source_target_pairs={{0,16},{8,24},{16,0},{24,8},{1,17},{9,25},{17,1},{25,9},{2,18},{10... | collective-permute-start | bytes 208904 | tf_op jit(solution)/shard_map/ppermute | solution.py:17
  6.7 0.6 %constant_dynamic-update-slice_fusion.4 = (bf16[1088,128]{1,0:T(8,128)(2,1)S(1)}, bf16[3264,128]{1,0:T(8,128)(2,1)}) fusion(bf16[256,128]{1,0:T(8,128)(2,1)S(1)} %bitcast.11), kind=kLoop, calls=%fused_computation.15 | loop fusion | bytes 196608
  7.3 0.6 %constant_dynamic-update-slice_fusion.3 = (bf16[1088,128]{1,0:T(8,128)(2,1)S(1)}, bf16[3264,128]{1,0:T(8,128)(2,1)}) fusion(bf16[1088,128]{1,0:T(8,128)(2,1)S(1)} %get-tuple-element.23, bf16[128]{0:T(256)(128)(2,1)S(1)} %get-tuple-element.12, bf16[3264,128]{1,0:T(8,128)(2,1)} %get-tuple-element.24), kind=kLoop, calls=%fused_computation.14 | loop fusion | bytes 8704
  7.9 0.6 %constant_dynamic-update-slice_fusion.2 = (bf16[1088,128]{1,0:T(8,128)(2,1)S(1)}, bf16[3264,128]{1,0:T(8,128)(2,1)}) fusion(bf16[1088,128]{1,0:T(8,128)(2,1)S(1)} %get-tuple-element.25, bf16[272,128]{1,0:T(8,128)(2,1)S(1)} %collective-permute-done, bf16[3264,128]{1,0:T(8,128)(2,1)} %get-tuple-element.26), kind=kLoop, calls=%fused_computation.13 | loop fusion | bytes 208896
  8.6 0.8 %collective-permute-done.1 = bf16[272,128]{1,0:T(8,128)(2,1)S(1)} collective-permute-done((bf16[272,128]{1,0:T(8,128)(2,1)S(1)}, bf16[272,128]{1,0:T(8,128)(2,1)S(1)}, u32[]{:S(2)}, u32[]{:S(2)}) %collective-permute-start.1) | collective-permute-done | bytes 69664 | tf_op jit(solution)/shard_map/ppermute | solution.py:17
  9.4 0.6 %constant_dynamic-update-slice_fusion.1 = (bf16[1088,128]{1,0:T(8,128)(2,1)S(1)}, bf16[3264,128]{1,0:T(8,128)(2,1)}) fusion(bf16[1088,128]{1,0:T(8,128)(2,1)S(1)} %get-tuple-element.21, bf16[272,128]{1,0:T(8,128)(2,1)S(1)} %collective-permute-done.1, bf16[3264,128]{1,0:T(8,128)(2,1)} %get-tuple-element.22), kind=kLoop, calls=%fused_computation.12 | loop fusion | bytes 208896
  10.0 1.9 %collective-permute-done.2 = bf16[272,128]{1,0:T(8,128)(2,1)S(1)} collective-permute-done((bf16[272,128]{1,0:T(8,128)(2,1)S(1)}, bf16[272,128]{1,0:T(8,128)(2,1)S(1)}, u32[]{:S(2)}, u32[]{:S(2)}) %collective-permute-start.2) | collective-permute-done | bytes 69664 | tf_op jit(solution)/shard_map/ppermute | solution.py:17
  11.9 0.6 %constant_dynamic-update-slice_fusion = (bf16[1088,128]{1,0:T(8,128)(2,1)S(1)}, bf16[3264,128]{1,0:T(8,128)(2,1)}) fusion(bf16[1088,128]{1,0:T(8,128)(2,1)S(1)} %get-tuple-element.19, bf16[272,128]{1,0:T(8,128)(2,1)S(1)} %collective-permute-done.2, bf16[3264,128]{1,0:T(8,128)(2,1)} %get-tuple-element.20), kind=kLoop, calls=%fused_computation.11 | loop fusion | bytes 208896 | tf_op jit(solution)/shard_map/concatenate | solution.py:188
  12.5 1.6 %collective-permute-start.3 = (bf16[1088,128]{1,0:T(8,128)(2,1)S(1)}, bf16[1088,128]{1,0:T(8,128)(2,1)S(1)}, u32[]{:S(2)}, u32[]{:S(2)}) collective-permute-start(bf16[1088,128]{1,0:T(8,128)(2,1)S(1)} %get-tuple-element.17), channel_id=1, source_target_pairs={{0,2},{1,3},{2,0},{3,1},{4,6},{5,7},{6,4},{7,5},{8,10},{9,11},{10,... | collective-permute-start | bytes 835592 | tf_op jit(solution)/shard_map/ppermute | solution.py:17
  14.1 0.5 collective-permute-start.8
  14.6 0.5 collective-permute-start.9
  15.1 2.5 %collective-permute-start.4 = (bf16[1088,128]{1,0:T(8,128)(2,1)S(1)}, bf16[1088,128]{1,0:T(8,128)(2,1)S(1)}, u32[]{:S(2)}, u32[]{:S(2)}) collective-permute-start(bf16[1088,128]{1,0:T(8,128)(2,1)S(1)} %get-tuple-element.17), channel_id=1, source_target_pairs={{0,6},{1,7},{2,4},{3,5},{4,2},{5,3},{6,0},{7,1},{8,14},{9,15},{10,... | collective-permute-start | bytes 835592 | tf_op jit(solution)/shard_map/ppermute | solution.py:17
  17.6 3.3 %collective-permute-done.3 = bf16[1088,128]{1,0:T(8,128)(2,1)S(1)} collective-permute-done((bf16[1088,128]{1,0:T(8,128)(2,1)S(1)}, bf16[1088,128]{1,0:T(8,128)(2,1)S(1)}, u32[]{:S(2)}, u32[]{:S(2)}) %collective-permute-start.3) | collective-permute-done | bytes 278560 | tf_op jit(solution)/shard_map/ppermute | solution.py:17
  20.9 0.7 %constant_dynamic-update-slice_fusion.6 = bf16[3264,128]{1,0:T(8,128)(2,1)} fusion(bf16[3264,128]{1,0:T(8,128)(2,1)} %get-tuple-element.18, bf16[1088,128]{1,0:T(8,128)(2,1)S(1)} %collective-permute-done.3), kind=kLoop, calls=%fused_computation.17 | loop fusion | bytes 557056
  21.7 5.6 %collective-permute-done.4 = bf16[1088,128]{1,0:T(8,128)(2,1)S(1)} collective-permute-done((bf16[1088,128]{1,0:T(8,128)(2,1)S(1)}, bf16[1088,128]{1,0:T(8,128)(2,1)S(1)}, u32[]{:S(2)}, u32[]{:S(2)}) %collective-permute-start.4) | collective-permute-done | bytes 278560 | tf_op jit(solution)/shard_map/ppermute | solution.py:17
  27.3 0.7 %constant_dynamic-update-slice_fusion.5.refs_0_ = bf16[3264,128]{1,0:T(8,128)(2,1)} fusion(bf16[3264,128]{1,0:T(8,128)(2,1)} %constant_dynamic-update-slice_fusion.6, bf16[1088,128]{1,0:T(8,128)(2,1)S(1)} %collective-permute-done.4), kind=kLoop, calls=%fused_computation.16 | loop fusion | bytes 557056 | tf_op jit(solution)/shard_map/concatenate | solution.py:196
  28.0 1.7 %collective-permute-start.5 = (bf16[1088,128]{1,0:T(8,128)(2,1)S(1)}, bf16[1088,128]{1,0:T(8,128)(2,1)S(1)}, u32[]{:S(2)}, u32[]{:S(2)}) collective-permute-start(bf16[1088,128]{1,0:T(8,128)(2,1)S(1)} %collective-permute-done.4), channel_id=1, source_target_pairs={{0,2},{1,3},{2,0},{3,1},{4,6},{5,7},{6,4},{7,5},{8,10},{9,11},{10,... | collective-permute-start | bytes 835592 | tf_op jit(solution)/shard_map/ppermute | solution.py:17
  29.7 7.5 %collective-permute-done.8.refs_5_ = bf16[512,1024]{1,0:T(8,128)(2,1)S(1)} collective-permute-done((bf16[512,1024]{1,0:T(8,128)(2,1)}, bf16[512,1024]{1,0:T(8,128)(2,1)S(1)}, u32[]{:S(2)}, u32[]{:S(2)}) %collective-permute-start.8) | collective-permute-done | bytes 1048608 | tf_op jit(solution)/shard_map/ppermute | solution.py:17
  37.2 0.8 %slice.8 = bf16[256,1024]{1,0:T(8,128)(2,1)} slice(bf16[512,1024]{1,0:T(8,128)(2,1)S(1)} %collective-permute-done.8.refs_5_), slice={[0:256], [0:1024]} | slice | bytes 1048576 | tf_op jit(solution)/shard_map/slice | solution.py:182
  38.1 0.6 collective-permute-start.10
  38.6 0.8 %slice.9 = bf16[256,1024]{1,0:T(8,128)(2,1)} slice(bf16[512,1024]{1,0:T(8,128)(2,1)S(1)} %collective-permute-done.9.refs_6_), slice={[256:512], [0:1024]} | slice | bytes 1048576 | tf_op jit(solution)/shard_map/slice | solution.py:182
  39.5 1.1 %collective-permute-start.11 = (bf16[256,1024]{1,0:T(8,128)(2,1)}, bf16[256,1024]{1,0:T(8,128)(2,1)}, u32[]{:S(2)}, u32[]{:S(2)}) collective-permute-start(bf16[256,1024]{1,0:T(8,128)(2,1)} %slice.9), channel_id=1, source_target_pairs={{0,8},{8,0},{16,24},{24,16},{1,9},{9,1},{17,25},{25,17},{2,10},{10... | collective-permute-start | bytes 1572872 | tf_op jit(solution)/shard_map/ppermute | solution.py:17
  40.6 0.1 copy.9.keep
  40.7 0.1 pad_add_fusion.spot
  40.8 1.5 %collective-permute-done.7.refs_3_ = bf16[1088,128]{1,0:T(8,128)(2,1)} collective-permute-done((bf16[1088,128]{1,0:T(8,128)(2,1)S(1)}, bf16[1088,128]{1,0:T(8,128)(2,1)}, u32[]{:S(2)}, u32[]{:S(2)}) %collective-permute-start.7) | collective-permute-done | bytes 278560 | tf_op jit(solution)/shard_map/ppermute | solution.py:17
  42.3 2.2 %copy-done = bf16[2048,1024]{1,0:T(8,128)(2,1)S(1)} copy-done((bf16[2048,1024]{1,0:T(8,128)(2,1)S(1)}, bf16[2048,1024]{1,0:T(8,128)(2,1)}, u32[]{:S(2)}) %copy-start) | copy-done | bytes 4194328
  44.5 8.0 %early_product.1 = (f32[2048,1024]{1,0:T(8,128)S(1)}, bf16[4,2048,128]{2,1,0:T(8,128)(2,1)S(1)}) custom-call(s32[2]{0:T(128)S(1)} %pad_add_fusion.spot, s32[8]{0:T(128)S(1)} %copy-done.2, bf16[3264,128]{1,0:T(8,128)(2,1)} %constant_dynamic-update-slice_fusion.5.refs_0_, bf16[1088,128]{1,0:T(8,128)(2,1)S(1)} %collective-permute-done.5.refs_1_, ...), custom_call_target="tpu_custom_call" | custom-call | tf_op jit(solution)/shard_map/early_product/pallas_call | solution.py:215
  52.6 4.6 %late_product.1 = bf16[2048,1024]{1,0:T(8,128)(2,1)} custom-call(s32[16,8]{1,0:T(8,128)S(1)} %copy.9.keep, f32[2048,1024]{1,0:T(8,128)S(1)} %get-tuple-element.7.acc, bf16[4,2048,128]{2,1,0:T(8,128)(2,1)S(1)} %get-tuple-element.8.late, bf16[256,1024]{1,0:T(8,128)(2,1)} %collective-permute-done.10.refs_0_, bf16[256,1024]{1,0:T(8,128)(2,1)} %collective-permute-done.11.refs_1_), custom_call_target="tpu_custom_call" | custom-call | tf_op jit(solution)/shard_map/late_product/pallas_call | solution.py:242
  (22 shorter events, 0.1 us)
Async XLA Ops:
  0.0 42.3 %copy-start.2 = (s32[8]{0:T(128)S(1)}, s32[8]{0:T(128)}, u32[]{:S(2)}) copy-start(s32[8]{0:T(128)} %constant.44.clone.offsets) | copy-start | bytes 100
  0.0 42.3 %copy-start.1 = (bf16[2,256,1024]{2,1,0:T(8,128)(2,1)S(1)}, bf16[2,256,1024]{2,1,0:T(8,128)(2,1)}, u32[]{:S(2)}) copy-start(bf16[2,256,1024]{2,1,0:T(8,128)(2,1)} %param.10) | copy-start | bytes 3145732
  0.0 40.6 %copy-start.3 = (s32[16,8]{0,1:T(8,128)S(1)}, s32[16,8]{0,1:T(8,128)}, u32[]{:S(2)}) copy-start(s32[16,8]{0,1:T(8,128)} %param.12) | copy-start | bytes 1540
  2.0 5.9 %collective-permute-start = (bf16[272,128]{1,0:T(8,128)(2,1)S(1)}, bf16[272,128]{1,0:T(8,128)(2,1)S(1)}, u32[]{:S(2)}, u32[]{:S(2)}) collective-permute-start(bf16[272,128]{1,0:T(8,128)(2,1)S(1)} %pad_maximum_fusion), channel_id=1, source_target_pairs={{0,8},{8,0},{16,24},{24,16},{1,9},{9,1},{17,25},{25,17},{2,10},{10... | collective-permute-start | bytes 208904 | tf_op jit(solution)/shard_map/ppermute | solution.py:17
  5.0 4.4 %collective-permute-start.1 = (bf16[272,128]{1,0:T(8,128)(2,1)S(1)}, bf16[272,128]{1,0:T(8,128)(2,1)S(1)}, u32[]{:S(2)}, u32[]{:S(2)}) collective-permute-start(bf16[272,128]{1,0:T(8,128)(2,1)S(1)} %pad_maximum_fusion.1), channel_id=1, source_target_pairs={{0,16},{8,24},{16,0},{24,8},{1,17},{9,25},{17,1},{25,9},{2,18},{10... | collective-permute-start | bytes 208904 | tf_op jit(solution)/shard_map/ppermute | solution.py:17
  6.6 5.3 %collective-permute-start.2 = (bf16[272,128]{1,0:T(8,128)(2,1)S(1)}, bf16[272,128]{1,0:T(8,128)(2,1)S(1)}, u32[]{:S(2)}, u32[]{:S(2)}) collective-permute-start(bf16[272,128]{1,0:T(8,128)(2,1)S(1)} %pad_maximum_fusion.2), channel_id=1, source_target_pairs={{0,24},{8,16},{16,8},{24,0},{1,25},{9,17},{17,9},{25,1},{2,26},{10... | collective-permute-start | bytes 208904 | tf_op jit(solution)/shard_map/ppermute | solution.py:17
  12.5 8.4 %collective-permute-start.3 = (bf16[1088,128]{1,0:T(8,128)(2,1)S(1)}, bf16[1088,128]{1,0:T(8,128)(2,1)S(1)}, u32[]{:S(2)}, u32[]{:S(2)}) collective-permute-start(bf16[1088,128]{1,0:T(8,128)(2,1)S(1)} %get-tuple-element.17), channel_id=1, source_target_pairs={{0,2},{1,3},{2,0},{3,1},{4,6},{5,7},{6,4},{7,5},{8,10},{9,11},{10,... | collective-permute-start | bytes 835592 | tf_op jit(solution)/shard_map/ppermute | solution.py:17
  14.1 23.1 %collective-permute-start.8 = (bf16[512,1024]{1,0:T(8,128)(2,1)}, bf16[512,1024]{1,0:T(8,128)(2,1)S(1)}, u32[]{:S(2)}, u32[]{:S(2)}) collective-permute-start(bf16[512,1024]{1,0:T(8,128)(2,1)} %bitcast.8), channel_id=1, source_target_pairs={{0,8},{8,0},{16,24},{24,16},{1,9},{9,1},{17,25},{25,17},{2,10},{10... | collective-permute-start | bytes 3145736 | tf_op jit(solution)/shard_map/ppermute | solution.py:17
  14.6 24.0 %collective-permute-start.9 = (bf16[512,1024]{1,0:T(8,128)(2,1)}, bf16[512,1024]{1,0:T(8,128)(2,1)S(1)}, u32[]{:S(2)}, u32[]{:S(2)}) collective-permute-start(bf16[512,1024]{1,0:T(8,128)(2,1)} %bitcast.9), channel_id=1, source_target_pairs={{0,16},{8,24},{16,0},{24,8},{1,17},{9,25},{17,1},{25,9},{2,18},{10... | collective-permute-start | bytes 3145736 | tf_op jit(solution)/shard_map/ppermute | solution.py:17
  15.1 12.2 %collective-permute-start.4 = (bf16[1088,128]{1,0:T(8,128)(2,1)S(1)}, bf16[1088,128]{1,0:T(8,128)(2,1)S(1)}, u32[]{:S(2)}, u32[]{:S(2)}) collective-permute-start(bf16[1088,128]{1,0:T(8,128)(2,1)S(1)} %get-tuple-element.17), channel_id=1, source_target_pairs={{0,6},{1,7},{2,4},{3,5},{4,2},{5,3},{6,0},{7,1},{8,14},{9,15},{10,... | collective-permute-start | bytes 835592 | tf_op jit(solution)/shard_map/ppermute | solution.py:17
  28.0 14.3 %collective-permute-start.6 = (bf16[3264,128]{1,0:T(8,128)(2,1)}, bf16[3264,128]{1,0:T(8,128)(2,1)}, u32[]{:S(2)}, u32[]{:S(2)}) collective-permute-start(bf16[3264,128]{1,0:T(8,128)(2,1)} %constant_dynamic-update-slice_fusion.5.refs_0_), channel_id=1, source_target_pairs={{0,1},{1,0},{2,3},{3,2},{4,5},{5,4},{6,7},{7,6},{8,9},{9,8},{10,11... | collective-permute-start | bytes 2506760 | tf_op jit(solution)/shard_map/ppermute | solution.py:17
  28.0 12.6 %collective-permute-start.5 = (bf16[1088,128]{1,0:T(8,128)(2,1)S(1)}, bf16[1088,128]{1,0:T(8,128)(2,1)S(1)}, u32[]{:S(2)}, u32[]{:S(2)}) collective-permute-start(bf16[1088,128]{1,0:T(8,128)(2,1)S(1)} %collective-permute-done.4), channel_id=1, source_target_pairs={{0,2},{1,3},{2,0},{3,1},{4,6},{5,7},{6,4},{7,5},{8,10},{9,11},{10,... | collective-permute-start | bytes 835592 | tf_op jit(solution)/shard_map/ppermute | solution.py:17
  38.1 14.5 %collective-permute-start.10 = (bf16[256,1024]{1,0:T(8,128)(2,1)}, bf16[256,1024]{1,0:T(8,128)(2,1)}, u32[]{:S(2)}, u32[]{:S(2)}) collective-permute-start(bf16[256,1024]{1,0:T(8,128)(2,1)} %slice.8), channel_id=1, source_target_pairs={{0,16},{8,24},{16,0},{24,8},{1,17},{9,25},{17,1},{25,9},{2,18},{10... | collective-permute-start | bytes 1572872 | tf_op jit(solution)/shard_map/ppermute | solution.py:17
  39.5 13.1 %collective-permute-start.11 = (bf16[256,1024]{1,0:T(8,128)(2,1)}, bf16[256,1024]{1,0:T(8,128)(2,1)}, u32[]{:S(2)}, u32[]{:S(2)}) collective-permute-start(bf16[256,1024]{1,0:T(8,128)(2,1)} %slice.9), channel_id=1, source_target_pairs={{0,8},{8,0},{16,24},{24,16},{1,9},{9,1},{17,25},{25,17},{2,10},{10... | collective-permute-start | bytes 1572872 | tf_op jit(solution)/shard_map/ppermute | solution.py:17
  40.6 1.7 %collective-permute-start.7 = (bf16[1088,128]{1,0:T(8,128)(2,1)S(1)}, bf16[1088,128]{1,0:T(8,128)(2,1)}, u32[]{:S(2)}, u32[]{:S(2)}) collective-permute-start(bf16[1088,128]{1,0:T(8,128)(2,1)S(1)} %collective-permute-done.5.refs_1_), channel_id=1, source_target_pairs={{0,1},{1,0},{2,3},{3,2},{4,5},{5,4},{6,7},{7,6},{8,9},{9,8},{10,11... | collective-permute-start | bytes 835592 | tf_op jit(solution)/shard_map/ppermute | solution.py:17
  42.3 2.2 %copy-start = (bf16[2048,1024]{1,0:T(8,128)(2,1)S(1)}, bf16[2048,1024]{1,0:T(8,128)(2,1)}, u32[]{:S(2)}) copy-start(bf16[2048,1024]{1,0:T(8,128)(2,1)} %refs_7_.1) | copy-start | bytes 12582916

commit v4 on v3

--- a/solution.py
+++ b/solution.py
@@ -22,8 +22,8 @@
     span = slots * block + PAD
     per_row = grid_cols // grid_rows
     record_refs = refs[:arrays]
-    term_refs = refs[arrays:-11]
-    previous, acc, late, terms, held, code_rows, codes, counts, firsts, depths, sems = refs[-11:]
+    term_refs = refs[arrays:-10]
+    acc, late, terms, held, code_rows, codes, counts, firsts, depths, sems = refs[-10:]
     row_blocks = acc.shape[0] // block
     count = grid_rows * grid_cols
     nothing = count * span
@@ -55,7 +55,7 @@
             depths[i, n] = 0
         return carry
 
-    lax.fori_loop(0, row_blocks, clear, 0)
+    lax.fori_loop(0, row_blocks + 1, clear, 0)
     for copy in first:
         copy.wait()
     for n in range(count):
@@ -76,12 +76,11 @@
             k = (source * panels + code % panels) * per_row + inner
             record = pl.multiple_of(n * span + j * block, PAD)
 
-            @pl.when((code >= 0) & (k < early))
-            def _():
-                at = counts[row]
-                firsts[row, at] = record
-                depths[row, at] = k * block
-                counts[row] = at + 1
+            to = jnp.where((code >= 0) & (k < early), row, row_blocks)
+            at = counts[to]
+            firsts[to, jnp.minimum(at, early - 1)] = record
+            depths[to, jnp.minimum(at, early - 1)] = k * block
+            counts[to] = at + 1
 
             @pl.when((code >= 0) & (k >= early))
             def _():
@@ -110,7 +109,7 @@
     for i in range(row_blocks):
         rows = pl.ds(i * block, block)
         product = pair(i, 0) + pair(i, 1)
-        acc[rows, :] = 2.0 * product - previous[rows, :].astype(jnp.float32)
+        acc[rows, :] = 2.0 * product
 
     def more(i, carry):
         rows = pl.ds(pl.multiple_of(i * block, block), block)
@@ -124,17 +123,18 @@
     lax.fori_loop(0, row_blocks, more, 0)
 
 
-def late_kernel(dims, keep, acc, late, *refs):
+def late_kernel(dims, keep, acc, late, previous, *refs):
     block = dims[-1]
-    term_refs, out, staged, sem = refs[:-3], refs[-3], refs[-2], refs[-1]
+    term_refs, out, staged, sem = refs[:-3], *refs[-3:]
     blocks = late.shape[0]
+    steps = acc.shape[0] // TILE
     right = jnp.concatenate([ref[...] for ref in term_refs], axis=0)
     copies = []
-    for t in range(acc.shape[0] // TILE):
+    for t in range(steps):
         rows = pl.ds(t * TILE, TILE)
         left = jnp.concatenate([late[k, rows, :] for k in range(blocks)], axis=1)
         product = jnp.dot(left, right, preferred_element_type=jnp.float32)
-        update = acc[rows, :] + 2.0 * product
+        update = acc[rows, :] + 2.0 * product - previous[rows, :].astype(jnp.float32)
         for i in range(TILE // block):
             for j in range(out.shape[1] // block):
                 wanted = keep[t * (TILE // block) + i, j] > 0
@@ -170,6 +170,8 @@
         records = lax.dynamic_index_in_dim(send_blocks, to, 0, keepdims=False)
         tail = lax.dynamic_index_in_dim(pad, to, 0, keepdims=False)
         return jnp.concatenate([records.reshape(slots * block, block), tail], axis=0)
+
+    got = [swap(payload(o), "row", o) for o in range(1, grid_rows)]
 
     last = grid_rows - 1
     rows = term_current.shape[1]
@@ -185,9 +187,7 @@
             pieces.append((swap(flat, "row", o), [(0, o * panels * rows, panels * rows)]))
         final = [swap(flat[p * rows : (p + 1) * rows], "row", last) for p in range(panels)]
 
-    own = jnp.concatenate(
-        [payload(0)] + [swap(payload(o), "row", o) for o in range(1, grid_rows)], axis=0
-    )
+    own = jnp.concatenate([payload(0)] + got, axis=0)
     if grid_cols == 8:
         far, near = swap(own, "col", 6), swap(own, "col", 2)
         middle = swap(far, "col", 2)
@@ -210,7 +210,7 @@
     vmem = pl.BlockSpec(memory_space=pltpu.VMEM)
     late_blocks = panels * per_row
     count = grid_cols * grid_rows
-    early_bytes = 2 * (early * block * tile_cols + count * span * block + tile_rows * tile_cols)
+    early_bytes = 2 * (early * block * tile_cols + count * span * block)
     passed_bytes = 4 * tile_rows * tile_cols + 2 * late_blocks * tile_rows * block
     acc, late = pl.pallas_call(
         functools.partial(early_kernel, dims, len(record_arrays), early, [p[1] for p in pieces]),
@@ -218,16 +218,16 @@
             jax.ShapeDtypeStruct((tile_rows, tile_cols), jnp.float32),
             jax.ShapeDtypeStruct((late_blocks, tile_rows, block), jnp.bfloat16),
         ],
-        in_specs=[smem, smem] + [anywhere] * (len(record_arrays) + len(pieces)) + [vmem],
+        in_specs=[smem, smem] + [anywhere] * (len(record_arrays) + len(pieces)),
         out_specs=[vmem, vmem],
         scratch_shapes=[
             pltpu.VMEM((early * block, tile_cols), jnp.bfloat16),
             pltpu.VMEM((count * span + block, block), jnp.bfloat16),
             pltpu.VMEM((count, block), jnp.int32),
             pltpu.SMEM((count, block), jnp.int32),
-            pltpu.SMEM((row_blocks,), jnp.int32),
-            pltpu.SMEM((row_blocks, early), jnp.int32),
-            pltpu.SMEM((row_blocks, early), jnp.int32),
+            pltpu.SMEM((row_blocks + 1,), jnp.int32),
+            pltpu.SMEM((row_blocks + 1, early), jnp.int32),
+            pltpu.SMEM((row_blocks + 1, early), jnp.int32),
             pltpu.SemaphoreType.DMA((3,)),
         ],
         compiler_params=pltpu.CompilerParams(vmem_limit_bytes=early_bytes + passed_bytes + SLACK),
@@ -237,20 +237,19 @@
         jnp.array(offsets, jnp.int32),
         *record_arrays,
         *[p[0] for p in pieces],
-        term_previous,
     )
     return pl.pallas_call(
         functools.partial(late_kernel, dims),
         out_shape=jax.ShapeDtypeStruct((tile_rows, tile_cols), term_previous.dtype),
-        in_specs=[smem, vmem, vmem] + [vmem] * len(final),
+        in_specs=[smem, vmem, vmem, vmem] + [vmem] * len(final),
         out_specs=anywhere,
         scratch_shapes=[
             pltpu.VMEM((tile_rows, tile_cols), term_previous.dtype),
             pltpu.SemaphoreType.DMA,
         ],
-        compiler_params=pltpu.CompilerParams(vmem_limit_bytes=passed_bytes + 2 * tile_rows * tile_cols + SLACK),
+        compiler_params=pltpu.CompilerParams(vmem_limit_bytes=passed_bytes + 4 * tile_rows * tile_cols + SLACK),
         name="late_product",
-    )(keep_mask, acc, late, *final)
+    )(keep_mask, acc, late, term_previous, *final)
 
 
 def solution(mesh):

time: 57.3 us -> 55.4 us (0.967)
  local copies, waits for them, and re-layouts: 9.74 us -> 7.56 us
    unnamed x14, local copies, waits for them, and re-layouts: 5.52 us -> 3.34 us
  transfers between devices with their start and end apart: 12 -> 12, of which waited for: 6 -> 7; matrix products, arithmetic and copies ran while one was open for 10% -> 11% of each run, Pallas kernels for 14% -> 14%
where the time goes in v4:
time: 55.4 us; the launch traced here: 55.2 us
  waiting for transfers between devices  21.2 us (38%)
  starting transfers between devices  13.2 us (24%)
  Pallas kernels  12.3 us (22%)
  local copies, waits for them, and re-layouts  7.56 us (14%)
  other arithmetic  0.88 us (2%)
    ppermute x12, waiting for transfers between devices, swap(): return lax.ppermute(x, axis, [(i, i ^ offset) for i in range(size)])  21.2 us
    ppermute x12, starting transfers between devices, swap(): return lax.ppermute(x, axis, [(i, i ^ offset) for i in range(size)])  13.2 us
    pallas_call x1, Pallas kernels, per_device(): pl.pallas_call(functools.partial(early_kernel, dims, len(record_arrays),...  7.47 us
    pallas_call x1, Pallas kernels, per_device(): pl.pallas_call(functools.partial(late_kernel, dims), out_shape=jax.ShapeD...  4.86 us
    unnamed x14, local copies, waits for them, and re-layouts  3.34 us
    slice x2, local copies, waits for them, and re-layouts, per_device(): final = [swap(up[:rows], 'row', 2), swap(down[rows:], 'row', 1)]  1.69 us
  transfers between devices with their start and end apart: 12, of which 7 were waited for; matrix products, arithmetic and copies ran while one was open for 11% of the time, Pallas kernels for 14%

profile of v4, /device:TPU:0, one launch (start us, length us, event | category | flops | bytes accessed | tf_op | source)
XLA Modules:
  0.0 55.2 jit_solution(8357289230809934877)
XLA Ops:
  0.0 0.8 %fusion.4 = bf16[4,2]{0,1:T(2,128)(2,1)S(1)} fusion(s32[4,2]{0,1:T(2,128)} %param.9, s32[4]{0:T(128)} %bitcast.15), kind=kLoop, calls=%fused_computation.28 | loop fusion | flops 24 | bytes 64 | tf_op jit(solution)/shard_map/convert_element_type | solution.py:163
  0.8 1.0 %constant_dynamic-slice_fusion = (bf16[1,2,128,128]{3,2,1,0:T(8,128)(2,1)S(1)}, bf16[1,2,128,128]{3,2,1,0:T(8,128)(2,1)S(1)}, bf16[1,2,128,128]{3,2,1,0:T(8,128)(2,1)S(1)}, bf16[1,2,128,128]{3,2,1,0:T(8,128)(2,1)S(1)}) fusion(bf16[4,2,128,128]{3,2,1,0:T(8,128)(2,1)} %param.7, s32[]{:T(128)S(6)} %select_n.26, s32[]{:T(128)S(6)} %select_n.24, ...), kind=kLoop, calls=%fused_computation.23 | loop fusion | bytes 524304 | tf_op jit(solution)/shard_map/jit(dynamic_index_in_dim)/dynamic_slice | solution.py:170
  1.8 0.2 fusion.3
  2.0 3.0 %collective-permute-start = (bf16[272,128]{1,0:T(8,128)(2,1)S(1)}, bf16[272,128]{1,0:T(8,128)(2,1)S(1)}, u32[]{:S(2)}, u32[]{:S(2)}) collective-permute-start(bf16[272,128]{1,0:T(8,128)(2,1)S(1)} %pad_maximum_fusion), channel_id=1, source_target_pairs={{0,8},{8,0},{16,24},{24,16},{1,9},{9,1},{17,25},{25,17},{2,10},{10... | collective-permute-start | bytes 208904 | tf_op jit(solution)/shard_map/ppermute | solution.py:17
  5.0 1.6 %collective-permute-start.1 = (bf16[272,128]{1,0:T(8,128)(2,1)S(1)}, bf16[272,128]{1,0:T(8,128)(2,1)S(1)}, u32[]{:S(2)}, u32[]{:S(2)}) collective-permute-start(bf16[272,128]{1,0:T(8,128)(2,1)S(1)} %pad_maximum_fusion.1), channel_id=1, source_target_pairs={{0,16},{8,24},{16,0},{24,8},{1,17},{9,25},{17,1},{25,9},{2,18},{10... | collective-permute-start | bytes 208904 | tf_op jit(solution)/shard_map/ppermute | solution.py:17
  6.7 0.6 %constant_dynamic-update-slice_fusion.4 = (bf16[1088,128]{1,0:T(8,128)(2,1)S(1)}, bf16[3264,128]{1,0:T(8,128)(2,1)}) fusion(bf16[256,128]{1,0:T(8,128)(2,1)S(1)} %bitcast.11), kind=kLoop, calls=%fused_computation.15 | loop fusion | bytes 196608
  7.3 0.6 %constant_dynamic-update-slice_fusion.3 = (bf16[1088,128]{1,0:T(8,128)(2,1)S(1)}, bf16[3264,128]{1,0:T(8,128)(2,1)}) fusion(bf16[1088,128]{1,0:T(8,128)(2,1)S(1)} %get-tuple-element.23, bf16[128]{0:T(256)(128)(2,1)S(1)} %get-tuple-element.12, bf16[3264,128]{1,0:T(8,128)(2,1)} %get-tuple-element.24), kind=kLoop, calls=%fused_computation.14 | loop fusion | bytes 8704
  7.9 0.6 %constant_dynamic-update-slice_fusion.2 = (bf16[1088,128]{1,0:T(8,128)(2,1)S(1)}, bf16[3264,128]{1,0:T(8,128)(2,1)}) fusion(bf16[1088,128]{1,0:T(8,128)(2,1)S(1)} %get-tuple-element.25, bf16[272,128]{1,0:T(8,128)(2,1)S(1)} %collective-permute-done, bf16[3264,128]{1,0:T(8,128)(2,1)} %get-tuple-element.26), kind=kLoop, calls=%fused_computation.13 | loop fusion | bytes 208896
  8.6 0.8 %collective-permute-done.1 = bf16[272,128]{1,0:T(8,128)(2,1)S(1)} collective-permute-done((bf16[272,128]{1,0:T(8,128)(2,1)S(1)}, bf16[272,128]{1,0:T(8,128)(2,1)S(1)}, u32[]{:S(2)}, u32[]{:S(2)}) %collective-permute-start.1) | collective-permute-done | bytes 69664 | tf_op jit(solution)/shard_map/ppermute | solution.py:17
  9.4 0.6 %constant_dynamic-update-slice_fusion.1 = (bf16[1088,128]{1,0:T(8,128)(2,1)S(1)}, bf16[3264,128]{1,0:T(8,128)(2,1)}) fusion(bf16[1088,128]{1,0:T(8,128)(2,1)S(1)} %get-tuple-element.21, bf16[272,128]{1,0:T(8,128)(2,1)S(1)} %collective-permute-done.1, bf16[3264,128]{1,0:T(8,128)(2,1)} %get-tuple-element.22), kind=kLoop, calls=%fused_computation.12 | loop fusion | bytes 208896
  10.0 1.9 %collective-permute-done.2 = bf16[272,128]{1,0:T(8,128)(2,1)S(1)} collective-permute-done((bf16[272,128]{1,0:T(8,128)(2,1)S(1)}, bf16[272,128]{1,0:T(8,128)(2,1)S(1)}, u32[]{:S(2)}, u32[]{:S(2)}) %collective-permute-start.2) | collective-permute-done | bytes 69664 | tf_op jit(solution)/shard_map/ppermute | solution.py:17
  11.9 0.6 %constant_dynamic-update-slice_fusion = (bf16[1088,128]{1,0:T(8,128)(2,1)S(1)}, bf16[3264,128]{1,0:T(8,128)(2,1)}) fusion(bf16[1088,128]{1,0:T(8,128)(2,1)S(1)} %get-tuple-element.19, bf16[272,128]{1,0:T(8,128)(2,1)S(1)} %collective-permute-done.2, bf16[3264,128]{1,0:T(8,128)(2,1)} %get-tuple-element.20), kind=kLoop, calls=%fused_computation.11 | loop fusion | bytes 208896 | tf_op jit(solution)/shard_map/concatenate | solution.py:190
  12.5 1.6 %collective-permute-start.3 = (bf16[1088,128]{1,0:T(8,128)(2,1)S(1)}, bf16[1088,128]{1,0:T(8,128)(2,1)S(1)}, u32[]{:S(2)}, u32[]{:S(2)}) collective-permute-start(bf16[1088,128]{1,0:T(8,128)(2,1)S(1)} %get-tuple-element.17), channel_id=1, source_target_pairs={{0,2},{1,3},{2,0},{3,1},{4,6},{5,7},{6,4},{7,5},{8,10},{9,11},{10,... | collective-permute-start | bytes 835592 | tf_op jit(solution)/shard_map/ppermute | solution.py:17
  14.1 0.5 collective-permute-start.8
  14.6 0.5 collective-permute-start.9
  15.1 2.5 %collective-permute-start.4 = (bf16[1088,128]{1,0:T(8,128)(2,1)S(1)}, bf16[1088,128]{1,0:T(8,128)(2,1)S(1)}, u32[]{:S(2)}, u32[]{:S(2)}) collective-permute-start(bf16[1088,128]{1,0:T(8,128)(2,1)S(1)} %get-tuple-element.17), channel_id=1, source_target_pairs={{0,6},{1,7},{2,4},{3,5},{4,2},{5,3},{6,0},{7,1},{8,14},{9,15},{10,... | collective-permute-start | bytes 835592 | tf_op jit(solution)/shard_map/ppermute | solution.py:17
  17.6 3.3 %collective-permute-done.3 = bf16[1088,128]{1,0:T(8,128)(2,1)S(1)} collective-permute-done((bf16[1088,128]{1,0:T(8,128)(2,1)S(1)}, bf16[1088,128]{1,0:T(8,128)(2,1)S(1)}, u32[]{:S(2)}, u32[]{:S(2)}) %collective-permute-start.3) | collective-permute-done | bytes 278560 | tf_op jit(solution)/shard_map/ppermute | solution.py:17
  20.9 0.7 %constant_dynamic-update-slice_fusion.6 = bf16[3264,128]{1,0:T(8,128)(2,1)} fusion(bf16[3264,128]{1,0:T(8,128)(2,1)} %get-tuple-element.18, bf16[1088,128]{1,0:T(8,128)(2,1)S(1)} %collective-permute-done.3), kind=kLoop, calls=%fused_computation.17 | loop fusion | bytes 557056
  21.7 5.6 %collective-permute-done.4 = bf16[1088,128]{1,0:T(8,128)(2,1)S(1)} collective-permute-done((bf16[1088,128]{1,0:T(8,128)(2,1)S(1)}, bf16[1088,128]{1,0:T(8,128)(2,1)S(1)}, u32[]{:S(2)}, u32[]{:S(2)}) %collective-permute-start.4) | collective-permute-done | bytes 278560 | tf_op jit(solution)/shard_map/ppermute | solution.py:17
  27.3 0.7 %constant_dynamic-update-slice_fusion.5.refs_0_ = bf16[3264,128]{1,0:T(8,128)(2,1)} fusion(bf16[3264,128]{1,0:T(8,128)(2,1)} %constant_dynamic-update-slice_fusion.6, bf16[1088,128]{1,0:T(8,128)(2,1)S(1)} %collective-permute-done.4), kind=kLoop, calls=%fused_computation.16 | loop fusion | bytes 557056 | tf_op jit(solution)/shard_map/concatenate | solution.py:196
  28.0 1.7 %collective-permute-start.5 = (bf16[1088,128]{1,0:T(8,128)(2,1)S(1)}, bf16[1088,128]{1,0:T(8,128)(2,1)S(1)}, u32[]{:S(2)}, u32[]{:S(2)}) collective-permute-start(bf16[1088,128]{1,0:T(8,128)(2,1)S(1)} %collective-permute-done.4), channel_id=1, source_target_pairs={{0,2},{1,3},{2,0},{3,1},{4,6},{5,7},{6,4},{7,5},{8,10},{9,11},{10,... | collective-permute-start | bytes 835592 | tf_op jit(solution)/shard_map/ppermute | solution.py:17
  29.7 7.5 %collective-permute-done.8.refs_5_ = bf16[512,1024]{1,0:T(8,128)(2,1)S(1)} collective-permute-done((bf16[512,1024]{1,0:T(8,128)(2,1)}, bf16[512,1024]{1,0:T(8,128)(2,1)S(1)}, u32[]{:S(2)}, u32[]{:S(2)}) %collective-permute-start.8) | collective-permute-done | bytes 1048608 | tf_op jit(solution)/shard_map/ppermute | solution.py:17
  37.2 0.8 %slice.8 = bf16[256,1024]{1,0:T(8,128)(2,1)} slice(bf16[512,1024]{1,0:T(8,128)(2,1)S(1)} %collective-permute-done.8.refs_5_), slice={[0:256], [0:1024]} | slice | bytes 1048576 | tf_op jit(solution)/shard_map/slice | solution.py:184
  38.1 0.6 %collective-permute-start.10 = (bf16[256,1024]{1,0:T(8,128)(2,1)}, bf16[256,1024]{1,0:T(8,128)(2,1)}, u32[]{:S(2)}, u32[]{:S(2)}) collective-permute-start(bf16[256,1024]{1,0:T(8,128)(2,1)} %slice.8), channel_id=1, source_target_pairs={{0,16},{8,24},{16,0},{24,8},{1,17},{9,25},{17,1},{25,9},{2,18},{10... | collective-permute-start | bytes 1572872 | tf_op jit(solution)/shard_map/ppermute | solution.py:17
  38.6 0.8 %slice.9 = bf16[256,1024]{1,0:T(8,128)(2,1)} slice(bf16[512,1024]{1,0:T(8,128)(2,1)S(1)} %collective-permute-done.9.refs_6_), slice={[256:512], [0:1024]} | slice | bytes 1048576 | tf_op jit(solution)/shard_map/slice | solution.py:184
  39.5 1.1 %collective-permute-start.11 = (bf16[256,1024]{1,0:T(8,128)(2,1)}, bf16[256,1024]{1,0:T(8,128)(2,1)}, u32[]{:S(2)}, u32[]{:S(2)}) collective-permute-start(bf16[256,1024]{1,0:T(8,128)(2,1)} %slice.9), channel_id=1, source_target_pairs={{0,8},{8,0},{16,24},{24,16},{1,9},{9,1},{17,25},{25,17},{2,10},{10... | collective-permute-start | bytes 1572872 | tf_op jit(solution)/shard_map/ppermute | solution.py:17
  40.6 0.1 copy.9.keep
  40.7 0.1 pad_add_fusion.spot
  40.8 1.5 %collective-permute-done.7.refs_3_ = bf16[1088,128]{1,0:T(8,128)(2,1)} collective-permute-done((bf16[1088,128]{1,0:T(8,128)(2,1)S(1)}, bf16[1088,128]{1,0:T(8,128)(2,1)}, u32[]{:S(2)}, u32[]{:S(2)}) %collective-permute-start.7) | collective-permute-done | bytes 278560 | tf_op jit(solution)/shard_map/ppermute | solution.py:17
  42.3 7.5 %early_product.1 = (f32[2048,1024]{1,0:T(8,128)S(1)}, bf16[4,2048,128]{2,1,0:T(8,128)(2,1)S(1)}) custom-call(s32[2]{0:T(128)S(1)} %pad_add_fusion.spot, s32[8]{0:T(128)S(1)} %copy-done.2, bf16[3264,128]{1,0:T(8,128)(2,1)} %constant_dynamic-update-slice_fusion.5.refs_0_, bf16[1088,128]{1,0:T(8,128)(2,1)S(1)} %collective-permute-done.5.refs_1_, ...), custom_call_target="tpu_custom_call" | custom-call | tf_op jit(solution)/shard_map/early_product/pallas_call | solution.py:215
  49.8 0.5 collective-permute-done.11.refs_1_
  50.3 4.9 %late_product.1 = bf16[2048,1024]{1,0:T(8,128)(2,1)} custom-call(s32[16,8]{1,0:T(8,128)S(1)} %copy.9.keep, f32[2048,1024]{1,0:T(8,128)S(1)} %get-tuple-element.7.acc, bf16[4,2048,128]{2,1,0:T(8,128)(2,1)S(1)} %get-tuple-element.8.late, bf16[2048,1024]{1,0:T(8,128)(2,1)S(1)} %copy-done, bf16[256,1024]{1,0:T(8,128)(2,1)} %collective-permute-done.10.refs_0_, ...), custom_call_target="tpu_custom_call" | custom-call | tf_op jit(solution)/shard_map/late_product/pallas_call | solution.py:241
  (22 shorter events, 0.1 us)
Async XLA Ops:
  0.0 42.3 %copy-start.2 = (s32[8]{0:T(128)S(1)}, s32[8]{0:T(128)}, u32[]{:S(2)}) copy-start(s32[8]{0:T(128)} %constant.44.clone.offsets) | copy-start | bytes 100
  0.0 42.3 %copy-start.1 = (bf16[2,256,1024]{2,1,0:T(8,128)(2,1)S(1)}, bf16[2,256,1024]{2,1,0:T(8,128)(2,1)}, u32[]{:S(2)}) copy-start(bf16[2,256,1024]{2,1,0:T(8,128)(2,1)} %param.10) | copy-start | bytes 3145732
  0.0 40.6 %copy-start.3 = (s32[16,8]{0,1:T(8,128)S(1)}, s32[16,8]{0,1:T(8,128)}, u32[]{:S(2)}) copy-start(s32[16,8]{0,1:T(8,128)} %param.12) | copy-start | bytes 1540
  2.0 5.9 %collective-permute-start = (bf16[272,128]{1,0:T(8,128)(2,1)S(1)}, bf16[272,128]{1,0:T(8,128)(2,1)S(1)}, u32[]{:S(2)}, u32[]{:S(2)}) collective-permute-start(bf16[272,128]{1,0:T(8,128)(2,1)S(1)} %pad_maximum_fusion), channel_id=1, source_target_pairs={{0,8},{8,0},{16,24},{24,16},{1,9},{9,1},{17,25},{25,17},{2,10},{10... | collective-permute-start | bytes 208904 | tf_op jit(solution)/shard_map/ppermute | solution.py:17
  5.0 4.4 %collective-permute-start.1 = (bf16[272,128]{1,0:T(8,128)(2,1)S(1)}, bf16[272,128]{1,0:T(8,128)(2,1)S(1)}, u32[]{:S(2)}, u32[]{:S(2)}) collective-permute-start(bf16[272,128]{1,0:T(8,128)(2,1)S(1)} %pad_maximum_fusion.1), channel_id=1, source_target_pairs={{0,16},{8,24},{16,0},{24,8},{1,17},{9,25},{17,1},{25,9},{2,18},{10... | collective-permute-start | bytes 208904 | tf_op jit(solution)/shard_map/ppermute | solution.py:17
  6.6 5.3 %collective-permute-start.2 = (bf16[272,128]{1,0:T(8,128)(2,1)S(1)}, bf16[272,128]{1,0:T(8,128)(2,1)S(1)}, u32[]{:S(2)}, u32[]{:S(2)}) collective-permute-start(bf16[272,128]{1,0:T(8,128)(2,1)S(1)} %pad_maximum_fusion.2), channel_id=1, source_target_pairs={{0,24},{8,16},{16,8},{24,0},{1,25},{9,17},{17,9},{25,1},{2,26},{10... | collective-permute-start | bytes 208904 | tf_op jit(solution)/shard_map/ppermute | solution.py:17
  12.5 8.4 %collective-permute-start.3 = (bf16[1088,128]{1,0:T(8,128)(2,1)S(1)}, bf16[1088,128]{1,0:T(8,128)(2,1)S(1)}, u32[]{:S(2)}, u32[]{:S(2)}) collective-permute-start(bf16[1088,128]{1,0:T(8,128)(2,1)S(1)} %get-tuple-element.17), channel_id=1, source_target_pairs={{0,2},{1,3},{2,0},{3,1},{4,6},{5,7},{6,4},{7,5},{8,10},{9,11},{10,... | collective-permute-start | bytes 835592 | tf_op jit(solution)/shard_map/ppermute | solution.py:17
  14.1 23.1 %collective-permute-start.8 = (bf16[512,1024]{1,0:T(8,128)(2,1)}, bf16[512,1024]{1,0:T(8,128)(2,1)S(1)}, u32[]{:S(2)}, u32[]{:S(2)}) collective-permute-start(bf16[512,1024]{1,0:T(8,128)(2,1)} %bitcast.8), channel_id=1, source_target_pairs={{0,8},{8,0},{16,24},{24,16},{1,9},{9,1},{17,25},{25,17},{2,10},{10... | collective-permute-start | bytes 3145736 | tf_op jit(solution)/shard_map/ppermute | solution.py:17
  14.6 24.0 %collective-permute-start.9 = (bf16[512,1024]{1,0:T(8,128)(2,1)}, bf16[512,1024]{1,0:T(8,128)(2,1)S(1)}, u32[]{:S(2)}, u32[]{:S(2)}) collective-permute-start(bf16[512,1024]{1,0:T(8,128)(2,1)} %bitcast.9), channel_id=1, source_target_pairs={{0,16},{8,24},{16,0},{24,8},{1,17},{9,25},{17,1},{25,9},{2,18},{10... | collective-permute-start | bytes 3145736 | tf_op jit(solution)/shard_map/ppermute | solution.py:17
  15.1 12.2 %collective-permute-start.4 = (bf16[1088,128]{1,0:T(8,128)(2,1)S(1)}, bf16[1088,128]{1,0:T(8,128)(2,1)S(1)}, u32[]{:S(2)}, u32[]{:S(2)}) collective-permute-start(bf16[1088,128]{1,0:T(8,128)(2,1)S(1)} %get-tuple-element.17), channel_id=1, source_target_pairs={{0,6},{1,7},{2,4},{3,5},{4,2},{5,3},{6,0},{7,1},{8,14},{9,15},{10,... | collective-permute-start | bytes 835592 | tf_op jit(solution)/shard_map/ppermute | solution.py:17
  28.0 14.3 %collective-permute-start.6 = (bf16[3264,128]{1,0:T(8,128)(2,1)}, bf16[3264,128]{1,0:T(8,128)(2,1)}, u32[]{:S(2)}, u32[]{:S(2)}) collective-permute-start(bf16[3264,128]{1,0:T(8,128)(2,1)} %constant_dynamic-update-slice_fusion.5.refs_0_), channel_id=1, source_target_pairs={{0,1},{1,0},{2,3},{3,2},{4,5},{5,4},{6,7},{7,6},{8,9},{9,8},{10,11... | collective-permute-start | bytes 2506760 | tf_op jit(solution)/shard_map/ppermute | solution.py:17
  28.0 12.6 %collective-permute-start.5 = (bf16[1088,128]{1,0:T(8,128)(2,1)S(1)}, bf16[1088,128]{1,0:T(8,128)(2,1)S(1)}, u32[]{:S(2)}, u32[]{:S(2)}) collective-permute-start(bf16[1088,128]{1,0:T(8,128)(2,1)S(1)} %collective-permute-done.4), channel_id=1, source_target_pairs={{0,2},{1,3},{2,0},{3,1},{4,6},{5,7},{6,4},{7,5},{8,10},{9,11},{10,... | collective-permute-start | bytes 835592 | tf_op jit(solution)/shard_map/ppermute | solution.py:17
  38.1 11.7 %collective-permute-start.10 = (bf16[256,1024]{1,0:T(8,128)(2,1)}, bf16[256,1024]{1,0:T(8,128)(2,1)}, u32[]{:S(2)}, u32[]{:S(2)}) collective-permute-start(bf16[256,1024]{1,0:T(8,128)(2,1)} %slice.8), channel_id=1, source_target_pairs={{0,16},{8,24},{16,0},{24,8},{1,17},{9,25},{17,1},{25,9},{2,18},{10... | collective-permute-start | bytes 1572872 | tf_op jit(solution)/shard_map/ppermute | solution.py:17
  39.5 10.8 %collective-permute-start.11 = (bf16[256,1024]{1,0:T(8,128)(2,1)}, bf16[256,1024]{1,0:T(8,128)(2,1)}, u32[]{:S(2)}, u32[]{:S(2)}) collective-permute-start(bf16[256,1024]{1,0:T(8,128)(2,1)} %slice.9), channel_id=1, source_target_pairs={{0,8},{8,0},{16,24},{24,16},{1,9},{9,1},{17,25},{25,17},{2,10},{10... | collective-permute-start | bytes 1572872 | tf_op jit(solution)/shard_map/ppermute | solution.py:17
  40.6 1.7 %collective-permute-start.7 = (bf16[1088,128]{1,0:T(8,128)(2,1)S(1)}, bf16[1088,128]{1,0:T(8,128)(2,1)}, u32[]{:S(2)}, u32[]{:S(2)}) collective-permute-start(bf16[1088,128]{1,0:T(8,128)(2,1)S(1)} %collective-permute-done.5.refs_1_), channel_id=1, source_target_pairs={{0,1},{1,0},{2,3},{3,2},{4,5},{5,4},{6,7},{7,6},{8,9},{9,8},{10,11... | collective-permute-start | bytes 835592 | tf_op jit(solution)/shard_map/ppermute | solution.py:17
  40.7 9.6 %copy-start = (bf16[2048,1024]{1,0:T(8,128)(2,1)S(1)}, bf16[2048,1024]{1,0:T(8,128)(2,1)}, u32[]{:S(2)}) copy-start(bf16[2048,1024]{1,0:T(8,128)(2,1)} %previous.1) | copy-start | bytes 12582916

commit v5 on v4

--- a/solution.py
+++ b/solution.py
@@ -7,6 +7,7 @@
 from jax.experimental.pallas import tpu as pltpu
 from jax.sharding import PartitionSpec as P
 
+SMALL = 1024 * 1024
 SLACK = 5 * 1024 * 1024
 PAD = 16
 TILE = 256
@@ -15,6 +16,47 @@
 def swap(x, axis, offset):
     size = lax.axis_size(axis)
     return lax.ppermute(x, axis, [(i, i ^ offset) for i in range(size)])
+
+
+def join_kernel(*refs):
+    parts, out, sems = refs[:-2], refs[-2], refs[-1]
+    copies, at = [], 0
+    for n, part in enumerate(parts):
+        rows = pl.ds(at, part.shape[0])
+        copies.append(pltpu.make_async_copy(part, out.at[rows], sems.at[n]))
+        copies[-1].start()
+        at += part.shape[0]
+    for copy in copies:
+        copy.wait()
+
+
+def join(parts):
+    rows = sum(part.shape[0] for part in parts)
+    return pl.pallas_call(
+        join_kernel,
+        out_shape=jax.ShapeDtypeStruct((rows, parts[0].shape[1]), parts[0].dtype),
+        in_specs=[pl.BlockSpec(memory_space=pl.ANY)] * len(parts),
+        out_specs=pl.BlockSpec(memory_space=pl.ANY),
+        scratch_shapes=[pltpu.SemaphoreType.DMA((len(parts),))],
+        compiler_params=pltpu.CompilerParams(vmem_limit_bytes=SMALL),
+        name="join",
+    )(*parts)
+
+
+def hold_kernel(*refs):
+    pass
+
+
+def hold(array, others):
+    return pl.pallas_call(
+        hold_kernel,
+        out_shape=jax.ShapeDtypeStruct(array.shape, array.dtype),
+        in_specs=[pl.BlockSpec(memory_space=pl.ANY)] * (1 + len(others)),
+        out_specs=pl.BlockSpec(memory_space=pl.ANY),
+        input_output_aliases={0: 0},
+        compiler_params=pltpu.CompilerParams(vmem_limit_bytes=SMALL),
+        name="hold",
+    )(array, *others)
 
 
 def early_kernel(dims, arrays, early, routes, spot, offsets, *refs):
@@ -179,6 +221,7 @@
     pieces = [(flat, [(0, 0, panels * rows)])]
     if grid_rows == 4 and panels == 2:
         size = panels * rows
+        flat = hold(flat, got)
         up, down = swap(flat, "row", 1), swap(flat, "row", 2)
         pieces += [(up, [(0, size, size)]), (down, [(0, 2 * size, size)])]
         final = [swap(up[:rows], "row", 2), swap(down[rows:], "row", 1)]
@@ -187,13 +230,12 @@
             pieces.append((swap(flat, "row", o), [(0, o * panels * rows, panels * rows)]))
         final = [swap(flat[p * rows : (p + 1) * rows], "row", last) for p in range(panels)]
 
-    own = jnp.concatenate([payload(0)] + got, axis=0)
+    own = join([payload(0)] + got)
     if grid_cols == 8:
         far, near = swap(own, "col", 6), swap(own, "col", 2)
         middle = swap(far, "col", 2)
-        offsets = [0, 2, 6, 4]
-        parts = [own, near, far, middle]
-        groups = [jnp.concatenate(parts[:3], axis=0), middle]
+        offsets = [0, 6, 2, 4]
+        groups = [jnp.concatenate([own, far], axis=0), near, middle]
         parts = groups
         others = [swap(group, "col", 1) for group in groups]
     else:

time: 55.4 us -> 53.6 us (0.968)
  local copies, waits for them, and re-layouts: 7.56 us -> 4.19 us
  starting transfers between devices: 13.2 us -> 14.2 us
  waiting for transfers between devices: 21.2 us -> 20.3 us
  other arithmetic: 0.88 us -> 1.63 us
  Pallas kernels: 12.3 us -> 12.9 us
    unnamed x14 -> x10, local copies, waits for them, and re-layouts: 3.34 us -> 1.31 us
    concatenate x2 -> x0, local copies, waits for them, and re-layouts: 1.37 us -> none  [the longest x1 0.73 us: per_device(): groups = [jnp.concatenate(parts[:3], axis=0), middle]]
    ppermute x12 -> x13, starting transfers between devices: 13.2 us -> 14.2 us  [swap(): return lax.ppermute(x, axis, [(i, i ^ offset) for i in range(size)])]
    ppermute x12 -> x13, waiting for transfers between devices: 21.2 us -> 20.3 us  [swap(): return lax.ppermute(x, axis, [(i, i ^ offset) for i in range(size)])]
    concatenate x0 -> x1, other arithmetic: none -> 0.84 us  [per_device(): groups = [jnp.concatenate([own, far], axis=0), near, middle]]
  transfers between devices with their start and end apart: 12 -> 13, of which waited for: 7 -> 7; matrix products, arithmetic and copies ran while one was open for 11% -> 7% of each run, Pallas kernels for 14% -> 15%
where the time goes in v5:
time: 53.6 us; the launch traced here: 53.3 us
  waiting for transfers between devices  20.3 us (38%)
  starting transfers between devices  14.2 us (26%)
  Pallas kernels  12.9 us (24%)
  local copies, waits for them, and re-layouts  4.19 us (8%)
  other arithmetic  1.63 us (3%)
    ppermute x13, waiting for transfers between devices, swap(): return lax.ppermute(x, axis, [(i, i ^ offset) for i in range(size)])  20.3 us
    ppermute x13, starting transfers between devices, swap(): return lax.ppermute(x, axis, [(i, i ^ offset) for i in range(size)])  14.2 us
    pallas_call x1, Pallas kernels, per_device(): pl.pallas_call(functools.partial(early_kernel, dims, len(record_arrays),...  7.72 us
    pallas_call x1, Pallas kernels, per_device(): pl.pallas_call(functools.partial(late_kernel, dims), out_shape=jax.ShapeD...  4.81 us
    slice x2, local copies, waits for them, and re-layouts, per_device(): final = [swap(up[:rows], 'row', 2), swap(down[rows:], 'row', 1)]  1.71 us
    unnamed x10, local copies, waits for them, and re-layouts  1.31 us
  transfers between devices with their start and end apart: 13, of which 7 were waited for; matrix products, arithmetic and copies ran while one was open for 7% of the time, Pallas kernels for 15%

profile of v5, /device:TPU:0, one launch (start us, length us, event | category | flops | bytes accessed | tf_op | source)
XLA Modules:
  0.0 53.3 jit_solution(12004716729483776295)
XLA Ops:
  0.0 0.7 %fusion.4 = bf16[4,2]{0,1:T(2,128)(2,1)S(1)} fusion(s32[4,2]{0,1:T(2,128)} %param.9, s32[4]{0:T(128)} %bitcast.14), kind=kLoop, calls=%fused_computation.18 | loop fusion | flops 24 | bytes 64 | tf_op jit(solution)/shard_map/convert_element_type | solution.py:205
  0.7 1.0 %constant_dynamic-slice_fusion = (bf16[1,2,128,128]{3,2,1,0:T(8,128)(2,1)S(1)}, bf16[1,2,128,128]{3,2,1,0:T(8,128)(2,1)S(1)}, bf16[1,2,128,128]{3,2,1,0:T(8,128)(2,1)S(1)}, bf16[1,2,128,128]{3,2,1,0:T(8,128)(2,1)S(1)}) fusion(bf16[4,2,128,128]{3,2,1,0:T(8,128)(2,1)} %param.7, s32[]{:T(128)S(6)} %select_n.26, s32[]{:T(128)S(6)} %select_n.24, ...), kind=kLoop, calls=%fused_computation.13 | loop fusion | bytes 524304 | tf_op jit(solution)/shard_map/jit(dynamic_index_in_dim)/dynamic_slice | solution.py:212
  1.6 0.2 fusion.3
  1.9 3.0 %collective-permute-start = (bf16[272,128]{1,0:T(8,128)(2,1)S(1)}, bf16[272,128]{1,0:T(8,128)(2,1)S(1)}, u32[]{:S(2)}, u32[]{:S(2)}) collective-permute-start(bf16[272,128]{1,0:T(8,128)(2,1)S(1)} %pad_maximum_fusion.2), channel_id=1, source_target_pairs={{0,8},{8,0},{16,24},{24,16},{1,9},{9,1},{17,25},{25,17},{2,10},{10... | collective-permute-start | bytes 208904 | tf_op jit(solution)/shard_map/ppermute | solution.py:18
  4.9 1.6 %collective-permute-start.1 = (bf16[272,128]{1,0:T(8,128)(2,1)S(1)}, bf16[272,128]{1,0:T(8,128)(2,1)S(1)}, u32[]{:S(2)}, u32[]{:S(2)}) collective-permute-start(bf16[272,128]{1,0:T(8,128)(2,1)S(1)} %pad_maximum_fusion.3), channel_id=1, source_target_pairs={{0,16},{8,24},{16,0},{24,8},{1,17},{9,25},{17,1},{25,9},{2,18},{10... | collective-permute-start | bytes 208904 | tf_op jit(solution)/shard_map/ppermute | solution.py:18
  6.5 0.1 collective-permute-start.2
  6.6 1.2 %copy.11.refs_0_ = bf16[512,1024]{1,0:T(8,128)(2,1)S(1)} copy(bf16[512,1024]{1,0:T(8,128)(2,1)} %bitcast.8) | data formatting | bytes 2097152
  7.8 1.5 %collective-permute-done.1.refs_2_ = bf16[272,128]{1,0:T(8,128)(2,1)S(1)} collective-permute-done((bf16[272,128]{1,0:T(8,128)(2,1)S(1)}, bf16[272,128]{1,0:T(8,128)(2,1)S(1)}, u32[]{:S(2)}, u32[]{:S(2)}) %collective-permute-start.1) | collective-permute-done | bytes 69664 | tf_op jit(solution)/shard_map/ppermute | solution.py:18
  9.3 2.5 %collective-permute-done.2.refs_3_ = bf16[272,128]{1,0:T(8,128)(2,1)S(1)} collective-permute-done((bf16[272,128]{1,0:T(8,128)(2,1)S(1)}, bf16[272,128]{1,0:T(8,128)(2,1)S(1)}, u32[]{:S(2)}, u32[]{:S(2)}) %collective-permute-start.2) | collective-permute-done | bytes 69664 | tf_op jit(solution)/shard_map/ppermute | solution.py:18
  11.8 0.6 %collective-permute-start.9 = (bf16[512,1024]{1,0:T(8,128)(2,1)S(1)}, bf16[512,1024]{1,0:T(8,128)(2,1)S(1)}, u32[]{:S(2)}, u32[]{:S(2)}) collective-permute-start(bf16[512,1024]{1,0:T(8,128)(2,1)S(1)} %hold.1), channel_id=1, source_target_pairs={{0,8},{8,0},{16,24},{24,16},{1,9},{9,1},{17,25},{25,17},{2,10},{10... | collective-permute-start | bytes 3145736 | tf_op jit(solution)/shard_map/ppermute | solution.py:18
  12.4 0.3 collective-permute-start.10
  12.7 0.4 join.1
  13.1 3.8 %collective-permute-start.3 = (bf16[1088,128]{1,0:T(8,128)(2,1)S(1)}, bf16[1088,128]{1,0:T(8,128)(2,1)S(1)}, u32[]{:S(2)}, u32[]{:S(2)}) collective-permute-start(bf16[1088,128]{1,0:T(8,128)(2,1)S(1)} %join.1), channel_id=1, source_target_pairs={{0,6},{1,7},{2,4},{3,5},{4,2},{5,3},{6,0},{7,1},{8,14},{9,15},{10,... | collective-permute-start | bytes 835592 | tf_op jit(solution)/shard_map/ppermute | solution.py:18
  17.0 0.0 collective-permute-start.4
  17.0 7.6 %collective-permute-done.3 = bf16[1088,128]{1,0:T(8,128)(2,1)S(1)} collective-permute-done((bf16[1088,128]{1,0:T(8,128)(2,1)S(1)}, bf16[1088,128]{1,0:T(8,128)(2,1)S(1)}, u32[]{:S(2)}, u32[]{:S(2)}) %collective-permute-start.3) | collective-permute-done | bytes 278560 | tf_op jit(solution)/shard_map/ppermute | solution.py:18
  24.6 0.8 %pad_maximum_fusion.refs_0_ = bf16[2176,128]{1,0:T(8,128)(2,1)} fusion(bf16[1088,128]{1,0:T(8,128)(2,1)S(1)} %collective-permute-done.3, bf16[1088,128]{1,0:T(8,128)(2,1)S(1)} %join.1), kind=kLoop, calls=%fused_computation | loop fusion | flops 1114112 | bytes 1114112 | tf_op jit(solution)/shard_map/concatenate | solution.py:238
  25.4 0.0 collective-permute-start.6
  25.4 2.8 %collective-permute-start.5 = (bf16[1088,128]{1,0:T(8,128)(2,1)S(1)}, bf16[1088,128]{1,0:T(8,128)(2,1)}, u32[]{:S(2)}, u32[]{:S(2)}) collective-permute-start(bf16[1088,128]{1,0:T(8,128)(2,1)S(1)} %collective-permute-done.3), channel_id=1, source_target_pairs={{0,2},{1,3},{2,0},{3,1},{4,6},{5,7},{6,4},{7,5},{8,10},{9,11},{10,... | collective-permute-start | bytes 835592 | tf_op jit(solution)/shard_map/ppermute | solution.py:18
  28.3 6.7 %collective-permute-done.9.refs_7_ = bf16[512,1024]{1,0:T(8,128)(2,1)S(1)} collective-permute-done((bf16[512,1024]{1,0:T(8,128)(2,1)S(1)}, bf16[512,1024]{1,0:T(8,128)(2,1)S(1)}, u32[]{:S(2)}, u32[]{:S(2)}) %collective-permute-start.9) | collective-permute-done | bytes 1048608 | tf_op jit(solution)/shard_map/ppermute | solution.py:18
  35.0 0.9 %slice.8 = bf16[256,1024]{1,0:T(8,128)(2,1)} slice(bf16[512,1024]{1,0:T(8,128)(2,1)S(1)} %collective-permute-done.9.refs_7_), slice={[0:256], [0:1024]} | slice | bytes 1048576 | tf_op jit(solution)/shard_map/slice | solution.py:227
  35.9 0.6 %collective-permute-start.11 = (bf16[256,1024]{1,0:T(8,128)(2,1)}, bf16[256,1024]{1,0:T(8,128)(2,1)}, u32[]{:S(2)}, u32[]{:S(2)}) collective-permute-start(bf16[256,1024]{1,0:T(8,128)(2,1)} %slice.8), channel_id=1, source_target_pairs={{0,16},{8,24},{16,0},{24,8},{1,17},{9,25},{17,1},{25,9},{2,18},{10... | collective-permute-start | bytes 1572872 | tf_op jit(solution)/shard_map/ppermute | solution.py:18
  36.4 0.8 %slice.9 = bf16[256,1024]{1,0:T(8,128)(2,1)} slice(bf16[512,1024]{1,0:T(8,128)(2,1)S(1)} %collective-permute-done.10.refs_8_), slice={[256:512], [0:1024]} | slice | bytes 1048576 | tf_op jit(solution)/shard_map/slice | solution.py:227
  37.3 0.9 %collective-permute-start.12 = (bf16[256,1024]{1,0:T(8,128)(2,1)}, bf16[256,1024]{1,0:T(8,128)(2,1)}, u32[]{:S(2)}, u32[]{:S(2)}) collective-permute-start(bf16[256,1024]{1,0:T(8,128)(2,1)} %slice.9), channel_id=1, source_target_pairs={{0,8},{8,0},{16,24},{24,16},{1,9},{9,1},{17,25},{25,17},{2,10},{10... | collective-permute-start | bytes 1572872 | tf_op jit(solution)/shard_map/ppermute | solution.py:18
  38.2 0.0 collective-permute-start.7
  38.2 0.5 collective-permute-start.8
  38.7 0.1 copy.10.keep
  38.8 0.1 pad_add_fusion.spot
  38.8 1.0 %collective-permute-done.7.refs_4_ = bf16[1088,128]{1,0:T(8,128)(2,1)} collective-permute-done((bf16[1088,128]{1,0:T(8,128)(2,1)S(1)}, bf16[1088,128]{1,0:T(8,128)(2,1)}, u32[]{:S(2)}, u32[]{:S(2)}) %collective-permute-start.7) | collective-permute-done | bytes 278560 | tf_op jit(solution)/shard_map/ppermute | solution.py:18
  39.9 0.6 %collective-permute-done.8.refs_5_ = bf16[1088,128]{1,0:T(8,128)(2,1)} collective-permute-done((bf16[1088,128]{1,0:T(8,128)(2,1)}, bf16[1088,128]{1,0:T(8,128)(2,1)}, u32[]{:S(2)}, u32[]{:S(2)}) %collective-permute-start.8) | collective-permute-done | bytes 278560 | tf_op jit(solution)/shard_map/ppermute | solution.py:18
  40.5 7.7 %early_product.1 = (f32[2048,1024]{1,0:T(8,128)S(1)}, bf16[4,2048,128]{2,1,0:T(8,128)(2,1)S(1)}) custom-call(s32[2]{0:T(128)S(1)} %pad_add_fusion.spot, s32[8]{0:T(128)S(1)} %copy-done.2, bf16[2176,128]{1,0:T(8,128)(2,1)} %pad_maximum_fusion.refs_0_, bf16[1088,128]{1,0:T(8,128)(2,1)S(1)} %collective-permute-done.4.refs_1_, ...), custom_call_target="tpu_custom_call" | custom-call | tf_op jit(solution)/shard_map/early_product/pallas_call | solution.py:257
  48.2 0.3 collective-permute-done.12.refs_1_
  48.5 4.8 %late_product.1 = bf16[2048,1024]{1,0:T(8,128)(2,1)} custom-call(s32[16,8]{1,0:T(8,128)S(1)} %copy.10.keep, f32[2048,1024]{1,0:T(8,128)S(1)} %get-tuple-element.7.acc, bf16[4,2048,128]{2,1,0:T(8,128)(2,1)S(1)} %get-tuple-element.8.late, bf16[2048,1024]{1,0:T(8,128)(2,1)S(1)} %copy-done.1, bf16[256,1024]{1,0:T(8,128)(2,1)} %collective-permute-done.11.refs_0_, ...), custom_call_target="tpu_custom_call" | custom-call | tf_op jit(solution)/shard_map/late_product/pallas_call | solution.py:283
  (23 shorter events, 0.1 us)
Async XLA Ops:
  1.9 5.9 %collective-permute-start = (bf16[272,128]{1,0:T(8,128)(2,1)S(1)}, bf16[272,128]{1,0:T(8,128)(2,1)S(1)}, u32[]{:S(2)}, u32[]{:S(2)}) collective-permute-start(bf16[272,128]{1,0:T(8,128)(2,1)S(1)} %pad_maximum_fusion.2), channel_id=1, source_target_pairs={{0,8},{8,0},{16,24},{24,16},{1,9},{9,1},{17,25},{25,17},{2,10},{10... | collective-permute-start | bytes 208904 | tf_op jit(solution)/shard_map/ppermute | solution.py:18
  4.9 4.4 %collective-permute-start.1 = (bf16[272,128]{1,0:T(8,128)(2,1)S(1)}, bf16[272,128]{1,0:T(8,128)(2,1)S(1)}, u32[]{:S(2)}, u32[]{:S(2)}) collective-permute-start(bf16[272,128]{1,0:T(8,128)(2,1)S(1)} %pad_maximum_fusion.3), channel_id=1, source_target_pairs={{0,16},{8,24},{16,0},{24,8},{1,17},{9,25},{17,1},{25,9},{2,18},{10... | collective-permute-start | bytes 208904 | tf_op jit(solution)/shard_map/ppermute | solution.py:18
  6.5 5.3 %collective-permute-start.2 = (bf16[272,128]{1,0:T(8,128)(2,1)S(1)}, bf16[272,128]{1,0:T(8,128)(2,1)S(1)}, u32[]{:S(2)}, u32[]{:S(2)}) collective-permute-start(bf16[272,128]{1,0:T(8,128)(2,1)S(1)} %pad_maximum_fusion.4), channel_id=1, source_target_pairs={{0,24},{8,16},{16,8},{24,0},{1,25},{9,17},{17,9},{25,1},{2,26},{10... | collective-permute-start | bytes 208904 | tf_op jit(solution)/shard_map/ppermute | solution.py:18
  11.8 26.9 %copy-start.3 = (s32[16,8]{0,1:T(8,128)S(1)}, s32[16,8]{0,1:T(8,128)}, u32[]{:S(2)}) copy-start(s32[16,8]{0,1:T(8,128)} %param.12) | copy-start | bytes 1540
  11.8 28.7 %copy-start = (bf16[2,256,1024]{2,1,0:T(8,128)(2,1)S(1)}, bf16[2,256,1024]{2,1,0:T(8,128)(2,1)}, u32[]{:S(2)}) copy-start(bf16[2,256,1024]{2,1,0:T(8,128)(2,1)} %param.10) | copy-start | bytes 3145732
  11.8 28.7 %copy-start.2 = (s32[8]{0:T(128)S(1)}, s32[8]{0:T(128)}, u32[]{:S(2)}) copy-start(s32[8]{0:T(128)} %constant.44.clone.offsets) | copy-start | bytes 100
  11.8 23.2 %collective-permute-start.9 = (bf16[512,1024]{1,0:T(8,128)(2,1)S(1)}, bf16[512,1024]{1,0:T(8,128)(2,1)S(1)}, u32[]{:S(2)}, u32[]{:S(2)}) collective-permute-start(bf16[512,1024]{1,0:T(8,128)(2,1)S(1)} %hold.1), channel_id=1, source_target_pairs={{0,8},{8,0},{16,24},{24,16},{1,9},{9,1},{17,25},{25,17},{2,10},{10... | collective-permute-start | bytes 3145736 | tf_op jit(solution)/shard_map/ppermute | solution.py:18
  12.4 24.1 %collective-permute-start.10 = (bf16[512,1024]{1,0:T(8,128)(2,1)S(1)}, bf16[512,1024]{1,0:T(8,128)(2,1)S(1)}, u32[]{:S(2)}, u32[]{:S(2)}) collective-permute-start(bf16[512,1024]{1,0:T(8,128)(2,1)S(1)} %hold.1), channel_id=1, source_target_pairs={{0,16},{8,24},{16,0},{24,8},{1,17},{9,25},{17,1},{25,9},{2,18},{10... | collective-permute-start | bytes 3145736 | tf_op jit(solution)/shard_map/ppermute | solution.py:18
  13.1 11.5 %collective-permute-start.3 = (bf16[1088,128]{1,0:T(8,128)(2,1)S(1)}, bf16[1088,128]{1,0:T(8,128)(2,1)S(1)}, u32[]{:S(2)}, u32[]{:S(2)}) collective-permute-start(bf16[1088,128]{1,0:T(8,128)(2,1)S(1)} %join.1), channel_id=1, source_target_pairs={{0,6},{1,7},{2,4},{3,5},{4,2},{5,3},{6,0},{7,1},{8,14},{9,15},{10,... | collective-permute-start | bytes 835592 | tf_op jit(solution)/shard_map/ppermute | solution.py:18
  17.0 21.2 %collective-permute-start.4 = (bf16[1088,128]{1,0:T(8,128)(2,1)S(1)}, bf16[1088,128]{1,0:T(8,128)(2,1)S(1)}, u32[]{:S(2)}, u32[]{:S(2)}) collective-permute-start(bf16[1088,128]{1,0:T(8,128)(2,1)S(1)} %join.1), channel_id=1, source_target_pairs={{0,2},{1,3},{2,0},{3,1},{4,6},{5,7},{6,4},{7,5},{8,10},{9,11},{10,... | collective-permute-start | bytes 835592 | tf_op jit(solution)/shard_map/ppermute | solution.py:18
  25.4 14.4 %collective-permute-start.6 = (bf16[2176,128]{1,0:T(8,128)(2,1)}, bf16[2176,128]{1,0:T(8,128)(2,1)}, u32[]{:S(2)}, u32[]{:S(2)}) collective-permute-start(bf16[2176,128]{1,0:T(8,128)(2,1)} %pad_maximum_fusion.refs_0_), channel_id=1, source_target_pairs={{0,1},{1,0},{2,3},{3,2},{4,5},{5,4},{6,7},{7,6},{8,9},{9,8},{10,11... | collective-permute-start | bytes 1671176 | tf_op jit(solution)/shard_map/ppermute | solution.py:18
  25.4 12.8 %collective-permute-start.5 = (bf16[1088,128]{1,0:T(8,128)(2,1)S(1)}, bf16[1088,128]{1,0:T(8,128)(2,1)}, u32[]{:S(2)}, u32[]{:S(2)}) collective-permute-start(bf16[1088,128]{1,0:T(8,128)(2,1)S(1)} %collective-permute-done.3), channel_id=1, source_target_pairs={{0,2},{1,3},{2,0},{3,1},{4,6},{5,7},{6,4},{7,5},{8,10},{9,11},{10,... | collective-permute-start | bytes 835592 | tf_op jit(solution)/shard_map/ppermute | solution.py:18
  35.9 12.3 %collective-permute-start.11 = (bf16[256,1024]{1,0:T(8,128)(2,1)}, bf16[256,1024]{1,0:T(8,128)(2,1)}, u32[]{:S(2)}, u32[]{:S(2)}) collective-permute-start(bf16[256,1024]{1,0:T(8,128)(2,1)} %slice.8), channel_id=1, source_target_pairs={{0,16},{8,24},{16,0},{24,8},{1,17},{9,25},{17,1},{25,9},{2,18},{10... | collective-permute-start | bytes 1572872 | tf_op jit(solution)/shard_map/ppermute | solution.py:18
  37.3 11.2 %collective-permute-start.12 = (bf16[256,1024]{1,0:T(8,128)(2,1)}, bf16[256,1024]{1,0:T(8,128)(2,1)}, u32[]{:S(2)}, u32[]{:S(2)}) collective-permute-start(bf16[256,1024]{1,0:T(8,128)(2,1)} %slice.9), channel_id=1, source_target_pairs={{0,8},{8,0},{16,24},{24,16},{1,9},{9,1},{17,25},{25,17},{2,10},{10... | collective-permute-start | bytes 1572872 | tf_op jit(solution)/shard_map/ppermute | solution.py:18
  38.2 1.7 %collective-permute-start.7 = (bf16[1088,128]{1,0:T(8,128)(2,1)S(1)}, bf16[1088,128]{1,0:T(8,128)(2,1)}, u32[]{:S(2)}, u32[]{:S(2)}) collective-permute-start(bf16[1088,128]{1,0:T(8,128)(2,1)S(1)} %collective-permute-done.4.refs_1_), channel_id=1, source_target_pairs={{0,1},{1,0},{2,3},{3,2},{4,5},{5,4},{6,7},{7,6},{8,9},{9,8},{10,11... | collective-permute-start | bytes 835592 | tf_op jit(solution)/shard_map/ppermute | solution.py:18
  38.2 2.3 %collective-permute-start.8 = (bf16[1088,128]{1,0:T(8,128)(2,1)}, bf16[1088,128]{1,0:T(8,128)(2,1)}, u32[]{:S(2)}, u32[]{:S(2)}) collective-permute-start(bf16[1088,128]{1,0:T(8,128)(2,1)} %collective-permute-done.5.refs_2_), channel_id=1, source_target_pairs={{0,1},{1,0},{2,3},{3,2},{4,5},{5,4},{6,7},{7,6},{8,9},{9,8},{10,11... | collective-permute-start | bytes 835592 | tf_op jit(solution)/shard_map/ppermute | solution.py:18
  38.8 9.7 %copy-start.1 = (bf16[2048,1024]{1,0:T(8,128)(2,1)S(1)}, bf16[2048,1024]{1,0:T(8,128)(2,1)}, u32[]{:S(2)}) copy-start(bf16[2048,1024]{1,0:T(8,128)(2,1)} %previous.1) | copy-start | bytes 12582916

commit v6 on v5

--- a/solution.py
+++ b/solution.py
@@ -57,6 +57,12 @@
         compiler_params=pltpu.CompilerParams(vmem_limit_bytes=SMALL),
         name="hold",
     )(array, *others)
+
+
+def split(number, size):
+    if size & (size - 1) == 0:
+        return number >> (size.bit_length() - 1), number & (size - 1)
+    return number // size, number % size
 
 
 def early_kernel(dims, arrays, early, routes, spot, offsets, *refs):
@@ -97,7 +103,7 @@
             depths[i, n] = 0
         return carry
 
-    lax.fori_loop(0, row_blocks + 1, clear, 0)
+    lax.fori_loop(0, row_blocks + 1, clear, 0, unroll=True)
     for copy in first:
         copy.wait()
     for n in range(count):
@@ -109,13 +115,12 @@
     my_row, my_col = spot[0], spot[1]
 
     def place(n, carry):
-        col = my_col ^ offsets[n // grid_rows]
-        source = (col // per_row) ^ my_row
-        inner = col % per_row
+        source, inner = split(my_col ^ offsets[split(n, grid_rows)[0]], per_row)
+        source = source ^ my_row
         for j in range(slots):
             code = codes[n, j]
-            row = code // panels
-            k = (source * panels + code % panels) * per_row + inner
+            row, panel = split(code, panels)
+            k = (source * panels + panel) * per_row + inner
             record = pl.multiple_of(n * span + j * block, PAD)
 
             to = jnp.where((code >= 0) & (k < early), row, row_blocks)
@@ -131,7 +136,7 @@
 
         return carry
 
-    lax.fori_loop(0, count, place, 0)
+    lax.fori_loop(0, count, place, 0, unroll=4)
     for copy in second:
         copy.wait()
 
@@ -160,7 +165,7 @@
             acc[rows, :] += 2.0 * pair(i, n)
             return inner
 
-        return lax.fori_loop(2, (counts[i] + 1) // 2, step, carry)
+        return lax.fori_loop(2, (counts[i] + 1) >> 1, step, carry)
 
     lax.fori_loop(0, row_blocks, more, 0)
 

time: 53.6 us -> 53.6 us (level)
  Pallas kernels: 12.9 us -> 12 us
  waiting for transfers between devices: 20.3 us -> 21.2 us
    ppermute x13, waiting for transfers between devices: 20.3 us -> 21.2 us  [swap(): return lax.ppermute(x, axis, [(i, i ^ offset) for i in range(size)])]
    pallas_call x1, Pallas kernels: 7.72 us -> 6.77 us  [per_device(): pl.pallas_call(functools.partial(early_kernel, dims, len(record_arrays),...]
  transfers between devices with their start and end apart: 13 -> 13, of which waited for: 7 -> 8; matrix products, arithmetic and copies ran while one was open for 7% -> 7% of each run, Pallas kernels for 15% -> 13%
where the time goes in v6:
time: 53.6 us; the launch traced here: 53.3 us
  waiting for transfers between devices  21.2 us (40%)
  starting transfers between devices  14.2 us (26%)
  Pallas kernels  12 us (22%)
  local copies, waits for them, and re-layouts  4.19 us (8%)
  other arithmetic  1.63 us (3%)
    ppermute x13, waiting for transfers between devices, swap(): return lax.ppermute(x, axis, [(i, i ^ offset) for i in range(size)])  21.2 us
    ppermute x13, starting transfers between devices, swap(): return lax.ppermute(x, axis, [(i, i ^ offset) for i in range(size)])  14.2 us
    pallas_call x1, Pallas kernels, per_device(): pl.pallas_call(functools.partial(early_kernel, dims, len(record_arrays),...  6.77 us
    pallas_call x1, Pallas kernels, per_device(): pl.pallas_call(functools.partial(late_kernel, dims), out_shape=jax.ShapeD...  4.81 us
    slice x2, local copies, waits for them, and re-layouts, per_device(): final = [swap(up[:rows], 'row', 2), swap(down[rows:], 'row', 1)]  1.71 us
    unnamed x10, local copies, waits for them, and re-layouts  1.31 us
  transfers between devices with their start and end apart: 13, of which 8 were waited for; matrix products, arithmetic and copies ran while one was open for 7% of the time, Pallas kernels for 13%

profile of v6, /device:TPU:0, one launch (start us, length us, event | category | flops | bytes accessed | tf_op | source)
XLA Modules:
  0.0 53.3 jit_solution(16350427596500458516)
XLA Ops:
  0.0 0.7 %fusion.4 = bf16[4,2]{0,1:T(2,128)(2,1)S(1)} fusion(s32[4,2]{0,1:T(2,128)} %param.9, s32[4]{0:T(128)} %bitcast.14), kind=kLoop, calls=%fused_computation.18 | loop fusion | flops 24 | bytes 64 | tf_op jit(solution)/shard_map/convert_element_type | solution.py:210
  0.7 1.0 %constant_dynamic-slice_fusion = (bf16[1,2,128,128]{3,2,1,0:T(8,128)(2,1)S(1)}, bf16[1,2,128,128]{3,2,1,0:T(8,128)(2,1)S(1)}, bf16[1,2,128,128]{3,2,1,0:T(8,128)(2,1)S(1)}, bf16[1,2,128,128]{3,2,1,0:T(8,128)(2,1)S(1)}) fusion(bf16[4,2,128,128]{3,2,1,0:T(8,128)(2,1)} %param.7, s32[]{:T(128)S(6)} %select_n.26, s32[]{:T(128)S(6)} %select_n.24, ...), kind=kLoop, calls=%fused_computation.13 | loop fusion | bytes 524304 | tf_op jit(solution)/shard_map/jit(dynamic_index_in_dim)/dynamic_slice | solution.py:217
  1.6 0.2 fusion.3
  1.9 3.0 %collective-permute-start = (bf16[272,128]{1,0:T(8,128)(2,1)S(1)}, bf16[272,128]{1,0:T(8,128)(2,1)S(1)}, u32[]{:S(2)}, u32[]{:S(2)}) collective-permute-start(bf16[272,128]{1,0:T(8,128)(2,1)S(1)} %pad_maximum_fusion.2), channel_id=1, source_target_pairs={{0,8},{8,0},{16,24},{24,16},{1,9},{9,1},{17,25},{25,17},{2,10},{10... | collective-permute-start | bytes 208904 | tf_op jit(solution)/shard_map/ppermute | solution.py:18
  4.9 1.6 %collective-permute-start.1 = (bf16[272,128]{1,0:T(8,128)(2,1)S(1)}, bf16[272,128]{1,0:T(8,128)(2,1)S(1)}, u32[]{:S(2)}, u32[]{:S(2)}) collective-permute-start(bf16[272,128]{1,0:T(8,128)(2,1)S(1)} %pad_maximum_fusion.3), channel_id=1, source_target_pairs={{0,16},{8,24},{16,0},{24,8},{1,17},{9,25},{17,1},{25,9},{2,18},{10... | collective-permute-start | bytes 208904 | tf_op jit(solution)/shard_map/ppermute | solution.py:18
  6.5 0.1 collective-permute-start.2
  6.6 1.2 %copy.11.refs_0_ = bf16[512,1024]{1,0:T(8,128)(2,1)S(1)} copy(bf16[512,1024]{1,0:T(8,128)(2,1)} %bitcast.8) | data formatting | bytes 2097152
  7.8 0.0 collective-permute-done.refs_1_
  7.8 1.5 %collective-permute-done.1.refs_2_ = bf16[272,128]{1,0:T(8,128)(2,1)S(1)} collective-permute-done((bf16[272,128]{1,0:T(8,128)(2,1)S(1)}, bf16[272,128]{1,0:T(8,128)(2,1)S(1)}, u32[]{:S(2)}, u32[]{:S(2)}) %collective-permute-start.1) | collective-permute-done | bytes 69664 | tf_op jit(solution)/shard_map/ppermute | solution.py:18
  9.3 2.5 %collective-permute-done.2.refs_3_ = bf16[272,128]{1,0:T(8,128)(2,1)S(1)} collective-permute-done((bf16[272,128]{1,0:T(8,128)(2,1)S(1)}, bf16[272,128]{1,0:T(8,128)(2,1)S(1)}, u32[]{:S(2)}, u32[]{:S(2)}) %collective-permute-start.2) | collective-permute-done | bytes 69664 | tf_op jit(solution)/shard_map/ppermute | solution.py:18
  11.8 0.6 %collective-permute-start.9 = (bf16[512,1024]{1,0:T(8,128)(2,1)S(1)}, bf16[512,1024]{1,0:T(8,128)(2,1)S(1)}, u32[]{:S(2)}, u32[]{:S(2)}) collective-permute-start(bf16[512,1024]{1,0:T(8,128)(2,1)S(1)} %hold.1), channel_id=1, source_target_pairs={{0,8},{8,0},{16,24},{24,16},{1,9},{9,1},{17,25},{25,17},{2,10},{10... | collective-permute-start | bytes 3145736 | tf_op jit(solution)/shard_map/ppermute | solution.py:18
  12.4 0.3 collective-permute-start.10
  12.7 0.4 join.1
  13.1 3.8 %collective-permute-start.3 = (bf16[1088,128]{1,0:T(8,128)(2,1)S(1)}, bf16[1088,128]{1,0:T(8,128)(2,1)S(1)}, u32[]{:S(2)}, u32[]{:S(2)}) collective-permute-start(bf16[1088,128]{1,0:T(8,128)(2,1)S(1)} %join.1), channel_id=1, source_target_pairs={{0,6},{1,7},{2,4},{3,5},{4,2},{5,3},{6,0},{7,1},{8,14},{9,15},{10,... | collective-permute-start | bytes 835592 | tf_op jit(solution)/shard_map/ppermute | solution.py:18
  17.0 7.6 %collective-permute-done.3 = bf16[1088,128]{1,0:T(8,128)(2,1)S(1)} collective-permute-done((bf16[1088,128]{1,0:T(8,128)(2,1)S(1)}, bf16[1088,128]{1,0:T(8,128)(2,1)S(1)}, u32[]{:S(2)}, u32[]{:S(2)}) %collective-permute-start.3) | collective-permute-done | bytes 278560 | tf_op jit(solution)/shard_map/ppermute | solution.py:18
  24.6 0.8 %pad_maximum_fusion.refs_0_ = bf16[2176,128]{1,0:T(8,128)(2,1)} fusion(bf16[1088,128]{1,0:T(8,128)(2,1)S(1)} %collective-permute-done.3, bf16[1088,128]{1,0:T(8,128)(2,1)S(1)} %join.1), kind=kLoop, calls=%fused_computation | loop fusion | flops 1114112 | bytes 1114112 | tf_op jit(solution)/shard_map/concatenate | solution.py:243
  25.4 0.0 collective-permute-start.6
  25.4 2.8 %collective-permute-start.5 = (bf16[1088,128]{1,0:T(8,128)(2,1)S(1)}, bf16[1088,128]{1,0:T(8,128)(2,1)}, u32[]{:S(2)}, u32[]{:S(2)}) collective-permute-start(bf16[1088,128]{1,0:T(8,128)(2,1)S(1)} %collective-permute-done.3), channel_id=1, source_target_pairs={{0,2},{1,3},{2,0},{3,1},{4,6},{5,7},{6,4},{7,5},{8,10},{9,11},{10,... | collective-permute-start | bytes 835592 | tf_op jit(solution)/shard_map/ppermute | solution.py:18
  28.3 6.7 %collective-permute-done.9.refs_7_ = bf16[512,1024]{1,0:T(8,128)(2,1)S(1)} collective-permute-done((bf16[512,1024]{1,0:T(8,128)(2,1)S(1)}, bf16[512,1024]{1,0:T(8,128)(2,1)S(1)}, u32[]{:S(2)}, u32[]{:S(2)}) %collective-permute-start.9) | collective-permute-done | bytes 1048608 | tf_op jit(solution)/shard_map/ppermute | solution.py:18
  35.0 0.9 %slice.8 = bf16[256,1024]{1,0:T(8,128)(2,1)} slice(bf16[512,1024]{1,0:T(8,128)(2,1)S(1)} %collective-permute-done.9.refs_7_), slice={[0:256], [0:1024]} | slice | bytes 1048576 | tf_op jit(solution)/shard_map/slice | solution.py:232
  35.9 0.6 %collective-permute-start.11 = (bf16[256,1024]{1,0:T(8,128)(2,1)}, bf16[256,1024]{1,0:T(8,128)(2,1)}, u32[]{:S(2)}, u32[]{:S(2)}) collective-permute-start(bf16[256,1024]{1,0:T(8,128)(2,1)} %slice.8), channel_id=1, source_target_pairs={{0,16},{8,24},{16,0},{24,8},{1,17},{9,25},{17,1},{25,9},{2,18},{10... | collective-permute-start | bytes 1572872 | tf_op jit(solution)/shard_map/ppermute | solution.py:18
  36.4 0.8 %slice.9 = bf16[256,1024]{1,0:T(8,128)(2,1)} slice(bf16[512,1024]{1,0:T(8,128)(2,1)S(1)} %collective-permute-done.10.refs_8_), slice={[256:512], [0:1024]} | slice | bytes 1048576 | tf_op jit(solution)/shard_map/slice | solution.py:232
  37.3 0.9 %collective-permute-start.12 = (bf16[256,1024]{1,0:T(8,128)(2,1)}, bf16[256,1024]{1,0:T(8,128)(2,1)}, u32[]{:S(2)}, u32[]{:S(2)}) collective-permute-start(bf16[256,1024]{1,0:T(8,128)(2,1)} %slice.9), channel_id=1, source_target_pairs={{0,8},{8,0},{16,24},{24,16},{1,9},{9,1},{17,25},{25,17},{2,10},{10... | collective-permute-start | bytes 1572872 | tf_op jit(solution)/shard_map/ppermute | solution.py:18
  38.2 0.5 collective-permute-start.8
  38.7 0.1 copy.10.keep
  38.8 0.1 pad_add_fusion.spot
  38.8 1.0 %collective-permute-done.7.refs_4_ = bf16[1088,128]{1,0:T(8,128)(2,1)} collective-permute-done((bf16[1088,128]{1,0:T(8,128)(2,1)S(1)}, bf16[1088,128]{1,0:T(8,128)(2,1)}, u32[]{:S(2)}, u32[]{:S(2)}) %collective-permute-start.7) | collective-permute-done | bytes 278560 | tf_op jit(solution)/shard_map/ppermute | solution.py:18
  39.9 0.6 %collective-permute-done.8.refs_5_ = bf16[1088,128]{1,0:T(8,128)(2,1)} collective-permute-done((bf16[1088,128]{1,0:T(8,128)(2,1)}, bf16[1088,128]{1,0:T(8,128)(2,1)}, u32[]{:S(2)}, u32[]{:S(2)}) %collective-permute-start.8) | collective-permute-done | bytes 278560 | tf_op jit(solution)/shard_map/ppermute | solution.py:18
  40.5 6.8 %early_product.1 = (f32[2048,1024]{1,0:T(8,128)S(1)}, bf16[4,2048,128]{2,1,0:T(8,128)(2,1)S(1)}) custom-call(s32[2]{0:T(128)S(1)} %pad_add_fusion.spot, s32[8]{0:T(128)S(1)} %copy-done.2, bf16[2176,128]{1,0:T(8,128)(2,1)} %pad_maximum_fusion.refs_0_, bf16[1088,128]{1,0:T(8,128)(2,1)S(1)} %collective-permute-done.4.refs_1_, ...), custom_call_target="tpu_custom_call" | custom-call | tf_op jit(solution)/shard_map/early_product/pallas_call | solution.py:262
  47.2 0.1 collective-permute-done.11.refs_0_
  47.3 1.2 %collective-permute-done.12.refs_1_ = bf16[256,1024]{1,0:T(8,128)(2,1)} collective-permute-done((bf16[256,1024]{1,0:T(8,128)(2,1)}, bf16[256,1024]{1,0:T(8,128)(2,1)}, u32[]{:S(2)}, u32[]{:S(2)}) %collective-permute-start.12) | collective-permute-done | bytes 524320 | tf_op jit(solution)/shard_map/ppermute | solution.py:18
  48.5 4.8 %late_product.1 = bf16[2048,1024]{1,0:T(8,128)(2,1)} custom-call(s32[16,8]{1,0:T(8,128)S(1)} %copy.10.keep, f32[2048,1024]{1,0:T(8,128)S(1)} %get-tuple-element.7.acc, bf16[4,2048,128]{2,1,0:T(8,128)(2,1)S(1)} %get-tuple-element.8.late, bf16[2048,1024]{1,0:T(8,128)(2,1)S(1)} %copy-done.1, bf16[256,1024]{1,0:T(8,128)(2,1)} %collective-permute-done.11.refs_0_, ...), custom_call_target="tpu_custom_call" | custom-call | tf_op jit(solution)/shard_map/late_product/pallas_call | solution.py:288
  (23 shorter events, 0.1 us)
Async XLA Ops:
  1.9 5.9 %collective-permute-start = (bf16[272,128]{1,0:T(8,128)(2,1)S(1)}, bf16[272,128]{1,0:T(8,128)(2,1)S(1)}, u32[]{:S(2)}, u32[]{:S(2)}) collective-permute-start(bf16[272,128]{1,0:T(8,128)(2,1)S(1)} %pad_maximum_fusion.2), channel_id=1, source_target_pairs={{0,8},{8,0},{16,24},{24,16},{1,9},{9,1},{17,25},{25,17},{2,10},{10... | collective-permute-start | bytes 208904 | tf_op jit(solution)/shard_map/ppermute | solution.py:18
  4.9 4.4 %collective-permute-start.1 = (bf16[272,128]{1,0:T(8,128)(2,1)S(1)}, bf16[272,128]{1,0:T(8,128)(2,1)S(1)}, u32[]{:S(2)}, u32[]{:S(2)}) collective-permute-start(bf16[272,128]{1,0:T(8,128)(2,1)S(1)} %pad_maximum_fusion.3), channel_id=1, source_target_pairs={{0,16},{8,24},{16,0},{24,8},{1,17},{9,25},{17,1},{25,9},{2,18},{10... | collective-permute-start | bytes 208904 | tf_op jit(solution)/shard_map/ppermute | solution.py:18
  6.5 5.3 %collective-permute-start.2 = (bf16[272,128]{1,0:T(8,128)(2,1)S(1)}, bf16[272,128]{1,0:T(8,128)(2,1)S(1)}, u32[]{:S(2)}, u32[]{:S(2)}) collective-permute-start(bf16[272,128]{1,0:T(8,128)(2,1)S(1)} %pad_maximum_fusion.4), channel_id=1, source_target_pairs={{0,24},{8,16},{16,8},{24,0},{1,25},{9,17},{17,9},{25,1},{2,26},{10... | collective-permute-start | bytes 208904 | tf_op jit(solution)/shard_map/ppermute | solution.py:18
  11.8 26.9 %copy-start.3 = (s32[16,8]{0,1:T(8,128)S(1)}, s32[16,8]{0,1:T(8,128)}, u32[]{:S(2)}) copy-start(s32[16,8]{0,1:T(8,128)} %param.12) | copy-start | bytes 1540
  11.8 28.7 %copy-start = (bf16[2,256,1024]{2,1,0:T(8,128)(2,1)S(1)}, bf16[2,256,1024]{2,1,0:T(8,128)(2,1)}, u32[]{:S(2)}) copy-start(bf16[2,256,1024]{2,1,0:T(8,128)(2,1)} %param.10) | copy-start | bytes 3145732
  11.8 28.7 %copy-start.2 = (s32[8]{0:T(128)S(1)}, s32[8]{0:T(128)}, u32[]{:S(2)}) copy-start(s32[8]{0:T(128)} %constant.44.clone.offsets) | copy-start | bytes 100
  11.8 23.2 %collective-permute-start.9 = (bf16[512,1024]{1,0:T(8,128)(2,1)S(1)}, bf16[512,1024]{1,0:T(8,128)(2,1)S(1)}, u32[]{:S(2)}, u32[]{:S(2)}) collective-permute-start(bf16[512,1024]{1,0:T(8,128)(2,1)S(1)} %hold.1), channel_id=1, source_target_pairs={{0,8},{8,0},{16,24},{24,16},{1,9},{9,1},{17,25},{25,17},{2,10},{10... | collective-permute-start | bytes 3145736 | tf_op jit(solution)/shard_map/ppermute | solution.py:18
  12.4 24.1 %collective-permute-start.10 = (bf16[512,1024]{1,0:T(8,128)(2,1)S(1)}, bf16[512,1024]{1,0:T(8,128)(2,1)S(1)}, u32[]{:S(2)}, u32[]{:S(2)}) collective-permute-start(bf16[512,1024]{1,0:T(8,128)(2,1)S(1)} %hold.1), channel_id=1, source_target_pairs={{0,16},{8,24},{16,0},{24,8},{1,17},{9,25},{17,1},{25,9},{2,18},{10... | collective-permute-start | bytes 3145736 | tf_op jit(solution)/shard_map/ppermute | solution.py:18
  13.1 11.5 %collective-permute-start.3 = (bf16[1088,128]{1,0:T(8,128)(2,1)S(1)}, bf16[1088,128]{1,0:T(8,128)(2,1)S(1)}, u32[]{:S(2)}, u32[]{:S(2)}) collective-permute-start(bf16[1088,128]{1,0:T(8,128)(2,1)S(1)} %join.1), channel_id=1, source_target_pairs={{0,6},{1,7},{2,4},{3,5},{4,2},{5,3},{6,0},{7,1},{8,14},{9,15},{10,... | collective-permute-start | bytes 835592 | tf_op jit(solution)/shard_map/ppermute | solution.py:18
  17.0 21.2 %collective-permute-start.4 = (bf16[1088,128]{1,0:T(8,128)(2,1)S(1)}, bf16[1088,128]{1,0:T(8,128)(2,1)S(1)}, u32[]{:S(2)}, u32[]{:S(2)}) collective-permute-start(bf16[1088,128]{1,0:T(8,128)(2,1)S(1)} %join.1), channel_id=1, source_target_pairs={{0,2},{1,3},{2,0},{3,1},{4,6},{5,7},{6,4},{7,5},{8,10},{9,11},{10,... | collective-permute-start | bytes 835592 | tf_op jit(solution)/shard_map/ppermute | solution.py:18
  25.4 14.4 %collective-permute-start.6 = (bf16[2176,128]{1,0:T(8,128)(2,1)}, bf16[2176,128]{1,0:T(8,128)(2,1)}, u32[]{:S(2)}, u32[]{:S(2)}) collective-permute-start(bf16[2176,128]{1,0:T(8,128)(2,1)} %pad_maximum_fusion.refs_0_), channel_id=1, source_target_pairs={{0,1},{1,0},{2,3},{3,2},{4,5},{5,4},{6,7},{7,6},{8,9},{9,8},{10,11... | collective-permute-start | bytes 1671176 | tf_op jit(solution)/shard_map/ppermute | solution.py:18
  25.4 12.8 %collective-permute-start.5 = (bf16[1088,128]{1,0:T(8,128)(2,1)S(1)}, bf16[1088,128]{1,0:T(8,128)(2,1)}, u32[]{:S(2)}, u32[]{:S(2)}) collective-permute-start(bf16[1088,128]{1,0:T(8,128)(2,1)S(1)} %collective-permute-done.3), channel_id=1, source_target_pairs={{0,2},{1,3},{2,0},{3,1},{4,6},{5,7},{6,4},{7,5},{8,10},{9,11},{10,... | collective-permute-start | bytes 835592 | tf_op jit(solution)/shard_map/ppermute | solution.py:18
  35.9 11.5 %collective-permute-start.11 = (bf16[256,1024]{1,0:T(8,128)(2,1)}, bf16[256,1024]{1,0:T(8,128)(2,1)}, u32[]{:S(2)}, u32[]{:S(2)}) collective-permute-start(bf16[256,1024]{1,0:T(8,128)(2,1)} %slice.8), channel_id=1, source_target_pairs={{0,16},{8,24},{16,0},{24,8},{1,17},{9,25},{17,1},{25,9},{2,18},{10... | collective-permute-start | bytes 1572872 | tf_op jit(solution)/shard_map/ppermute | solution.py:18
  37.3 11.2 %collective-permute-start.12 = (bf16[256,1024]{1,0:T(8,128)(2,1)}, bf16[256,1024]{1,0:T(8,128)(2,1)}, u32[]{:S(2)}, u32[]{:S(2)}) collective-permute-start(bf16[256,1024]{1,0:T(8,128)(2,1)} %slice.9), channel_id=1, source_target_pairs={{0,8},{8,0},{16,24},{24,16},{1,9},{9,1},{17,25},{25,17},{2,10},{10... | collective-permute-start | bytes 1572872 | tf_op jit(solution)/shard_map/ppermute | solution.py:18
  38.2 1.7 %collective-permute-start.7 = (bf16[1088,128]{1,0:T(8,128)(2,1)S(1)}, bf16[1088,128]{1,0:T(8,128)(2,1)}, u32[]{:S(2)}, u32[]{:S(2)}) collective-permute-start(bf16[1088,128]{1,0:T(8,128)(2,1)S(1)} %collective-permute-done.4.refs_1_), channel_id=1, source_target_pairs={{0,1},{1,0},{2,3},{3,2},{4,5},{5,4},{6,7},{7,6},{8,9},{9,8},{10,11... | collective-permute-start | bytes 835592 | tf_op jit(solution)/shard_map/ppermute | solution.py:18
  38.2 2.3 %collective-permute-start.8 = (bf16[1088,128]{1,0:T(8,128)(2,1)}, bf16[1088,128]{1,0:T(8,128)(2,1)}, u32[]{:S(2)}, u32[]{:S(2)}) collective-permute-start(bf16[1088,128]{1,0:T(8,128)(2,1)} %collective-permute-done.5.refs_2_), channel_id=1, source_target_pairs={{0,1},{1,0},{2,3},{3,2},{4,5},{5,4},{6,7},{7,6},{8,9},{9,8},{10,11... | collective-permute-start | bytes 835592 | tf_op jit(solution)/shard_map/ppermute | solution.py:18
  38.8 9.7 %copy-start.1 = (bf16[2048,1024]{1,0:T(8,128)(2,1)S(1)}, bf16[2048,1024]{1,0:T(8,128)(2,1)}, u32[]{:S(2)}) copy-start(bf16[2048,1024]{1,0:T(8,128)(2,1)} %previous.1) | copy-start | bytes 12582916

commit v7 on v6

--- a/solution.py
+++ b/solution.py
@@ -229,7 +229,8 @@
         flat = hold(flat, got)
         up, down = swap(flat, "row", 1), swap(flat, "row", 2)
         pieces += [(up, [(0, size, size)]), (down, [(0, 2 * size, size)])]
-        final = [swap(up[:rows], "row", 2), swap(down[rows:], "row", 1)]
+        at = rows + PAD
+        final = [swap(up[:at], "row", 2), swap(down[at:], "row", 1)]
     else:
         for o in range(1, last):
             pieces.append((swap(flat, "row", o), [(0, o * panels * rows, panels * rows)]))

time: 53.6 us -> 53.1 us (level)
  transfers between devices with their start and end apart: 13 -> 13, of which waited for: 8 -> 8; matrix products, arithmetic and copies ran while one was open for 7% -> 7% of each run, Pallas kernels for 13% -> 14%
where the time goes in v7:
time: 53.1 us; the launch traced here: 52.8 us
  waiting for transfers between devices  20.8 us (39%)
  starting transfers between devices  14.2 us (27%)
  Pallas kernels  12 us (23%)
  local copies, waits for them, and re-layouts  4.14 us (8%)
  other arithmetic  1.63 us (3%)
    ppermute x13, waiting for transfers between devices, swap(): return lax.ppermute(x, axis, [(i, i ^ offset) for i in range(size)])  20.8 us
    ppermute x13, starting transfers between devices, swap(): return lax.ppermute(x, axis, [(i, i ^ offset) for i in range(size)])  14.2 us
    pallas_call x1, Pallas kernels, per_device(): pl.pallas_call(functools.partial(early_kernel, dims, len(record_arrays),...  6.75 us
    pallas_call x1, Pallas kernels, per_device(): pl.pallas_call(functools.partial(late_kernel, dims), out_shape=jax.ShapeD...  4.82 us
    slice x2, local copies, waits for them, and re-layouts, per_device(): final = [swap(up[:at], 'row', 2), swap(down[at:], 'row', 1)]  1.66 us
    unnamed x10, local copies, waits for them, and re-layouts  1.31 us
  transfers between devices with their start and end apart: 13, of which 8 were waited for; matrix products, arithmetic and copies ran while one was open for 7% of the time, Pallas kernels for 14%

profile of v7, /device:TPU:0, one launch (start us, length us, event | category | flops | bytes accessed | tf_op | source)
XLA Modules:
  0.0 52.8 jit_solution(5336574538073266781)
XLA Ops:
  0.0 0.7 %fusion.4 = bf16[4,2]{0,1:T(2,128)(2,1)S(1)} fusion(s32[4,2]{0,1:T(2,128)} %param.9, s32[4]{0:T(128)} %bitcast.14), kind=kLoop, calls=%fused_computation.18 | loop fusion | flops 24 | bytes 64 | tf_op jit(solution)/shard_map/convert_element_type | solution.py:210
  0.7 1.0 %constant_dynamic-slice_fusion = (bf16[1,2,128,128]{3,2,1,0:T(8,128)(2,1)S(1)}, bf16[1,2,128,128]{3,2,1,0:T(8,128)(2,1)S(1)}, bf16[1,2,128,128]{3,2,1,0:T(8,128)(2,1)S(1)}, bf16[1,2,128,128]{3,2,1,0:T(8,128)(2,1)S(1)}) fusion(bf16[4,2,128,128]{3,2,1,0:T(8,128)(2,1)} %param.7, s32[]{:T(128)S(6)} %select_n.26, s32[]{:T(128)S(6)} %select_n.24, ...), kind=kLoop, calls=%fused_computation.13 | loop fusion | bytes 524304 | tf_op jit(solution)/shard_map/jit(dynamic_index_in_dim)/dynamic_slice | solution.py:217
  1.6 0.2 fusion.3
  1.9 3.0 %collective-permute-start = (bf16[272,128]{1,0:T(8,128)(2,1)S(1)}, bf16[272,128]{1,0:T(8,128)(2,1)S(1)}, u32[]{:S(2)}, u32[]{:S(2)}) collective-permute-start(bf16[272,128]{1,0:T(8,128)(2,1)S(1)} %pad_maximum_fusion.2), channel_id=1, source_target_pairs={{0,8},{8,0},{16,24},{24,16},{1,9},{9,1},{17,25},{25,17},{2,10},{10... | collective-permute-start | bytes 208904 | tf_op jit(solution)/shard_map/ppermute | solution.py:18
  4.9 1.6 %collective-permute-start.1 = (bf16[272,128]{1,0:T(8,128)(2,1)S(1)}, bf16[272,128]{1,0:T(8,128)(2,1)S(1)}, u32[]{:S(2)}, u32[]{:S(2)}) collective-permute-start(bf16[272,128]{1,0:T(8,128)(2,1)S(1)} %pad_maximum_fusion.3), channel_id=1, source_target_pairs={{0,16},{8,24},{16,0},{24,8},{1,17},{9,25},{17,1},{25,9},{2,18},{10... | collective-permute-start | bytes 208904 | tf_op jit(solution)/shard_map/ppermute | solution.py:18
  6.5 0.1 collective-permute-start.2
  6.6 1.2 %copy.11.refs_0_ = bf16[512,1024]{1,0:T(8,128)(2,1)S(1)} copy(bf16[512,1024]{1,0:T(8,128)(2,1)} %bitcast.8) | data formatting | bytes 2097152
  7.8 0.0 collective-permute-done.refs_1_
  7.8 1.5 %collective-permute-done.1.refs_2_ = bf16[272,128]{1,0:T(8,128)(2,1)S(1)} collective-permute-done((bf16[272,128]{1,0:T(8,128)(2,1)S(1)}, bf16[272,128]{1,0:T(8,128)(2,1)S(1)}, u32[]{:S(2)}, u32[]{:S(2)}) %collective-permute-start.1) | collective-permute-done | bytes 69664 | tf_op jit(solution)/shard_map/ppermute | solution.py:18
  9.3 2.5 %collective-permute-done.2.refs_3_ = bf16[272,128]{1,0:T(8,128)(2,1)S(1)} collective-permute-done((bf16[272,128]{1,0:T(8,128)(2,1)S(1)}, bf16[272,128]{1,0:T(8,128)(2,1)S(1)}, u32[]{:S(2)}, u32[]{:S(2)}) %collective-permute-start.2) | collective-permute-done | bytes 69664 | tf_op jit(solution)/shard_map/ppermute | solution.py:18
  11.8 0.6 %collective-permute-start.9 = (bf16[512,1024]{1,0:T(8,128)(2,1)S(1)}, bf16[512,1024]{1,0:T(8,128)(2,1)S(1)}, u32[]{:S(2)}, u32[]{:S(2)}) collective-permute-start(bf16[512,1024]{1,0:T(8,128)(2,1)S(1)} %hold.1), channel_id=1, source_target_pairs={{0,8},{8,0},{16,24},{24,16},{1,9},{9,1},{17,25},{25,17},{2,10},{10... | collective-permute-start | bytes 3145736 | tf_op jit(solution)/shard_map/ppermute | solution.py:18
  12.4 0.3 collective-permute-start.10
  12.7 0.4 join.1
  13.1 3.8 %collective-permute-start.3 = (bf16[1088,128]{1,0:T(8,128)(2,1)S(1)}, bf16[1088,128]{1,0:T(8,128)(2,1)S(1)}, u32[]{:S(2)}, u32[]{:S(2)}) collective-permute-start(bf16[1088,128]{1,0:T(8,128)(2,1)S(1)} %join.1), channel_id=1, source_target_pairs={{0,6},{1,7},{2,4},{3,5},{4,2},{5,3},{6,0},{7,1},{8,14},{9,15},{10,... | collective-permute-start | bytes 835592 | tf_op jit(solution)/shard_map/ppermute | solution.py:18
  17.0 0.0 collective-permute-start.4
  17.0 7.6 %collective-permute-done.3 = bf16[1088,128]{1,0:T(8,128)(2,1)S(1)} collective-permute-done((bf16[1088,128]{1,0:T(8,128)(2,1)S(1)}, bf16[1088,128]{1,0:T(8,128)(2,1)S(1)}, u32[]{:S(2)}, u32[]{:S(2)}) %collective-permute-start.3) | collective-permute-done | bytes 278560 | tf_op jit(solution)/shard_map/ppermute | solution.py:18
  24.6 0.8 %pad_maximum_fusion.refs_0_ = bf16[2176,128]{1,0:T(8,128)(2,1)} fusion(bf16[1088,128]{1,0:T(8,128)(2,1)S(1)} %collective-permute-done.3, bf16[1088,128]{1,0:T(8,128)(2,1)S(1)} %join.1), kind=kLoop, calls=%fused_computation | loop fusion | flops 1114112 | bytes 1114112 | tf_op jit(solution)/shard_map/concatenate | solution.py:244
  25.4 2.8 %collective-permute-start.5 = (bf16[1088,128]{1,0:T(8,128)(2,1)S(1)}, bf16[1088,128]{1,0:T(8,128)(2,1)}, u32[]{:S(2)}, u32[]{:S(2)}) collective-permute-start(bf16[1088,128]{1,0:T(8,128)(2,1)S(1)} %collective-permute-done.3), channel_id=1, source_target_pairs={{0,2},{1,3},{2,0},{3,1},{4,6},{5,7},{6,4},{7,5},{8,10},{9,11},{10,... | collective-permute-start | bytes 835592 | tf_op jit(solution)/shard_map/ppermute | solution.py:18
  28.3 6.7 %collective-permute-done.9.refs_7_ = bf16[512,1024]{1,0:T(8,128)(2,1)S(1)} collective-permute-done((bf16[512,1024]{1,0:T(8,128)(2,1)S(1)}, bf16[512,1024]{1,0:T(8,128)(2,1)S(1)}, u32[]{:S(2)}, u32[]{:S(2)}) %collective-permute-start.9) | collective-permute-done | bytes 1048608 | tf_op jit(solution)/shard_map/ppermute | solution.py:18
  35.0 0.8 %slice.8 = bf16[272,1024]{1,0:T(8,128)(2,1)} slice(bf16[512,1024]{1,0:T(8,128)(2,1)S(1)} %collective-permute-done.9.refs_7_), slice={[0:272], [0:1024]} | slice | bytes 1114112 | tf_op jit(solution)/shard_map/slice | solution.py:233
  35.9 0.6 %collective-permute-start.11 = (bf16[272,1024]{1,0:T(8,128)(2,1)}, bf16[272,1024]{1,0:T(8,128)(2,1)}, u32[]{:S(2)}, u32[]{:S(2)}) collective-permute-start(bf16[272,1024]{1,0:T(8,128)(2,1)} %slice.8), channel_id=1, source_target_pairs={{0,16},{8,24},{16,0},{24,8},{1,17},{9,25},{17,1},{25,9},{2,18},{10... | collective-permute-start | bytes 1671176 | tf_op jit(solution)/shard_map/ppermute | solution.py:18
  36.4 0.8 %slice.9 = bf16[240,1024]{1,0:T(8,128)(2,1)} slice(bf16[512,1024]{1,0:T(8,128)(2,1)S(1)} %collective-permute-done.10.refs_8_), slice={[272:512], [0:1024]} | slice | bytes 983040 | tf_op jit(solution)/shard_map/slice | solution.py:233
  37.2 0.9 %collective-permute-start.12 = (bf16[240,1024]{1,0:T(8,128)(2,1)}, bf16[240,1024]{1,0:T(8,128)(2,1)}, u32[]{:S(2)}, u32[]{:S(2)}) collective-permute-start(bf16[240,1024]{1,0:T(8,128)(2,1)} %slice.9), channel_id=1, source_target_pairs={{0,8},{8,0},{16,24},{24,16},{1,9},{9,1},{17,25},{25,17},{2,10},{10... | collective-permute-start | bytes 1474568 | tf_op jit(solution)/shard_map/ppermute | solution.py:18
  38.1 0.5 collective-permute-start.8
  38.6 0.1 copy.10.keep
  38.7 0.1 pad_add_fusion.spot
  38.8 1.0 %collective-permute-done.7.refs_4_ = bf16[1088,128]{1,0:T(8,128)(2,1)} collective-permute-done((bf16[1088,128]{1,0:T(8,128)(2,1)S(1)}, bf16[1088,128]{1,0:T(8,128)(2,1)}, u32[]{:S(2)}, u32[]{:S(2)}) %collective-permute-start.7) | collective-permute-done | bytes 278560 | tf_op jit(solution)/shard_map/ppermute | solution.py:18
  39.8 0.6 %collective-permute-done.8.refs_5_ = bf16[1088,128]{1,0:T(8,128)(2,1)} collective-permute-done((bf16[1088,128]{1,0:T(8,128)(2,1)}, bf16[1088,128]{1,0:T(8,128)(2,1)}, u32[]{:S(2)}, u32[]{:S(2)}) %collective-permute-start.8) | collective-permute-done | bytes 278560 | tf_op jit(solution)/shard_map/ppermute | solution.py:18
  40.4 6.8 %early_product.1 = (f32[2048,1024]{1,0:T(8,128)S(1)}, bf16[4,2048,128]{2,1,0:T(8,128)(2,1)S(1)}) custom-call(s32[2]{0:T(128)S(1)} %pad_add_fusion.spot, s32[8]{0:T(128)S(1)} %copy-done.2, bf16[2176,128]{1,0:T(8,128)(2,1)} %pad_maximum_fusion.refs_0_, bf16[1088,128]{1,0:T(8,128)(2,1)S(1)} %collective-permute-done.4.refs_1_, ...), custom_call_target="tpu_custom_call" | custom-call | tf_op jit(solution)/shard_map/early_product/pallas_call | solution.py:263
  47.2 0.6 %collective-permute-done.12.refs_1_ = bf16[240,1024]{1,0:T(8,128)(2,1)} collective-permute-done((bf16[240,1024]{1,0:T(8,128)(2,1)}, bf16[240,1024]{1,0:T(8,128)(2,1)}, u32[]{:S(2)}, u32[]{:S(2)}) %collective-permute-start.12) | collective-permute-done | bytes 491552 | tf_op jit(solution)/shard_map/ppermute | solution.py:18
  47.8 0.2 collective-permute-done.11.refs_0_
  48.0 4.8 %late_product.1 = bf16[2048,1024]{1,0:T(8,128)(2,1)} custom-call(s32[16,8]{1,0:T(8,128)S(1)} %copy.10.keep, f32[2048,1024]{1,0:T(8,128)S(1)} %get-tuple-element.7.acc, bf16[4,2048,128]{2,1,0:T(8,128)(2,1)S(1)} %get-tuple-element.8.late, bf16[2048,1024]{1,0:T(8,128)(2,1)S(1)} %copy-done.1, bf16[272,1024]{1,0:T(8,128)(2,1)} %collective-permute-done.11.refs_0_, ...), custom_call_target="tpu_custom_call" | custom-call | tf_op jit(solution)/shard_map/late_product/pallas_call | solution.py:289
  (23 shorter events, 0.1 us)
Async XLA Ops:
  1.9 5.9 %collective-permute-start = (bf16[272,128]{1,0:T(8,128)(2,1)S(1)}, bf16[272,128]{1,0:T(8,128)(2,1)S(1)}, u32[]{:S(2)}, u32[]{:S(2)}) collective-permute-start(bf16[272,128]{1,0:T(8,128)(2,1)S(1)} %pad_maximum_fusion.2), channel_id=1, source_target_pairs={{0,8},{8,0},{16,24},{24,16},{1,9},{9,1},{17,25},{25,17},{2,10},{10... | collective-permute-start | bytes 208904 | tf_op jit(solution)/shard_map/ppermute | solution.py:18
  4.9 4.4 %collective-permute-start.1 = (bf16[272,128]{1,0:T(8,128)(2,1)S(1)}, bf16[272,128]{1,0:T(8,128)(2,1)S(1)}, u32[]{:S(2)}, u32[]{:S(2)}) collective-permute-start(bf16[272,128]{1,0:T(8,128)(2,1)S(1)} %pad_maximum_fusion.3), channel_id=1, source_target_pairs={{0,16},{8,24},{16,0},{24,8},{1,17},{9,25},{17,1},{25,9},{2,18},{10... | collective-permute-start | bytes 208904 | tf_op jit(solution)/shard_map/ppermute | solution.py:18
  6.5 5.3 %collective-permute-start.2 = (bf16[272,128]{1,0:T(8,128)(2,1)S(1)}, bf16[272,128]{1,0:T(8,128)(2,1)S(1)}, u32[]{:S(2)}, u32[]{:S(2)}) collective-permute-start(bf16[272,128]{1,0:T(8,128)(2,1)S(1)} %pad_maximum_fusion.4), channel_id=1, source_target_pairs={{0,24},{8,16},{16,8},{24,0},{1,25},{9,17},{17,9},{25,1},{2,26},{10... | collective-permute-start | bytes 208904 | tf_op jit(solution)/shard_map/ppermute | solution.py:18
  11.8 26.9 %copy-start.3 = (s32[16,8]{0,1:T(8,128)S(1)}, s32[16,8]{0,1:T(8,128)}, u32[]{:S(2)}) copy-start(s32[16,8]{0,1:T(8,128)} %param.12) | copy-start | bytes 1540
  11.8 28.7 %copy-start = (bf16[2,256,1024]{2,1,0:T(8,128)(2,1)S(1)}, bf16[2,256,1024]{2,1,0:T(8,128)(2,1)}, u32[]{:S(2)}) copy-start(bf16[2,256,1024]{2,1,0:T(8,128)(2,1)} %param.10) | copy-start | bytes 3145732
  11.8 28.7 %copy-start.2 = (s32[8]{0:T(128)S(1)}, s32[8]{0:T(128)}, u32[]{:S(2)}) copy-start(s32[8]{0:T(128)} %constant.44.clone.offsets) | copy-start | bytes 100
  11.8 23.2 %collective-permute-start.9 = (bf16[512,1024]{1,0:T(8,128)(2,1)S(1)}, bf16[512,1024]{1,0:T(8,128)(2,1)S(1)}, u32[]{:S(2)}, u32[]{:S(2)}) collective-permute-start(bf16[512,1024]{1,0:T(8,128)(2,1)S(1)} %hold.1), channel_id=1, source_target_pairs={{0,8},{8,0},{16,24},{24,16},{1,9},{9,1},{17,25},{25,17},{2,10},{10... | collective-permute-start | bytes 3145736 | tf_op jit(solution)/shard_map/ppermute | solution.py:18
  12.4 24.1 %collective-permute-start.10 = (bf16[512,1024]{1,0:T(8,128)(2,1)S(1)}, bf16[512,1024]{1,0:T(8,128)(2,1)S(1)}, u32[]{:S(2)}, u32[]{:S(2)}) collective-permute-start(bf16[512,1024]{1,0:T(8,128)(2,1)S(1)} %hold.1), channel_id=1, source_target_pairs={{0,16},{8,24},{16,0},{24,8},{1,17},{9,25},{17,1},{25,9},{2,18},{10... | collective-permute-start | bytes 3145736 | tf_op jit(solution)/shard_map/ppermute | solution.py:18
  13.1 11.5 %collective-permute-start.3 = (bf16[1088,128]{1,0:T(8,128)(2,1)S(1)}, bf16[1088,128]{1,0:T(8,128)(2,1)S(1)}, u32[]{:S(2)}, u32[]{:S(2)}) collective-permute-start(bf16[1088,128]{1,0:T(8,128)(2,1)S(1)} %join.1), channel_id=1, source_target_pairs={{0,6},{1,7},{2,4},{3,5},{4,2},{5,3},{6,0},{7,1},{8,14},{9,15},{10,... | collective-permute-start | bytes 835592 | tf_op jit(solution)/shard_map/ppermute | solution.py:18
  17.0 21.2 %collective-permute-start.4 = (bf16[1088,128]{1,0:T(8,128)(2,1)S(1)}, bf16[1088,128]{1,0:T(8,128)(2,1)S(1)}, u32[]{:S(2)}, u32[]{:S(2)}) collective-permute-start(bf16[1088,128]{1,0:T(8,128)(2,1)S(1)} %join.1), channel_id=1, source_target_pairs={{0,2},{1,3},{2,0},{3,1},{4,6},{5,7},{6,4},{7,5},{8,10},{9,11},{10,... | collective-permute-start | bytes 835592 | tf_op jit(solution)/shard_map/ppermute | solution.py:18
  25.4 14.4 %collective-permute-start.6 = (bf16[2176,128]{1,0:T(8,128)(2,1)}, bf16[2176,128]{1,0:T(8,128)(2,1)}, u32[]{:S(2)}, u32[]{:S(2)}) collective-permute-start(bf16[2176,128]{1,0:T(8,128)(2,1)} %pad_maximum_fusion.refs_0_), channel_id=1, source_target_pairs={{0,1},{1,0},{2,3},{3,2},{4,5},{5,4},{6,7},{7,6},{8,9},{9,8},{10,11... | collective-permute-start | bytes 1671176 | tf_op jit(solution)/shard_map/ppermute | solution.py:18
  25.4 12.7 %collective-permute-start.5 = (bf16[1088,128]{1,0:T(8,128)(2,1)S(1)}, bf16[1088,128]{1,0:T(8,128)(2,1)}, u32[]{:S(2)}, u32[]{:S(2)}) collective-permute-start(bf16[1088,128]{1,0:T(8,128)(2,1)S(1)} %collective-permute-done.3), channel_id=1, source_target_pairs={{0,2},{1,3},{2,0},{3,1},{4,6},{5,7},{6,4},{7,5},{8,10},{9,11},{10,... | collective-permute-start | bytes 835592 | tf_op jit(solution)/shard_map/ppermute | solution.py:18
  35.9 12.2 %collective-permute-start.11 = (bf16[272,1024]{1,0:T(8,128)(2,1)}, bf16[272,1024]{1,0:T(8,128)(2,1)}, u32[]{:S(2)}, u32[]{:S(2)}) collective-permute-start(bf16[272,1024]{1,0:T(8,128)(2,1)} %slice.8), channel_id=1, source_target_pairs={{0,16},{8,24},{16,0},{24,8},{1,17},{9,25},{17,1},{25,9},{2,18},{10... | collective-permute-start | bytes 1671176 | tf_op jit(solution)/shard_map/ppermute | solution.py:18
  37.2 10.5 %collective-permute-start.12 = (bf16[240,1024]{1,0:T(8,128)(2,1)}, bf16[240,1024]{1,0:T(8,128)(2,1)}, u32[]{:S(2)}, u32[]{:S(2)}) collective-permute-start(bf16[240,1024]{1,0:T(8,128)(2,1)} %slice.9), channel_id=1, source_target_pairs={{0,8},{8,0},{16,24},{24,16},{1,9},{9,1},{17,25},{25,17},{2,10},{10... | collective-permute-start | bytes 1474568 | tf_op jit(solution)/shard_map/ppermute | solution.py:18
  38.1 1.7 %collective-permute-start.7 = (bf16[1088,128]{1,0:T(8,128)(2,1)S(1)}, bf16[1088,128]{1,0:T(8,128)(2,1)}, u32[]{:S(2)}, u32[]{:S(2)}) collective-permute-start(bf16[1088,128]{1,0:T(8,128)(2,1)S(1)} %collective-permute-done.4.refs_1_), channel_id=1, source_target_pairs={{0,1},{1,0},{2,3},{3,2},{4,5},{5,4},{6,7},{7,6},{8,9},{9,8},{10,11... | collective-permute-start | bytes 835592 | tf_op jit(solution)/shard_map/ppermute | solution.py:18
  38.1 2.3 %collective-permute-start.8 = (bf16[1088,128]{1,0:T(8,128)(2,1)}, bf16[1088,128]{1,0:T(8,128)(2,1)}, u32[]{:S(2)}, u32[]{:S(2)}) collective-permute-start(bf16[1088,128]{1,0:T(8,128)(2,1)} %collective-permute-done.5.refs_2_), channel_id=1, source_target_pairs={{0,1},{1,0},{2,3},{3,2},{4,5},{5,4},{6,7},{7,6},{8,9},{9,8},{10,11... | collective-permute-start | bytes 835592 | tf_op jit(solution)/shard_map/ppermute | solution.py:18
  38.8 9.2 %copy-start.1 = (bf16[2048,1024]{1,0:T(8,128)(2,1)S(1)}, bf16[2048,1024]{1,0:T(8,128)(2,1)}, u32[]{:S(2)}) copy-start(bf16[2048,1024]{1,0:T(8,128)(2,1)} %previous.1) | copy-start | bytes 12582916

commit v8 on v7

--- a/solution.py
+++ b/solution.py
@@ -132,11 +132,11 @@
             @pl.when((code >= 0) & (k >= early))
             def _():
                 to = pl.ds(pl.multiple_of(row * block, block), block)
-                late[k - early, to, :] = held[pl.ds(record, block), :]
+                late[k - early, to, :] = 2 * held[pl.ds(record, block), :]
 
         return carry
 
-    lax.fori_loop(0, count, place, 0, unroll=4)
+    lax.fori_loop(0, count, place, 0, unroll=True)
     for copy in second:
         copy.wait()
 
@@ -181,7 +181,7 @@
         rows = pl.ds(t * TILE, TILE)
         left = jnp.concatenate([late[k, rows, :] for k in range(blocks)], axis=1)
         product = jnp.dot(left, right, preferred_element_type=jnp.float32)
-        update = acc[rows, :] + 2.0 * product - previous[rows, :].astype(jnp.float32)
+        update = acc[rows, :] + product - previous[rows, :].astype(jnp.float32)
         for i in range(TILE // block):
             for j in range(out.shape[1] // block):
                 wanted = keep[t * (TILE // block) + i, j] > 0

time: 53.1 us -> 53.1 us (level)
  transfers between devices with their start and end apart: 13 -> 13, of which waited for: 8 -> 8; matrix products, arithmetic and copies ran while one was open for 7% -> 7% of each run, Pallas kernels for 14% -> 13%
where the time goes in v8:
time: 53.1 us; the launch traced here: 52.9 us
  waiting for transfers between devices  20.9 us (39%)
  starting transfers between devices  14.2 us (27%)
  Pallas kernels  11.9 us (22%)
  local copies, waits for them, and re-layouts  4.14 us (8%)
  other arithmetic  1.63 us (3%)
    ppermute x13, waiting for transfers between devices, swap(): return lax.ppermute(x, axis, [(i, i ^ offset) for i in range(size)])  20.9 us
    ppermute x13, starting transfers between devices, swap(): return lax.ppermute(x, axis, [(i, i ^ offset) for i in range(size)])  14.2 us
    pallas_call x1, Pallas kernels, per_device(): pl.pallas_call(functools.partial(early_kernel, dims, len(record_arrays),...  6.65 us
    pallas_call x1, Pallas kernels, per_device(): pl.pallas_call(functools.partial(late_kernel, dims), out_shape=jax.ShapeD...  4.84 us
    slice x2, local copies, waits for them, and re-layouts, per_device(): final = [swap(up[:at], 'row', 2), swap(down[at:], 'row', 1)]  1.66 us
    unnamed x10, local copies, waits for them, and re-layouts  1.31 us
  transfers between devices with their start and end apart: 13, of which 8 were waited for; matrix products, arithmetic and copies ran while one was open for 7% of the time, Pallas kernels for 13%

profile of v8, /device:TPU:0, one launch (start us, length us, event | category | flops | bytes accessed | tf_op | source)
XLA Modules:
  0.0 52.9 jit_solution(5851017416900826144)
XLA Ops:
  0.0 0.7 %fusion.4 = bf16[4,2]{0,1:T(2,128)(2,1)S(1)} fusion(s32[4,2]{0,1:T(2,128)} %param.9, s32[4]{0:T(128)} %bitcast.14), kind=kLoop, calls=%fused_computation.18 | loop fusion | flops 24 | bytes 64 | tf_op jit(solution)/shard_map/convert_element_type | solution.py:210
  0.7 1.0 %constant_dynamic-slice_fusion = (bf16[1,2,128,128]{3,2,1,0:T(8,128)(2,1)S(1)}, bf16[1,2,128,128]{3,2,1,0:T(8,128)(2,1)S(1)}, bf16[1,2,128,128]{3,2,1,0:T(8,128)(2,1)S(1)}, bf16[1,2,128,128]{3,2,1,0:T(8,128)(2,1)S(1)}) fusion(bf16[4,2,128,128]{3,2,1,0:T(8,128)(2,1)} %param.7, s32[]{:T(128)S(6)} %select_n.26, s32[]{:T(128)S(6)} %select_n.24, ...), kind=kLoop, calls=%fused_computation.13 | loop fusion | bytes 524304 | tf_op jit(solution)/shard_map/jit(dynamic_index_in_dim)/dynamic_slice | solution.py:217
  1.6 0.2 fusion.3
  1.9 3.0 %collective-permute-start = (bf16[272,128]{1,0:T(8,128)(2,1)S(1)}, bf16[272,128]{1,0:T(8,128)(2,1)S(1)}, u32[]{:S(2)}, u32[]{:S(2)}) collective-permute-start(bf16[272,128]{1,0:T(8,128)(2,1)S(1)} %pad_maximum_fusion.2), channel_id=1, source_target_pairs={{0,8},{8,0},{16,24},{24,16},{1,9},{9,1},{17,25},{25,17},{2,10},{10... | collective-permute-start | bytes 208904 | tf_op jit(solution)/shard_map/ppermute | solution.py:18
  4.9 1.6 %collective-permute-start.1 = (bf16[272,128]{1,0:T(8,128)(2,1)S(1)}, bf16[272,128]{1,0:T(8,128)(2,1)S(1)}, u32[]{:S(2)}, u32[]{:S(2)}) collective-permute-start(bf16[272,128]{1,0:T(8,128)(2,1)S(1)} %pad_maximum_fusion.3), channel_id=1, source_target_pairs={{0,16},{8,24},{16,0},{24,8},{1,17},{9,25},{17,1},{25,9},{2,18},{10... | collective-permute-start | bytes 208904 | tf_op jit(solution)/shard_map/ppermute | solution.py:18
  6.5 0.1 collective-permute-start.2
  6.6 1.2 %copy.11.refs_0_ = bf16[512,1024]{1,0:T(8,128)(2,1)S(1)} copy(bf16[512,1024]{1,0:T(8,128)(2,1)} %bitcast.8) | data formatting | bytes 2097152
  7.8 0.0 collective-permute-done.refs_1_
  7.8 1.5 %collective-permute-done.1.refs_2_ = bf16[272,128]{1,0:T(8,128)(2,1)S(1)} collective-permute-done((bf16[272,128]{1,0:T(8,128)(2,1)S(1)}, bf16[272,128]{1,0:T(8,128)(2,1)S(1)}, u32[]{:S(2)}, u32[]{:S(2)}) %collective-permute-start.1) | collective-permute-done | bytes 69664 | tf_op jit(solution)/shard_map/ppermute | solution.py:18
  9.3 2.5 %collective-permute-done.2.refs_3_ = bf16[272,128]{1,0:T(8,128)(2,1)S(1)} collective-permute-done((bf16[272,128]{1,0:T(8,128)(2,1)S(1)}, bf16[272,128]{1,0:T(8,128)(2,1)S(1)}, u32[]{:S(2)}, u32[]{:S(2)}) %collective-permute-start.2) | collective-permute-done | bytes 69664 | tf_op jit(solution)/shard_map/ppermute | solution.py:18
  11.8 0.6 %collective-permute-start.9 = (bf16[512,1024]{1,0:T(8,128)(2,1)S(1)}, bf16[512,1024]{1,0:T(8,128)(2,1)S(1)}, u32[]{:S(2)}, u32[]{:S(2)}) collective-permute-start(bf16[512,1024]{1,0:T(8,128)(2,1)S(1)} %hold.1), channel_id=1, source_target_pairs={{0,8},{8,0},{16,24},{24,16},{1,9},{9,1},{17,25},{25,17},{2,10},{10... | collective-permute-start | bytes 3145736 | tf_op jit(solution)/shard_map/ppermute | solution.py:18
  12.4 0.3 collective-permute-start.10
  12.7 0.4 join.1
  13.1 3.8 %collective-permute-start.3 = (bf16[1088,128]{1,0:T(8,128)(2,1)S(1)}, bf16[1088,128]{1,0:T(8,128)(2,1)S(1)}, u32[]{:S(2)}, u32[]{:S(2)}) collective-permute-start(bf16[1088,128]{1,0:T(8,128)(2,1)S(1)} %join.1), channel_id=1, source_target_pairs={{0,6},{1,7},{2,4},{3,5},{4,2},{5,3},{6,0},{7,1},{8,14},{9,15},{10,... | collective-permute-start | bytes 835592 | tf_op jit(solution)/shard_map/ppermute | solution.py:18
  17.0 7.6 %collective-permute-done.3 = bf16[1088,128]{1,0:T(8,128)(2,1)S(1)} collective-permute-done((bf16[1088,128]{1,0:T(8,128)(2,1)S(1)}, bf16[1088,128]{1,0:T(8,128)(2,1)S(1)}, u32[]{:S(2)}, u32[]{:S(2)}) %collective-permute-start.3) | collective-permute-done | bytes 278560 | tf_op jit(solution)/shard_map/ppermute | solution.py:18
  24.6 0.8 %pad_maximum_fusion.refs_0_ = bf16[2176,128]{1,0:T(8,128)(2,1)} fusion(bf16[1088,128]{1,0:T(8,128)(2,1)S(1)} %collective-permute-done.3, bf16[1088,128]{1,0:T(8,128)(2,1)S(1)} %join.1), kind=kLoop, calls=%fused_computation | loop fusion | flops 1114112 | bytes 1114112 | tf_op jit(solution)/shard_map/concatenate | solution.py:244
  25.4 2.8 %collective-permute-start.5 = (bf16[1088,128]{1,0:T(8,128)(2,1)S(1)}, bf16[1088,128]{1,0:T(8,128)(2,1)}, u32[]{:S(2)}, u32[]{:S(2)}) collective-permute-start(bf16[1088,128]{1,0:T(8,128)(2,1)S(1)} %collective-permute-done.3), channel_id=1, source_target_pairs={{0,2},{1,3},{2,0},{3,1},{4,6},{5,7},{6,4},{7,5},{8,10},{9,11},{10,... | collective-permute-start | bytes 835592 | tf_op jit(solution)/shard_map/ppermute | solution.py:18
  28.3 6.7 %collective-permute-done.9.refs_7_ = bf16[512,1024]{1,0:T(8,128)(2,1)S(1)} collective-permute-done((bf16[512,1024]{1,0:T(8,128)(2,1)S(1)}, bf16[512,1024]{1,0:T(8,128)(2,1)S(1)}, u32[]{:S(2)}, u32[]{:S(2)}) %collective-permute-start.9) | collective-permute-done | bytes 1048608 | tf_op jit(solution)/shard_map/ppermute | solution.py:18
  35.0 0.8 %slice.8 = bf16[272,1024]{1,0:T(8,128)(2,1)} slice(bf16[512,1024]{1,0:T(8,128)(2,1)S(1)} %collective-permute-done.9.refs_7_), slice={[0:272], [0:1024]} | slice | bytes 1114112 | tf_op jit(solution)/shard_map/slice | solution.py:233
  35.9 0.6 %collective-permute-start.11 = (bf16[272,1024]{1,0:T(8,128)(2,1)}, bf16[272,1024]{1,0:T(8,128)(2,1)}, u32[]{:S(2)}, u32[]{:S(2)}) collective-permute-start(bf16[272,1024]{1,0:T(8,128)(2,1)} %slice.8), channel_id=1, source_target_pairs={{0,16},{8,24},{16,0},{24,8},{1,17},{9,25},{17,1},{25,9},{2,18},{10... | collective-permute-start | bytes 1671176 | tf_op jit(solution)/shard_map/ppermute | solution.py:18
  36.4 0.0 collective-permute-done.10.refs_8_
  36.4 0.8 %slice.9 = bf16[240,1024]{1,0:T(8,128)(2,1)} slice(bf16[512,1024]{1,0:T(8,128)(2,1)S(1)} %collective-permute-done.10.refs_8_), slice={[272:512], [0:1024]} | slice | bytes 983040 | tf_op jit(solution)/shard_map/slice | solution.py:233
  37.2 0.9 %collective-permute-start.12 = (bf16[240,1024]{1,0:T(8,128)(2,1)}, bf16[240,1024]{1,0:T(8,128)(2,1)}, u32[]{:S(2)}, u32[]{:S(2)}) collective-permute-start(bf16[240,1024]{1,0:T(8,128)(2,1)} %slice.9), channel_id=1, source_target_pairs={{0,8},{8,0},{16,24},{24,16},{1,9},{9,1},{17,25},{25,17},{2,10},{10... | collective-permute-start | bytes 1474568 | tf_op jit(solution)/shard_map/ppermute | solution.py:18
  38.1 0.5 collective-permute-start.8
  38.6 0.1 copy.10.keep
  38.7 0.1 pad_add_fusion.spot
  38.8 1.0 %collective-permute-done.7.refs_4_ = bf16[1088,128]{1,0:T(8,128)(2,1)} collective-permute-done((bf16[1088,128]{1,0:T(8,128)(2,1)S(1)}, bf16[1088,128]{1,0:T(8,128)(2,1)}, u32[]{:S(2)}, u32[]{:S(2)}) %collective-permute-start.7) | collective-permute-done | bytes 278560 | tf_op jit(solution)/shard_map/ppermute | solution.py:18
  39.8 0.6 %collective-permute-done.8.refs_5_ = bf16[1088,128]{1,0:T(8,128)(2,1)} collective-permute-done((bf16[1088,128]{1,0:T(8,128)(2,1)}, bf16[1088,128]{1,0:T(8,128)(2,1)}, u32[]{:S(2)}, u32[]{:S(2)}) %collective-permute-start.8) | collective-permute-done | bytes 278560 | tf_op jit(solution)/shard_map/ppermute | solution.py:18
  40.4 6.7 %early_product.1 = (f32[2048,1024]{1,0:T(8,128)S(1)}, bf16[4,2048,128]{2,1,0:T(8,128)(2,1)S(1)}) custom-call(s32[2]{0:T(128)S(1)} %pad_add_fusion.spot, s32[8]{0:T(128)S(1)} %copy-done.2, bf16[2176,128]{1,0:T(8,128)(2,1)} %pad_maximum_fusion.refs_0_, bf16[1088,128]{1,0:T(8,128)(2,1)S(1)} %collective-permute-done.4.refs_1_, ...), custom_call_target="tpu_custom_call" | custom-call | tf_op jit(solution)/shard_map/early_product/pallas_call | solution.py:263
  47.1 0.7 %collective-permute-done.12.refs_1_ = bf16[240,1024]{1,0:T(8,128)(2,1)} collective-permute-done((bf16[240,1024]{1,0:T(8,128)(2,1)}, bf16[240,1024]{1,0:T(8,128)(2,1)}, u32[]{:S(2)}, u32[]{:S(2)}) %collective-permute-start.12) | collective-permute-done | bytes 491552 | tf_op jit(solution)/shard_map/ppermute | solution.py:18
  47.8 0.2 collective-permute-done.11.refs_0_
  48.0 4.8 %late_product.1 = bf16[2048,1024]{1,0:T(8,128)(2,1)} custom-call(s32[16,8]{1,0:T(8,128)S(1)} %copy.10.keep, f32[2048,1024]{1,0:T(8,128)S(1)} %get-tuple-element.7.acc, bf16[4,2048,128]{2,1,0:T(8,128)(2,1)S(1)} %get-tuple-element.8.late, bf16[2048,1024]{1,0:T(8,128)(2,1)S(1)} %copy-done.1, bf16[272,1024]{1,0:T(8,128)(2,1)} %collective-permute-done.11.refs_0_, ...), custom_call_target="tpu_custom_call" | custom-call | tf_op jit(solution)/shard_map/late_product/pallas_call | solution.py:289
  (23 shorter events, 0.1 us)
Async XLA Ops:
  1.9 5.9 %collective-permute-start = (bf16[272,128]{1,0:T(8,128)(2,1)S(1)}, bf16[272,128]{1,0:T(8,128)(2,1)S(1)}, u32[]{:S(2)}, u32[]{:S(2)}) collective-permute-start(bf16[272,128]{1,0:T(8,128)(2,1)S(1)} %pad_maximum_fusion.2), channel_id=1, source_target_pairs={{0,8},{8,0},{16,24},{24,16},{1,9},{9,1},{17,25},{25,17},{2,10},{10... | collective-permute-start | bytes 208904 | tf_op jit(solution)/shard_map/ppermute | solution.py:18
  4.9 4.4 %collective-permute-start.1 = (bf16[272,128]{1,0:T(8,128)(2,1)S(1)}, bf16[272,128]{1,0:T(8,128)(2,1)S(1)}, u32[]{:S(2)}, u32[]{:S(2)}) collective-permute-start(bf16[272,128]{1,0:T(8,128)(2,1)S(1)} %pad_maximum_fusion.3), channel_id=1, source_target_pairs={{0,16},{8,24},{16,0},{24,8},{1,17},{9,25},{17,1},{25,9},{2,18},{10... | collective-permute-start | bytes 208904 | tf_op jit(solution)/shard_map/ppermute | solution.py:18
  6.5 5.3 %collective-permute-start.2 = (bf16[272,128]{1,0:T(8,128)(2,1)S(1)}, bf16[272,128]{1,0:T(8,128)(2,1)S(1)}, u32[]{:S(2)}, u32[]{:S(2)}) collective-permute-start(bf16[272,128]{1,0:T(8,128)(2,1)S(1)} %pad_maximum_fusion.4), channel_id=1, source_target_pairs={{0,24},{8,16},{16,8},{24,0},{1,25},{9,17},{17,9},{25,1},{2,26},{10... | collective-permute-start | bytes 208904 | tf_op jit(solution)/shard_map/ppermute | solution.py:18
  11.8 26.9 %copy-start.3 = (s32[16,8]{0,1:T(8,128)S(1)}, s32[16,8]{0,1:T(8,128)}, u32[]{:S(2)}) copy-start(s32[16,8]{0,1:T(8,128)} %param.12) | copy-start | bytes 1540
  11.8 28.7 %copy-start = (bf16[2,256,1024]{2,1,0:T(8,128)(2,1)S(1)}, bf16[2,256,1024]{2,1,0:T(8,128)(2,1)}, u32[]{:S(2)}) copy-start(bf16[2,256,1024]{2,1,0:T(8,128)(2,1)} %param.10) | copy-start | bytes 3145732
  11.8 28.7 %copy-start.2 = (s32[8]{0:T(128)S(1)}, s32[8]{0:T(128)}, u32[]{:S(2)}) copy-start(s32[8]{0:T(128)} %constant.44.clone.offsets) | copy-start | bytes 100
  11.8 23.2 %collective-permute-start.9 = (bf16[512,1024]{1,0:T(8,128)(2,1)S(1)}, bf16[512,1024]{1,0:T(8,128)(2,1)S(1)}, u32[]{:S(2)}, u32[]{:S(2)}) collective-permute-start(bf16[512,1024]{1,0:T(8,128)(2,1)S(1)} %hold.1), channel_id=1, source_target_pairs={{0,8},{8,0},{16,24},{24,16},{1,9},{9,1},{17,25},{25,17},{2,10},{10... | collective-permute-start | bytes 3145736 | tf_op jit(solution)/shard_map/ppermute | solution.py:18
  12.4 24.1 %collective-permute-start.10 = (bf16[512,1024]{1,0:T(8,128)(2,1)S(1)}, bf16[512,1024]{1,0:T(8,128)(2,1)S(1)}, u32[]{:S(2)}, u32[]{:S(2)}) collective-permute-start(bf16[512,1024]{1,0:T(8,128)(2,1)S(1)} %hold.1), channel_id=1, source_target_pairs={{0,16},{8,24},{16,0},{24,8},{1,17},{9,25},{17,1},{25,9},{2,18},{10... | collective-permute-start | bytes 3145736 | tf_op jit(solution)/shard_map/ppermute | solution.py:18
  13.1 11.5 %collective-permute-start.3 = (bf16[1088,128]{1,0:T(8,128)(2,1)S(1)}, bf16[1088,128]{1,0:T(8,128)(2,1)S(1)}, u32[]{:S(2)}, u32[]{:S(2)}) collective-permute-start(bf16[1088,128]{1,0:T(8,128)(2,1)S(1)} %join.1), channel_id=1, source_target_pairs={{0,6},{1,7},{2,4},{3,5},{4,2},{5,3},{6,0},{7,1},{8,14},{9,15},{10,... | collective-permute-start | bytes 835592 | tf_op jit(solution)/shard_map/ppermute | solution.py:18
  17.0 21.2 %collective-permute-start.4 = (bf16[1088,128]{1,0:T(8,128)(2,1)S(1)}, bf16[1088,128]{1,0:T(8,128)(2,1)S(1)}, u32[]{:S(2)}, u32[]{:S(2)}) collective-permute-start(bf16[1088,128]{1,0:T(8,128)(2,1)S(1)} %join.1), channel_id=1, source_target_pairs={{0,2},{1,3},{2,0},{3,1},{4,6},{5,7},{6,4},{7,5},{8,10},{9,11},{10,... | collective-permute-start | bytes 835592 | tf_op jit(solution)/shard_map/ppermute | solution.py:18
  25.4 14.4 %collective-permute-start.6 = (bf16[2176,128]{1,0:T(8,128)(2,1)}, bf16[2176,128]{1,0:T(8,128)(2,1)}, u32[]{:S(2)}, u32[]{:S(2)}) collective-permute-start(bf16[2176,128]{1,0:T(8,128)(2,1)} %pad_maximum_fusion.refs_0_), channel_id=1, source_target_pairs={{0,1},{1,0},{2,3},{3,2},{4,5},{5,4},{6,7},{7,6},{8,9},{9,8},{10,11... | collective-permute-start | bytes 1671176 | tf_op jit(solution)/shard_map/ppermute | solution.py:18
  25.4 12.7 %collective-permute-start.5 = (bf16[1088,128]{1,0:T(8,128)(2,1)S(1)}, bf16[1088,128]{1,0:T(8,128)(2,1)}, u32[]{:S(2)}, u32[]{:S(2)}) collective-permute-start(bf16[1088,128]{1,0:T(8,128)(2,1)S(1)} %collective-permute-done.3), channel_id=1, source_target_pairs={{0,2},{1,3},{2,0},{3,1},{4,6},{5,7},{6,4},{7,5},{8,10},{9,11},{10,... | collective-permute-start | bytes 835592 | tf_op jit(solution)/shard_map/ppermute | solution.py:18
  35.9 12.2 %collective-permute-start.11 = (bf16[272,1024]{1,0:T(8,128)(2,1)}, bf16[272,1024]{1,0:T(8,128)(2,1)}, u32[]{:S(2)}, u32[]{:S(2)}) collective-permute-start(bf16[272,1024]{1,0:T(8,128)(2,1)} %slice.8), channel_id=1, source_target_pairs={{0,16},{8,24},{16,0},{24,8},{1,17},{9,25},{17,1},{25,9},{2,18},{10... | collective-permute-start | bytes 1671176 | tf_op jit(solution)/shard_map/ppermute | solution.py:18
  37.2 10.5 %collective-permute-start.12 = (bf16[240,1024]{1,0:T(8,128)(2,1)}, bf16[240,1024]{1,0:T(8,128)(2,1)}, u32[]{:S(2)}, u32[]{:S(2)}) collective-permute-start(bf16[240,1024]{1,0:T(8,128)(2,1)} %slice.9), channel_id=1, source_target_pairs={{0,8},{8,0},{16,24},{24,16},{1,9},{9,1},{17,25},{25,17},{2,10},{10... | collective-permute-start | bytes 1474568 | tf_op jit(solution)/shard_map/ppermute | solution.py:18
  38.1 1.7 %collective-permute-start.7 = (bf16[1088,128]{1,0:T(8,128)(2,1)S(1)}, bf16[1088,128]{1,0:T(8,128)(2,1)}, u32[]{:S(2)}, u32[]{:S(2)}) collective-permute-start(bf16[1088,128]{1,0:T(8,128)(2,1)S(1)} %collective-permute-done.4.refs_1_), channel_id=1, source_target_pairs={{0,1},{1,0},{2,3},{3,2},{4,5},{5,4},{6,7},{7,6},{8,9},{9,8},{10,11... | collective-permute-start | bytes 835592 | tf_op jit(solution)/shard_map/ppermute | solution.py:18
  38.1 2.3 %collective-permute-start.8 = (bf16[1088,128]{1,0:T(8,128)(2,1)}, bf16[1088,128]{1,0:T(8,128)(2,1)}, u32[]{:S(2)}, u32[]{:S(2)}) collective-permute-start(bf16[1088,128]{1,0:T(8,128)(2,1)} %collective-permute-done.5.refs_2_), channel_id=1, source_target_pairs={{0,1},{1,0},{2,3},{3,2},{4,5},{5,4},{6,7},{7,6},{8,9},{9,8},{10,11... | collective-permute-start | bytes 835592 | tf_op jit(solution)/shard_map/ppermute | solution.py:18
  38.8 9.2 %copy-start.1 = (bf16[2048,1024]{1,0:T(8,128)(2,1)S(1)}, bf16[2048,1024]{1,0:T(8,128)(2,1)}, u32[]{:S(2)}) copy-start(bf16[2048,1024]{1,0:T(8,128)(2,1)} %previous.1) | copy-start | bytes 12582916

commit v9 on v8

--- a/solution.py
+++ b/solution.py
@@ -174,19 +174,21 @@
     block = dims[-1]
     term_refs, out, staged, sem = refs[:-3], *refs[-3:]
     blocks = late.shape[0]
-    steps = acc.shape[0] // TILE
+    whole = acc.shape[0] // TILE - 1
+    tiles = [(t * TILE, TILE) for t in range(whole)]
+    tiles += [(whole * TILE + i * block, block) for i in range(TILE // block)]
     right = jnp.concatenate([ref[...] for ref in term_refs], axis=0)
     copies = []
-    for t in range(steps):
-        rows = pl.ds(t * TILE, TILE)
+    for start, size in tiles:
+        rows = pl.ds(start, size)
         left = jnp.concatenate([late[k, rows, :] for k in range(blocks)], axis=1)
         product = jnp.dot(left, right, preferred_element_type=jnp.float32)
         update = acc[rows, :] + product - previous[rows, :].astype(jnp.float32)
-        for i in range(TILE // block):
+        for i in range(size // block):
             for j in range(out.shape[1] // block):
-                wanted = keep[t * (TILE // block) + i, j] > 0
+                wanted = keep[start // block + i, j] > 0
                 part = update[i * block : (i + 1) * block, j * block : (j + 1) * block]
-                staged[pl.ds(t * TILE + i * block, block), pl.ds(j * block, block)] = jnp.where(
+                staged[pl.ds(start + i * block, block), pl.ds(j * block, block)] = jnp.where(
                     wanted, part, jnp.zeros_like(part)
                 ).astype(out.dtype)
         copies.append(pltpu.make_async_copy(staged.at[rows], out.at[rows], sem))

time: 53.1 us -> 53.1 us (level)
  no operation moved by 1% of the time
where the time goes in v9:
time: 53.1 us; the launch traced here: 52.8 us
  waiting for transfers between devices  20.9 us (39%)
  starting transfers between devices  14.2 us (27%)
  Pallas kernels  11.8 us (22%)
  local copies, waits for them, and re-layouts  4.14 us (8%)
  other arithmetic  1.63 us (3%)
    ppermute x13, waiting for transfers between devices, swap(): return lax.ppermute(x, axis, [(i, i ^ offset) for i in range(size)])  20.9 us
    ppermute x13, starting transfers between devices, swap(): return lax.ppermute(x, axis, [(i, i ^ offset) for i in range(size)])  14.2 us
    pallas_call x1, Pallas kernels, per_device(): pl.pallas_call(functools.partial(early_kernel, dims, len(record_arrays),...  6.66 us
    pallas_call x1, Pallas kernels, per_device(): pl.pallas_call(functools.partial(late_kernel, dims), out_shape=jax.ShapeD...  4.78 us
    slice x2, local copies, waits for them, and re-layouts, per_device(): final = [swap(up[:at], 'row', 2), swap(down[at:], 'row', 1)]  1.66 us
    unnamed x10, local copies, waits for them, and re-layouts  1.31 us
  transfers between devices with their start and end apart: 13, of which 8 were waited for; matrix products, arithmetic and copies ran while one was open for 7% of the time, Pallas kernels for 13%

profile of v9, /device:TPU:0, one launch (start us, length us, event | category | flops | bytes accessed | tf_op | source)
XLA Modules:
  0.0 52.8 jit_solution(13502047146520045974)
XLA Ops:
  0.0 0.7 %fusion.4 = bf16[4,2]{0,1:T(2,128)(2,1)S(1)} fusion(s32[4,2]{0,1:T(2,128)} %param.9, s32[4]{0:T(128)} %bitcast.14), kind=kLoop, calls=%fused_computation.18 | loop fusion | flops 24 | bytes 64 | tf_op jit(solution)/shard_map/convert_element_type | solution.py:212
  0.7 1.0 %constant_dynamic-slice_fusion = (bf16[1,2,128,128]{3,2,1,0:T(8,128)(2,1)S(1)}, bf16[1,2,128,128]{3,2,1,0:T(8,128)(2,1)S(1)}, bf16[1,2,128,128]{3,2,1,0:T(8,128)(2,1)S(1)}, bf16[1,2,128,128]{3,2,1,0:T(8,128)(2,1)S(1)}) fusion(bf16[4,2,128,128]{3,2,1,0:T(8,128)(2,1)} %param.7, s32[]{:T(128)S(6)} %select_n.26, s32[]{:T(128)S(6)} %select_n.24, ...), kind=kLoop, calls=%fused_computation.13 | loop fusion | bytes 524304 | tf_op jit(solution)/shard_map/jit(dynamic_index_in_dim)/dynamic_slice | solution.py:219
  1.6 0.2 fusion.3
  1.9 3.0 %collective-permute-start = (bf16[272,128]{1,0:T(8,128)(2,1)S(1)}, bf16[272,128]{1,0:T(8,128)(2,1)S(1)}, u32[]{:S(2)}, u32[]{:S(2)}) collective-permute-start(bf16[272,128]{1,0:T(8,128)(2,1)S(1)} %pad_maximum_fusion.2), channel_id=1, source_target_pairs={{0,8},{8,0},{16,24},{24,16},{1,9},{9,1},{17,25},{25,17},{2,10},{10... | collective-permute-start | bytes 208904 | tf_op jit(solution)/shard_map/ppermute | solution.py:18
  4.9 1.6 %collective-permute-start.1 = (bf16[272,128]{1,0:T(8,128)(2,1)S(1)}, bf16[272,128]{1,0:T(8,128)(2,1)S(1)}, u32[]{:S(2)}, u32[]{:S(2)}) collective-permute-start(bf16[272,128]{1,0:T(8,128)(2,1)S(1)} %pad_maximum_fusion.3), channel_id=1, source_target_pairs={{0,16},{8,24},{16,0},{24,8},{1,17},{9,25},{17,1},{25,9},{2,18},{10... | collective-permute-start | bytes 208904 | tf_op jit(solution)/shard_map/ppermute | solution.py:18
  6.5 0.1 collective-permute-start.2
  6.6 1.2 %copy.11.refs_0_ = bf16[512,1024]{1,0:T(8,128)(2,1)S(1)} copy(bf16[512,1024]{1,0:T(8,128)(2,1)} %bitcast.8) | data formatting | bytes 2097152
  7.8 0.0 collective-permute-done.refs_1_
  7.8 1.5 %collective-permute-done.1.refs_2_ = bf16[272,128]{1,0:T(8,128)(2,1)S(1)} collective-permute-done((bf16[272,128]{1,0:T(8,128)(2,1)S(1)}, bf16[272,128]{1,0:T(8,128)(2,1)S(1)}, u32[]{:S(2)}, u32[]{:S(2)}) %collective-permute-start.1) | collective-permute-done | bytes 69664 | tf_op jit(solution)/shard_map/ppermute | solution.py:18
  9.3 2.5 %collective-permute-done.2.refs_3_ = bf16[272,128]{1,0:T(8,128)(2,1)S(1)} collective-permute-done((bf16[272,128]{1,0:T(8,128)(2,1)S(1)}, bf16[272,128]{1,0:T(8,128)(2,1)S(1)}, u32[]{:S(2)}, u32[]{:S(2)}) %collective-permute-start.2) | collective-permute-done | bytes 69664 | tf_op jit(solution)/shard_map/ppermute | solution.py:18
  11.8 0.6 %collective-permute-start.9 = (bf16[512,1024]{1,0:T(8,128)(2,1)S(1)}, bf16[512,1024]{1,0:T(8,128)(2,1)S(1)}, u32[]{:S(2)}, u32[]{:S(2)}) collective-permute-start(bf16[512,1024]{1,0:T(8,128)(2,1)S(1)} %hold.1), channel_id=1, source_target_pairs={{0,8},{8,0},{16,24},{24,16},{1,9},{9,1},{17,25},{25,17},{2,10},{10... | collective-permute-start | bytes 3145736 | tf_op jit(solution)/shard_map/ppermute | solution.py:18
  12.4 0.3 collective-permute-start.10
  12.7 0.4 join.1
  13.1 3.8 %collective-permute-start.3 = (bf16[1088,128]{1,0:T(8,128)(2,1)S(1)}, bf16[1088,128]{1,0:T(8,128)(2,1)S(1)}, u32[]{:S(2)}, u32[]{:S(2)}) collective-permute-start(bf16[1088,128]{1,0:T(8,128)(2,1)S(1)} %join.1), channel_id=1, source_target_pairs={{0,6},{1,7},{2,4},{3,5},{4,2},{5,3},{6,0},{7,1},{8,14},{9,15},{10,... | collective-permute-start | bytes 835592 | tf_op jit(solution)/shard_map/ppermute | solution.py:18
  17.0 0.0 collective-permute-start.4
  17.0 7.6 %collective-permute-done.3 = bf16[1088,128]{1,0:T(8,128)(2,1)S(1)} collective-permute-done((bf16[1088,128]{1,0:T(8,128)(2,1)S(1)}, bf16[1088,128]{1,0:T(8,128)(2,1)S(1)}, u32[]{:S(2)}, u32[]{:S(2)}) %collective-permute-start.3) | collective-permute-done | bytes 278560 | tf_op jit(solution)/shard_map/ppermute | solution.py:18
  24.6 0.8 %pad_maximum_fusion.refs_0_ = bf16[2176,128]{1,0:T(8,128)(2,1)} fusion(bf16[1088,128]{1,0:T(8,128)(2,1)S(1)} %collective-permute-done.3, bf16[1088,128]{1,0:T(8,128)(2,1)S(1)} %join.1), kind=kLoop, calls=%fused_computation | loop fusion | flops 1114112 | bytes 1114112 | tf_op jit(solution)/shard_map/concatenate | solution.py:246
  25.4 2.8 %collective-permute-start.5 = (bf16[1088,128]{1,0:T(8,128)(2,1)S(1)}, bf16[1088,128]{1,0:T(8,128)(2,1)}, u32[]{:S(2)}, u32[]{:S(2)}) collective-permute-start(bf16[1088,128]{1,0:T(8,128)(2,1)S(1)} %collective-permute-done.3), channel_id=1, source_target_pairs={{0,2},{1,3},{2,0},{3,1},{4,6},{5,7},{6,4},{7,5},{8,10},{9,11},{10,... | collective-permute-start | bytes 835592 | tf_op jit(solution)/shard_map/ppermute | solution.py:18
  28.3 6.7 %collective-permute-done.9.refs_7_ = bf16[512,1024]{1,0:T(8,128)(2,1)S(1)} collective-permute-done((bf16[512,1024]{1,0:T(8,128)(2,1)S(1)}, bf16[512,1024]{1,0:T(8,128)(2,1)S(1)}, u32[]{:S(2)}, u32[]{:S(2)}) %collective-permute-start.9) | collective-permute-done | bytes 1048608 | tf_op jit(solution)/shard_map/ppermute | solution.py:18
  35.0 0.8 %slice.8 = bf16[272,1024]{1,0:T(8,128)(2,1)} slice(bf16[512,1024]{1,0:T(8,128)(2,1)S(1)} %collective-permute-done.9.refs_7_), slice={[0:272], [0:1024]} | slice | bytes 1114112 | tf_op jit(solution)/shard_map/slice | solution.py:235
  35.9 0.6 %collective-permute-start.11 = (bf16[272,1024]{1,0:T(8,128)(2,1)}, bf16[272,1024]{1,0:T(8,128)(2,1)}, u32[]{:S(2)}, u32[]{:S(2)}) collective-permute-start(bf16[272,1024]{1,0:T(8,128)(2,1)} %slice.8), channel_id=1, source_target_pairs={{0,16},{8,24},{16,0},{24,8},{1,17},{9,25},{17,1},{25,9},{2,18},{10... | collective-permute-start | bytes 1671176 | tf_op jit(solution)/shard_map/ppermute | solution.py:18
  36.4 0.8 %slice.9 = bf16[240,1024]{1,0:T(8,128)(2,1)} slice(bf16[512,1024]{1,0:T(8,128)(2,1)S(1)} %collective-permute-done.10.refs_8_), slice={[272:512], [0:1024]} | slice | bytes 983040 | tf_op jit(solution)/shard_map/slice | solution.py:235
  37.2 0.9 %collective-permute-start.12 = (bf16[240,1024]{1,0:T(8,128)(2,1)}, bf16[240,1024]{1,0:T(8,128)(2,1)}, u32[]{:S(2)}, u32[]{:S(2)}) collective-permute-start(bf16[240,1024]{1,0:T(8,128)(2,1)} %slice.9), channel_id=1, source_target_pairs={{0,8},{8,0},{16,24},{24,16},{1,9},{9,1},{17,25},{25,17},{2,10},{10... | collective-permute-start | bytes 1474568 | tf_op jit(solution)/shard_map/ppermute | solution.py:18
  38.1 0.5 collective-permute-start.8
  38.6 0.1 copy.10.keep
  38.7 0.1 pad_add_fusion.spot
  38.8 1.0 %collective-permute-done.7.refs_4_ = bf16[1088,128]{1,0:T(8,128)(2,1)} collective-permute-done((bf16[1088,128]{1,0:T(8,128)(2,1)S(1)}, bf16[1088,128]{1,0:T(8,128)(2,1)}, u32[]{:S(2)}, u32[]{:S(2)}) %collective-permute-start.7) | collective-permute-done | bytes 278560 | tf_op jit(solution)/shard_map/ppermute | solution.py:18
  39.8 0.6 %collective-permute-done.8.refs_5_ = bf16[1088,128]{1,0:T(8,128)(2,1)} collective-permute-done((bf16[1088,128]{1,0:T(8,128)(2,1)}, bf16[1088,128]{1,0:T(8,128)(2,1)}, u32[]{:S(2)}, u32[]{:S(2)}) %collective-permute-start.8) | collective-permute-done | bytes 278560 | tf_op jit(solution)/shard_map/ppermute | solution.py:18
  40.4 6.7 %early_product.1 = (f32[2048,1024]{1,0:T(8,128)S(1)}, bf16[4,2048,128]{2,1,0:T(8,128)(2,1)S(1)}) custom-call(s32[2]{0:T(128)S(1)} %pad_add_fusion.spot, s32[8]{0:T(128)S(1)} %copy-done.2, bf16[2176,128]{1,0:T(8,128)(2,1)} %pad_maximum_fusion.refs_0_, bf16[1088,128]{1,0:T(8,128)(2,1)S(1)} %collective-permute-done.4.refs_1_, ...), custom_call_target="tpu_custom_call" | custom-call | tf_op jit(solution)/shard_map/early_product/pallas_call | solution.py:265
  47.1 0.7 %collective-permute-done.12.refs_1_ = bf16[240,1024]{1,0:T(8,128)(2,1)} collective-permute-done((bf16[240,1024]{1,0:T(8,128)(2,1)}, bf16[240,1024]{1,0:T(8,128)(2,1)}, u32[]{:S(2)}, u32[]{:S(2)}) %collective-permute-start.12) | collective-permute-done | bytes 491552 | tf_op jit(solution)/shard_map/ppermute | solution.py:18
  47.8 0.2 collective-permute-done.11.refs_0_
  48.0 4.8 %late_product.1 = bf16[2048,1024]{1,0:T(8,128)(2,1)} custom-call(s32[16,8]{1,0:T(8,128)S(1)} %copy.10.keep, f32[2048,1024]{1,0:T(8,128)S(1)} %get-tuple-element.7.acc, bf16[4,2048,128]{2,1,0:T(8,128)(2,1)S(1)} %get-tuple-element.8.late, bf16[2048,1024]{1,0:T(8,128)(2,1)S(1)} %copy-done.1, bf16[272,1024]{1,0:T(8,128)(2,1)} %collective-permute-done.11.refs_0_, ...), custom_call_target="tpu_custom_call" | custom-call | tf_op jit(solution)/shard_map/late_product/pallas_call | solution.py:291
  (23 shorter events, 0.1 us)
Async XLA Ops:
  1.9 5.9 %collective-permute-start = (bf16[272,128]{1,0:T(8,128)(2,1)S(1)}, bf16[272,128]{1,0:T(8,128)(2,1)S(1)}, u32[]{:S(2)}, u32[]{:S(2)}) collective-permute-start(bf16[272,128]{1,0:T(8,128)(2,1)S(1)} %pad_maximum_fusion.2), channel_id=1, source_target_pairs={{0,8},{8,0},{16,24},{24,16},{1,9},{9,1},{17,25},{25,17},{2,10},{10... | collective-permute-start | bytes 208904 | tf_op jit(solution)/shard_map/ppermute | solution.py:18
  4.9 4.4 %collective-permute-start.1 = (bf16[272,128]{1,0:T(8,128)(2,1)S(1)}, bf16[272,128]{1,0:T(8,128)(2,1)S(1)}, u32[]{:S(2)}, u32[]{:S(2)}) collective-permute-start(bf16[272,128]{1,0:T(8,128)(2,1)S(1)} %pad_maximum_fusion.3), channel_id=1, source_target_pairs={{0,16},{8,24},{16,0},{24,8},{1,17},{9,25},{17,1},{25,9},{2,18},{10... | collective-permute-start | bytes 208904 | tf_op jit(solution)/shard_map/ppermute | solution.py:18
  6.5 5.3 %collective-permute-start.2 = (bf16[272,128]{1,0:T(8,128)(2,1)S(1)}, bf16[272,128]{1,0:T(8,128)(2,1)S(1)}, u32[]{:S(2)}, u32[]{:S(2)}) collective-permute-start(bf16[272,128]{1,0:T(8,128)(2,1)S(1)} %pad_maximum_fusion.4), channel_id=1, source_target_pairs={{0,24},{8,16},{16,8},{24,0},{1,25},{9,17},{17,9},{25,1},{2,26},{10... | collective-permute-start | bytes 208904 | tf_op jit(solution)/shard_map/ppermute | solution.py:18
  11.8 26.9 %copy-start.3 = (s32[16,8]{0,1:T(8,128)S(1)}, s32[16,8]{0,1:T(8,128)}, u32[]{:S(2)}) copy-start(s32[16,8]{0,1:T(8,128)} %param.12) | copy-start | bytes 1540
  11.8 28.7 %copy-start = (bf16[2,256,1024]{2,1,0:T(8,128)(2,1)S(1)}, bf16[2,256,1024]{2,1,0:T(8,128)(2,1)}, u32[]{:S(2)}) copy-start(bf16[2,256,1024]{2,1,0:T(8,128)(2,1)} %param.10) | copy-start | bytes 3145732
  11.8 28.7 %copy-start.2 = (s32[8]{0:T(128)S(1)}, s32[8]{0:T(128)}, u32[]{:S(2)}) copy-start(s32[8]{0:T(128)} %constant.44.clone.offsets) | copy-start | bytes 100
  11.8 23.2 %collective-permute-start.9 = (bf16[512,1024]{1,0:T(8,128)(2,1)S(1)}, bf16[512,1024]{1,0:T(8,128)(2,1)S(1)}, u32[]{:S(2)}, u32[]{:S(2)}) collective-permute-start(bf16[512,1024]{1,0:T(8,128)(2,1)S(1)} %hold.1), channel_id=1, source_target_pairs={{0,8},{8,0},{16,24},{24,16},{1,9},{9,1},{17,25},{25,17},{2,10},{10... | collective-permute-start | bytes 3145736 | tf_op jit(solution)/shard_map/ppermute | solution.py:18
  12.4 24.1 %collective-permute-start.10 = (bf16[512,1024]{1,0:T(8,128)(2,1)S(1)}, bf16[512,1024]{1,0:T(8,128)(2,1)S(1)}, u32[]{:S(2)}, u32[]{:S(2)}) collective-permute-start(bf16[512,1024]{1,0:T(8,128)(2,1)S(1)} %hold.1), channel_id=1, source_target_pairs={{0,16},{8,24},{16,0},{24,8},{1,17},{9,25},{17,1},{25,9},{2,18},{10... | collective-permute-start | bytes 3145736 | tf_op jit(solution)/shard_map/ppermute | solution.py:18
  13.1 11.5 %collective-permute-start.3 = (bf16[1088,128]{1,0:T(8,128)(2,1)S(1)}, bf16[1088,128]{1,0:T(8,128)(2,1)S(1)}, u32[]{:S(2)}, u32[]{:S(2)}) collective-permute-start(bf16[1088,128]{1,0:T(8,128)(2,1)S(1)} %join.1), channel_id=1, source_target_pairs={{0,6},{1,7},{2,4},{3,5},{4,2},{5,3},{6,0},{7,1},{8,14},{9,15},{10,... | collective-permute-start | bytes 835592 | tf_op jit(solution)/shard_map/ppermute | solution.py:18
  17.0 21.2 %collective-permute-start.4 = (bf16[1088,128]{1,0:T(8,128)(2,1)S(1)}, bf16[1088,128]{1,0:T(8,128)(2,1)S(1)}, u32[]{:S(2)}, u32[]{:S(2)}) collective-permute-start(bf16[1088,128]{1,0:T(8,128)(2,1)S(1)} %join.1), channel_id=1, source_target_pairs={{0,2},{1,3},{2,0},{3,1},{4,6},{5,7},{6,4},{7,5},{8,10},{9,11},{10,... | collective-permute-start | bytes 835592 | tf_op jit(solution)/shard_map/ppermute | solution.py:18
  25.4 14.4 %collective-permute-start.6 = (bf16[2176,128]{1,0:T(8,128)(2,1)}, bf16[2176,128]{1,0:T(8,128)(2,1)}, u32[]{:S(2)}, u32[]{:S(2)}) collective-permute-start(bf16[2176,128]{1,0:T(8,128)(2,1)} %pad_maximum_fusion.refs_0_), channel_id=1, source_target_pairs={{0,1},{1,0},{2,3},{3,2},{4,5},{5,4},{6,7},{7,6},{8,9},{9,8},{10,11... | collective-permute-start | bytes 1671176 | tf_op jit(solution)/shard_map/ppermute | solution.py:18
  25.4 12.7 %collective-permute-start.5 = (bf16[1088,128]{1,0:T(8,128)(2,1)S(1)}, bf16[1088,128]{1,0:T(8,128)(2,1)}, u32[]{:S(2)}, u32[]{:S(2)}) collective-permute-start(bf16[1088,128]{1,0:T(8,128)(2,1)S(1)} %collective-permute-done.3), channel_id=1, source_target_pairs={{0,2},{1,3},{2,0},{3,1},{4,6},{5,7},{6,4},{7,5},{8,10},{9,11},{10,... | collective-permute-start | bytes 835592 | tf_op jit(solution)/shard_map/ppermute | solution.py:18
  35.9 12.2 %collective-permute-start.11 = (bf16[272,1024]{1,0:T(8,128)(2,1)}, bf16[272,1024]{1,0:T(8,128)(2,1)}, u32[]{:S(2)}, u32[]{:S(2)}) collective-permute-start(bf16[272,1024]{1,0:T(8,128)(2,1)} %slice.8), channel_id=1, source_target_pairs={{0,16},{8,24},{16,0},{24,8},{1,17},{9,25},{17,1},{25,9},{2,18},{10... | collective-permute-start | bytes 1671176 | tf_op jit(solution)/shard_map/ppermute | solution.py:18
  37.2 10.5 %collective-permute-start.12 = (bf16[240,1024]{1,0:T(8,128)(2,1)}, bf16[240,1024]{1,0:T(8,128)(2,1)}, u32[]{:S(2)}, u32[]{:S(2)}) collective-permute-start(bf16[240,1024]{1,0:T(8,128)(2,1)} %slice.9), channel_id=1, source_target_pairs={{0,8},{8,0},{16,24},{24,16},{1,9},{9,1},{17,25},{25,17},{2,10},{10... | collective-permute-start | bytes 1474568 | tf_op jit(solution)/shard_map/ppermute | solution.py:18
  38.1 1.7 %collective-permute-start.7 = (bf16[1088,128]{1,0:T(8,128)(2,1)S(1)}, bf16[1088,128]{1,0:T(8,128)(2,1)}, u32[]{:S(2)}, u32[]{:S(2)}) collective-permute-start(bf16[1088,128]{1,0:T(8,128)(2,1)S(1)} %collective-permute-done.4.refs_1_), channel_id=1, source_target_pairs={{0,1},{1,0},{2,3},{3,2},{4,5},{5,4},{6,7},{7,6},{8,9},{9,8},{10,11... | collective-permute-start | bytes 835592 | tf_op jit(solution)/shard_map/ppermute | solution.py:18
  38.1 2.3 %collective-permute-start.8 = (bf16[1088,128]{1,0:T(8,128)(2,1)}, bf16[1088,128]{1,0:T(8,128)(2,1)}, u32[]{:S(2)}, u32[]{:S(2)}) collective-permute-start(bf16[1088,128]{1,0:T(8,128)(2,1)} %collective-permute-done.5.refs_2_), channel_id=1, source_target_pairs={{0,1},{1,0},{2,3},{3,2},{4,5},{5,4},{6,7},{7,6},{8,9},{9,8},{10,11... | collective-permute-start | bytes 835592 | tf_op jit(solution)/shard_map/ppermute | solution.py:18
  38.8 9.2 %copy-start.1 = (bf16[2048,1024]{1,0:T(8,128)(2,1)S(1)}, bf16[2048,1024]{1,0:T(8,128)(2,1)}, u32[]{:S(2)}) copy-start(bf16[2048,1024]{1,0:T(8,128)(2,1)} %previous.1) | copy-start | bytes 12582916
